TPU v7x, 32 devices: a whole 2x2x4 slice. The times are simulated.
32 devices in a mesh: dp: 2 (over core), row: 4 (over y, x), col: 4 (over z).
Axes of the slice: x: 2, y: 2, z: 4, core: 2. Of those that a mesh axis runs over, the one named last changes fastest.
Arguments:
- hidden_in: bfloat16 [8192, 2048], P(('dp', 'col'), 'row'), may hold values from -6 to 6
- teacher: bfloat16 [8192, 2048], P(('dp', 'col'), 'row'), may hold values from -6 to 6
- valid: int32 [8192], P(('dp', 'col')), may hold values from 0 to 1, as said below
- segment_ids: int32 [2, 4096], P('dp'), may hold values from 0 to 8, as said below
- query_weight: bfloat16 [2048, 2048], P('row', 'col'), may hold values from -0.1875 to 0.1875
- key_weight: bfloat16 [2048, 2048], P('row', 'col'), may hold values from -0.1875 to 0.1875
- value_weight: bfloat16 [2048, 2048], P('row', 'col'), may hold values from -0.125 to 0.125
- output_weight: bfloat16 [2048, 2048], P('col', 'row'), may hold values from -1 to 1
- gate_weight: bfloat16 [2048, 8192], P('row', 'col'), may hold values from -0.125 to 0.125
- up_weight: bfloat16 [2048, 8192], P('row', 'col'), may hold values from -0.125 to 0.125
- down_weight: bfloat16 [8192, 2048], P('col', 'row'), may hold values from -0.09375 to 0.09375
Outputs:
- layer_output: bfloat16 [8192, 2048], P(('dp', 'col'), 'row')
- mean_loss: float32 [1], replicated
- input_gradient: float32 [8192, 2048], P(('dp', 'col'), 'row')
- query_gradient: float32 [2048, 2048], P('row', 'col')
- key_gradient: float32 [2048, 2048], P('row', 'col')
- value_gradient: float32 [2048, 2048], P('row', 'col')
- output_gradient: float32 [2048, 2048], P('col', 'row')
- gate_gradient: float32 [2048, 8192], P('row', 'col')
- up_gradient: float32 [2048, 8192], P('row', 'col')
- down_gradient: float32 [8192, 2048], P('col', 'row')
Inputs may be any that keep to these rules, and one draw needn't show every extreme that they name: `valid`: 1 marks a token that counts in the loss. `segment_ids`: along each group's row the ids never fall: segment 0, the prompt, holds at least 2048 tokens at the start, then continuations 1 to 8 follow in order, each of 128 to 256 tokens.
All inputs are finite; a program needn't handle non-finite values.
Results may differ from a plain program's by a relative error of at most 0.014.
The roundings to bfloat16 on the way count: a program that leaves them out, or rounds other values in their place, can miss the bound.
Values may be sent and summed in bfloat16 or wider, within the bound.
No kernel may reach another device: no remote copies, remote signals or barrier semaphores. Data moves between devices by JAX's collectives and lax.ppermute only.
A program may use at most 448 MiB of HBM per device.

v0:
```python
import math

import jax
import jax.numpy as jnp
from jax import lax
from jax.sharding import PartitionSpec as P

D = 2048
HD = 128
CONT = 8


EPSILON = 1e-05
MASKED_SCORE = -1e30


def positions(segment):
    labels = jnp.arange(CONT + 1, dtype=jnp.int32)
    onehot = (segment[:, None] == labels[None, :]).astype(jnp.int32)
    counts = jnp.sum(onehot, axis=0)
    starts = jnp.cumsum(counts) - counts
    leading = jnp.sum(onehot * starts[None, :], axis=1)
    indices = jnp.arange(segment.shape[0], dtype=jnp.int32)
    return indices - leading + jnp.where(segment > 0, counts[0], 0)


def rotary(offsets):
    half_width = HD // 2
    frequency = jnp.power(10000.0, jnp.arange(half_width, dtype=jnp.float32) * (-2.0 / HD))
    angles = offsets.astype(jnp.float32)[:, None] * frequency[None, :]
    return (jnp.cos(angles), jnp.sin(angles))


def rotate(values, cosine, sine_table):
    half_width = values.shape[-1] // 2
    leading, trailing = (values[..., :half_width], values[..., half_width:])
    cos_wide = cosine[:, None, :]
    sin_wide = sine_table[:, None, :]
    return jnp.concatenate(
        (leading * cos_wide - trailing * sin_wide, trailing * cos_wide + leading * sin_wide),
        axis=-1,
    )


def unrotate(gradient, cosine, sine_table):
    half_width = gradient.shape[-1] // 2
    leading, trailing = (gradient[..., :half_width], gradient[..., half_width:])
    cos_wide = cosine[:, None, :]
    sin_wide = sine_table[:, None, :]
    return jnp.concatenate(
        (leading * cos_wide + trailing * sin_wide, trailing * cos_wide - leading * sin_wide),
        axis=-1,
    )


def feature_sums(left, right):
    return lax.psum((jnp.sum(left, axis=1), jnp.sum(right, axis=1)), "row")


def normalize(values):
    summed, squared = feature_sums(values, values * values)
    average = (summed / D)[:, None]
    inverse = lax.rsqrt(squared[:, None] / D - average * average + EPSILON)
    return ((values - average) * inverse, inverse)


def norm_backward(gradient, normed, inverse):
    summed, crossed = feature_sums(gradient, gradient * normed)
    return inverse * (gradient - summed[:, None] / D - normed * (crossed[:, None] / D))


def widen(values):
    return lax.all_gather(values, "col", axis=0, tiled=True)


def collect(values):
    return lax.all_gather(values, "row", axis=0, tiled=True)


def row_product(full, matrix, contract):
    return lax.psum_scatter(
        lax.dot_general(
            full, matrix, (((1,), (contract,)), ((), ())), preferred_element_type=jnp.float32
        ),
        "row",
        scatter_dimension=0,
        tiled=True,
    )


def column_product(full, matrix, contract):
    return lax.psum_scatter(
        lax.dot_general(
            full, matrix, (((1,), (contract,)), ((), ())), preferred_element_type=jnp.float32
        ),
        "col",
        scatter_dimension=0,
        tiled=True,
    )


def project_in(gathered, matrix):
    result = row_product(gathered, matrix, 0)
    return result


def project_back(gathered, matrix):
    result = row_product(gathered, matrix, 1)
    return result


def weight_product(left, right):
    return lax.dot_general(
        left, right, (((0,), (0,)), ((), ())), preferred_element_type=jnp.float32
    )


def block_layout(tok_rows):
    blocks = max(1, tok_rows // 512)
    return (blocks, tok_rows // blocks)


def score_maker(key_rows, segment, block):
    key_index = jnp.arange(key_rows.shape[0], dtype=jnp.int32)
    scale = 1.0 / math.sqrt(HD)

    def scores_for(query_block, offset):
        query_index = offset + jnp.arange(block, dtype=jnp.int32)
        query_segment = lax.dynamic_slice_in_dim(segment, offset, block, 0)
        allowed = (key_index[None, :] <= query_index[:, None]) & (
            (segment[None, :] == 0) | (segment[None, :] == query_segment[:, None])
        )
        scores = (
            jnp.einsum("qhd,khd->hqk", query_block, key_rows, preferred_element_type=jnp.float32)
            * scale
        )
        return jnp.where(allowed[None, :, :], scores, MASKED_SCORE)

    return scores_for


def attend(queries, key_rows, value_rows, segment, row_offset):
    tok_rows, heads_here = (queries.shape[0], queries.shape[1])
    blocks, block = block_layout(tok_rows)
    scores_for = score_maker(key_rows, segment, block)
    offsets = row_offset + jnp.arange(blocks, dtype=jnp.int32) * block

    def forward_block(inputs):
        query_block, offset = inputs
        scores = scores_for(query_block, offset)
        highest = jnp.max(scores, axis=-1, keepdims=True)
        exponent = jnp.exp(scores - highest)
        summed = jnp.sum(exponent, axis=-1, keepdims=True)
        probability = (exponent / summed).astype(jnp.bfloat16)
        mixed_block = jnp.einsum(
            "hqk,khd->qhd", probability, value_rows, preferred_element_type=jnp.float32
        )
        return (mixed_block, highest + jnp.log(summed))

    mixed_blocks, log_total = lax.map(
        forward_block, (queries.reshape(blocks, block, heads_here, HD), offsets)
    )
    return (mixed_blocks.reshape(tok_rows, heads_here * HD), log_total)


def attend_back(queries, key_rows, value_rows, segment, row_offset, log_total, attended_grad):
    tok_rows, heads_here = (queries.shape[0], queries.shape[1])
    blocks, block = block_layout(tok_rows)
    scores_for = score_maker(key_rows, segment, block)
    offsets = row_offset + jnp.arange(blocks, dtype=jnp.int32) * block
    scale = 1.0 / math.sqrt(HD)

    def backward_block(carry, inputs):
        key_sum, value_sum = carry
        query_block, grad_block, log_block, offset = inputs
        scores = scores_for(query_block, offset)
        probability = jnp.exp(scores - log_block)
        rounded = probability.astype(jnp.bfloat16)
        prob_grad = jnp.einsum(
            "qhd,khd->hqk", grad_block, value_rows, preferred_element_type=jnp.float32
        )
        row_dot = jnp.sum(probability * prob_grad, axis=-1, keepdims=True)
        score_grad = (probability * (prob_grad - row_dot)).astype(jnp.bfloat16)
        query_grad = (
            jnp.einsum("hqk,khd->qhd", score_grad, key_rows, preferred_element_type=jnp.float32)
            * scale
        )
        key_sum = (
            key_sum
            + jnp.einsum(
                "hqk,qhd->khd", score_grad, query_block, preferred_element_type=jnp.float32
            )
            * scale
        )
        value_sum = value_sum + jnp.einsum(
            "hqk,qhd->khd", rounded, grad_block, preferred_element_type=jnp.float32
        )
        return ((key_sum, value_sum), query_grad)

    empty = jnp.zeros(key_rows.shape, jnp.float32)
    inputs = (
        queries.reshape(blocks, block, heads_here, HD),
        attended_grad.reshape(blocks, block, heads_here, HD),
        log_total,
        offsets,
    )
    (key_sum, value_sum), query_grads = lax.scan(backward_block, (empty, empty), inputs)
    return (query_grads.reshape(tok_rows, heads_here, HD), key_sum, value_sum)


def shards(
    hidden_in,
    teacher,
    valid,
    segment_ids,
    query_weight,
    key_weight,
    value_weight,
    output_weight,
    gate_weight,
    up_weight,
    down_weight,
):
    row_devices = lax.axis_size("row")
    col_devices = lax.axis_size("col")
    tok_cols = hidden_in.shape[0]
    group_tokens = tok_cols * col_devices
    tok_rows = group_tokens // row_devices
    query_width = query_weight.shape[1]
    heads_here = query_width // HD
    unit_width = gate_weight.shape[1]
    segment = segment_ids[0]
    row_offset = lax.axis_index("row") * tok_rows
    cosine_all, sine_all = rotary(positions(segment))
    cosine = lax.dynamic_slice_in_dim(cosine_all, row_offset, tok_rows, 0)
    sine_table = lax.dynamic_slice_in_dim(sine_all, row_offset, tok_rows, 0)
    counted = valid.astype(jnp.float32)
    total_count = jnp.maximum(lax.psum(jnp.sum(counted), ("dp", "col")), 1.0)
    hidden = hidden_in.astype(jnp.float32)
    normed, inverse_one = normalize(hidden)
    normed_wide = widen(normed.astype(jnp.bfloat16))
    attn_weights = jnp.concatenate((query_weight, key_weight, value_weight), axis=1)
    projected = project_in(normed_wide, attn_weights)
    queries = rotate(
        projected[:, :query_width].reshape(tok_rows, heads_here, HD), cosine, sine_table
    ).astype(jnp.bfloat16)
    key_local = rotate(
        projected[:, query_width : 2 * query_width].reshape(tok_rows, heads_here, HD),
        cosine,
        sine_table,
    )
    key_local = key_local.reshape(tok_rows, query_width).astype(jnp.bfloat16)
    value_local = projected[:, 2 * query_width :].astype(jnp.bfloat16)
    key_flat, value_flat = (
        lax.all_gather(key_local, "row", axis=0, tiled=True),
        lax.all_gather(value_local, "row", axis=0, tiled=True),
    )
    key_rows = key_flat.reshape(group_tokens, heads_here, HD)
    value_rows = value_flat.reshape(group_tokens, heads_here, HD)
    attended, log_total = attend(queries, key_rows, value_rows, segment, row_offset)
    attended_wide = collect(attended.astype(jnp.bfloat16))
    after_attention = hidden + column_product(attended_wide, output_weight, 0)
    normed_two, inverse_two = normalize(after_attention)
    normed_two_wide = widen(normed_two.astype(jnp.bfloat16))
    mlp_weights = jnp.concatenate((gate_weight, up_weight), axis=1)
    gated = project_in(normed_two_wide, mlp_weights)
    gating = gated[:, :unit_width]
    upward = gated[:, unit_width:]
    sigmoid = jax.nn.sigmoid(gating)
    activated = gating * sigmoid
    units_wide = collect((activated * upward).astype(jnp.bfloat16))
    output = after_attention + column_product(units_wide, down_weight, 0)
    differ = output - teacher.astype(jnp.float32)
    local_loss = jnp.sum(counted[:, None] * (differ * differ)) / D
    all_tokens = group_tokens * lax.axis_size("dp")
    out_grad = counted[:, None] * differ * (all_tokens / total_count)
    out_wide = widen(out_grad.astype(jnp.bfloat16))
    units_grad = project_back(out_wide, down_weight)
    down_grad = weight_product(units_wide, out_wide)
    gating_grad = units_grad * upward * sigmoid * (1.0 + gating * (1.0 - sigmoid))
    upward_grad = units_grad * activated
    gated_wide = collect(jnp.concatenate((gating_grad, upward_grad), axis=1).astype(jnp.bfloat16))
    mlp_grads = weight_product(normed_two_wide, gated_wide)
    normed_two_grad = column_product(gated_wide, mlp_weights, 1)
    middle_grad = out_grad + norm_backward(normed_two_grad, normed_two, inverse_two)
    middle_wide = widen(middle_grad.astype(jnp.bfloat16))
    attended_grad = project_back(middle_wide, output_weight).astype(jnp.bfloat16)
    output_grad_sum = weight_product(attended_wide, middle_wide)
    query_grad, key_sum, value_sum = attend_back(
        queries, key_rows, value_rows, segment, row_offset, log_total, attended_grad
    )
    key_grad, value_grad = (
        lax.psum_scatter(
            key_sum.reshape(group_tokens, query_width), "row", scatter_dimension=0, tiled=True
        ),
        lax.psum_scatter(
            value_sum.reshape(group_tokens, query_width), "row", scatter_dimension=0, tiled=True
        ),
    )
    query_pre = unrotate(query_grad, cosine, sine_table).reshape(tok_rows, query_width)
    key_pre = unrotate(key_grad.reshape(tok_rows, heads_here, HD), cosine, sine_table).reshape(
        tok_rows, query_width
    )
    projected_wide = collect(
        jnp.concatenate((query_pre, key_pre, value_grad), axis=1).astype(jnp.bfloat16)
    )
    attn_grads = weight_product(normed_wide, projected_wide)
    normed_grad = column_product(projected_wide, attn_weights, 1)
    input_gradient = middle_grad + norm_backward(normed_grad, normed, inverse_one)
    summed_grads = (
        lax.psum(attn_grads[:, :query_width].astype(jnp.bfloat16), "dp").astype(jnp.float32),
        lax.psum(attn_grads[:, query_width : 2 * query_width].astype(jnp.bfloat16), "dp").astype(
            jnp.float32
        ),
        lax.psum(attn_grads[:, 2 * query_width :].astype(jnp.bfloat16), "dp").astype(jnp.float32),
        lax.psum(output_grad_sum.astype(jnp.bfloat16), "dp").astype(jnp.float32),
        lax.psum(mlp_grads[:, :unit_width].astype(jnp.bfloat16), "dp").astype(jnp.float32),
        lax.psum(mlp_grads[:, unit_width:].astype(jnp.bfloat16), "dp").astype(jnp.float32),
        lax.psum(down_grad.astype(jnp.bfloat16), "dp").astype(jnp.float32),
    )
    mean_loss = lax.psum(local_loss, ("dp", "row", "col")) / total_count
    return (
        output.astype(jnp.bfloat16),
        mean_loss.reshape(1),
        input_gradient,
        summed_grads[0],
        summed_grads[1],
        summed_grads[2],
        summed_grads[3],
        summed_grads[4],
        summed_grads[5],
        summed_grads[6],
    )


def solution(mesh):
    in_specs = (
        P(("dp", "col"), "row"),
        P(("dp", "col"), "row"),
        P(("dp", "col")),
        P("dp", None),
        P("row", "col"),
        P("row", "col"),
        P("row", "col"),
        P("col", "row"),
        P("row", "col"),
        P("row", "col"),
        P("col", "row"),
    )
    out_specs = (
        P(("dp", "col"), "row"),
        P(),
        P(("dp", "col"), "row"),
        P("row", "col"),
        P("row", "col"),
        P("row", "col"),
        P("col", "row"),
        P("row", "col"),
        P("row", "col"),
        P("col", "row"),
    )
    return jax.shard_map(shards, mesh=mesh, in_specs=in_specs, out_specs=out_specs, check_vma=False)
```

profile of v0, /device:TPU:0, one launch (start us, length us, event | category | flops | bytes accessed | tf_op | source)
XLA Modules:
  0.0 4208.1 jit_solution(10490348117474792527)
XLA Ops:
  27.4 76.6 %all-gather.11.cloned.1.call-done = bf16[4096,512]{1,0:T(8,128)(2,1)} async-done(((bf16[1024,512]{1,0:T(8,128)(2,1)}), bf16[4096,512]{1,0:T(8,128)(2,1)}) %all-gather.11.cloned.1.call-update) | async-done | bytes 4194320 | tf_op jit(solution)/shard_map/all_gather | solution.py:73
  122.2 216.1 %reduce-scatter.10.cloned.1.call-done = f32[1024,1536]{1,0:T(8,128)} async-done(((f32[4096,1536]{1,0:T(8,128)}), f32[1024,1536]{1,0:T(8,128)}) %reduce-scatter.10.cloned.1.call-update) | async-done | bytes 6291472 | tf_op jit(solution)/shard_map/reduce_scatter | solution.py:81
  374.8 39.0 all-gather.13.cloned.1.call-done
  420.1 48.8 %all-gather.15.cloned.1.call-done = bf16[4096,512]{1,0:T(8,128)(2,1)} async-done(((bf16[1024,512]{1,0:T(8,128)(2,1)}), bf16[4096,512]{1,0:T(8,128)(2,1)}) %all-gather.15.cloned.1.call-update) | async-done | bytes 4194320 | tf_op jit(solution)/shard_map/all_gather | solution.py:256
  473.9 112.2 %while.28 = (s32[]{:T(128)}, bf16[2,512,4,128]{3,1,2,0:T(8,128)(2,1)}, f32[2,4,512,1]{2,1,3,0:T(4,128)S(1)}, s32[2]{0:T(128)S(1)}, s32[1,4096]{1,0:T(1,128)S(1)}...) while((s32[]{:T(128)}, ...), condition=%wide.region_11.12_spmd.clone, body=%wide.region_8.11_spmd.clone.sunk | while | flops 4404021760 | bytes 127519944 | solution.py:160
  589.5 52.8 %all-gather.17.cloned.1.call-done = bf16[4096,512]{1,0:T(8,128)(2,1)} async-done(((bf16[1024,512]{1,0:T(8,128)(2,1)}), bf16[4096,512]{1,0:T(8,128)(2,1)}) %all-gather.17.cloned.1.call-update) | async-done | bytes 4194320 | tf_op jit(solution)/shard_map/all_gather | solution.py:77
  650.2 144.6 %reduce-scatter.12.cloned.1.call-done = f32[1024,512]{1,0:T(8,128)} async-done(((f32[4096,512]{1,0:T(8,128)}), f32[1024,512]{1,0:T(8,128)}) %reduce-scatter.12.cloned.1.call-update) | async-done | bytes 2097168 | tf_op jit(solution)/shard_map/reduce_scatter | solution.py:92
  816.3 74.9 %all-gather.19.cloned.1.call-done = bf16[4096,512]{1,0:T(8,128)(2,1)} async-done(((bf16[1024,512]{1,0:T(8,128)(2,1)}), bf16[4096,512]{1,0:T(8,128)(2,1)}) %all-gather.19.cloned.1.call-update) | async-done | bytes 4194320 | tf_op jit(solution)/shard_map/all_gather | solution.py:73
  891.2 30.0 fusion.59
  923.1 1113.8 %all-reduce.9.cloned.1.call-done = f32[4096,4096]{1,0:T(8,128)} async-done(((f32[4096,4096]{1,0:T(8,128)}), f32[4096,4096]{1,0:T(8,128)}) %all-reduce.9.cloned.1.call-update) | async-done | bytes 67108880
  2045.6 158.9 %all-gather.21.cloned.1.call-done = bf16[4096,2048]{1,0:T(8,128)(2,1)} async-done(((bf16[1024,2048]{1,0:T(8,128)(2,1)}), bf16[4096,2048]{1,0:T(8,128)(2,1)}) %all-gather.21.cloned.1.call-update) | async-done | bytes 16777232 | tf_op jit(solution)/shard_map/all_gather | solution.py:77
  2240.0 124.4 %reduce-scatter.14.cloned.1.call-done = f32[1024,512]{1,0:T(8,128)} async-done(((f32[4096,512]{1,0:T(8,128)}), f32[1024,512]{1,0:T(8,128)}) %reduce-scatter.14.cloned.1.call-update) | async-done | bytes 2097168 | tf_op jit(solution)/shard_map/reduce_scatter | solution.py:92
  2368.0 81.6 %all-gather.23.cloned.1.call-done = bf16[4096,512]{1,0:T(8,128)(2,1)} async-done(((bf16[1024,512]{1,0:T(8,128)(2,1)}), bf16[4096,512]{1,0:T(8,128)(2,1)}) %all-gather.23.cloned.1.call-update) | async-done | bytes 4194320 | tf_op jit(solution)/shard_map/all_gather | solution.py:73
  2467.2 287.3 %reduce-scatter.16.cloned.1.call-done = f32[1024,2048]{1,0:T(8,128)} async-done(((f32[4096,2048]{1,0:T(8,128)}), f32[1024,2048]{1,0:T(8,128)}) %reduce-scatter.16.cloned.1.call-update) | async-done | bytes 8388624 | tf_op jit(solution)/shard_map/reduce_scatter | solution.py:81
  2775.6 297.3 %all-gather.25.cloned.1.call-done = bf16[4096,4096]{1,0:T(8,128)(2,1)} async-done(((bf16[1024,4096]{1,0:T(8,128)(2,1)}), bf16[4096,4096]{1,0:T(8,128)(2,1)}) %all-gather.25.cloned.1.call-update) | async-done | bytes 33554448 | tf_op jit(solution)/shard_map/all_gather | solution.py:77
  3098.0 144.6 %reduce-scatter.18.cloned.1.call-done = f32[1024,512]{1,0:T(8,128)} async-done(((f32[4096,512]{1,0:T(8,128)}), f32[1024,512]{1,0:T(8,128)}) %reduce-scatter.18.cloned.1.call-update) | async-done | bytes 2097168 | tf_op jit(solution)/shard_map/reduce_scatter | solution.py:92
  3260.7 79.7 %all-gather.27.cloned.1.call-done = bf16[4096,512]{1,0:T(8,128)(2,1)} async-done(((bf16[1024,512]{1,0:T(8,128)(2,1)}), bf16[4096,512]{1,0:T(8,128)(2,1)}) %all-gather.27.cloned.1.call-update) | async-done | bytes 4194320 | tf_op jit(solution)/shard_map/all_gather | solution.py:73
  3348.5 85.0 %reduce-scatter.20.cloned.1.call-done = f32[1024,512]{1,0:T(8,128)} async-done(((f32[4096,512]{1,0:T(8,128)}), f32[1024,512]{1,0:T(8,128)}) %reduce-scatter.20.cloned.1.call-update) | async-done | bytes 2097168 | tf_op jit(solution)/shard_map/reduce_scatter | solution.py:81
  3436.4 244.2 %while.29 = (s32[]{:T(128)}, f32[4096,4,128]{0,2,1:T(8,128)}, f32[4096,4,128]{0,2,1:T(8,128)}, f32[2,512,4,128]{3,1,0,2:T(8,128)}, bf16[2,512,4,128]{3,1,2,0:T(8...) while((s32[]{:T(128)}, f32[4096,4,128]{0,2,1:T(8,128)}, ...), condition=%wide.region_32.33_spmd.clone, body=%wide.region_30.32_spmd.clone.sunk | while | flops 10882385920 | bytes 371305376 | solution.py:207
  3681.2 85.9 %reduce-scatter.22.cloned.1.call-done = f32[1024,512]{0,1:T(8,128)} async-done(((f32[4096,512]{0,1:T(8,128)}), f32[1024,512]{0,1:T(8,128)}) %reduce-scatter.22.cloned.1.call-update) | async-done | bytes 2097168 | tf_op jit(solution)/shard_map/reduce_scatter | solution.py:293
  3785.4 71.4 %reduce-scatter.24.cloned.1.call-done = f32[1024,512]{0,1:T(8,128)} async-done(((f32[4096,512]{0,1:T(8,128)}), f32[1024,512]{0,1:T(8,128)}) %reduce-scatter.24.cloned.1.call-update) | async-done | bytes 2097168 | tf_op jit(solution)/shard_map/reduce_scatter | solution.py:296
  3905.7 77.3 %all-gather.29.cloned.1.call-done = bf16[4096,1536]{0,1:T(8,128)(2,1)} async-done(((bf16[1024,1536]{0,1:T(8,128)(2,1)}), bf16[4096,1536]{0,1:T(8,128)(2,1)}) %all-gather.29.cloned.1.call-update) | async-done | bytes 12582928 | tf_op jit(solution)/shard_map/all_gather | solution.py:77
  4009.0 39.4 psum.123
  4063.0 120.5 %reduce-scatter.26.cloned.1.call-done = f32[1024,512]{1,0:T(8,128)} async-done(((f32[4096,512]{1,0:T(8,128)}), f32[1024,512]{1,0:T(8,128)}) %reduce-scatter.26.cloned.1.call-update) | async-done | bytes 2097168 | tf_op jit(solution)/shard_map/reduce_scatter | solution.py:92
  (294 shorter events, 730.4 us)
Async XLA Ops:
  7.2 2197.3 %copy-start = (bf16[2048,512]{1,0:T(8,128)(2,1)S(1)}, bf16[2048,512]{1,0:T(8,128)(2,1)}, u32[]{:S(2)}) copy-start(bf16[2048,512]{1,0:T(8,128)(2,1)} %param.25) | copy-start | bytes 6291460
  7.2 96.8 %all-gather.11.cloned.1.call-start = ((), (), s32[]{:S(2)}) async-start(), calls=%async_computation.9 | async-start | bytes 5242880 | tf_op jit(solution)/shard_map/all_gather | solution.py:73
  23.7 314.6 %reduce-scatter.10.cloned.1.call-start = ((), (), s32[]{:S(2)}) async-start(), calls=%async_computation.10 | async-start | bytes 31457280 | tf_op jit(solution)/shard_map/reduce_scatter | solution.py:81
  117.8 296.0 %all-gather.13.cloned.1.call-start = ((), (), s32[]{:S(2)}) async-start(), calls=%async_computation.11 | async-start | bytes 5242880 | tf_op jit(solution)/shard_map/all_gather | solution.py:255
  122.2 232.5 %copy-start.19 = (f32[1024,64]{1,0:T(8,128)}, f32[1024,64]{1,0:T(8,128)S(1)}, u32[]{:S(2)}) copy-start(f32[1024,64]{1,0:T(8,128)S(1)} %get-tuple-element.395) | copy-start | bytes 786436
  361.0 108.0 %all-gather.15.cloned.1.call-start = ((), (), s32[]{:S(2)}) async-start(), calls=%async_computation.12 | async-start | bytes 5242880 | tf_op jit(solution)/shard_map/all_gather | solution.py:256
  363.7 278.6 %all-gather.17.cloned.1.call-start = ((), (), s32[]{:S(2)}) async-start(), calls=%async_computation.13 | async-start | bytes 5242880 | tf_op jit(solution)/shard_map/all_gather | solution.py:77
  589.4 205.3 %reduce-scatter.12.cloned.1.call-start = ((), (), s32[]{:S(2)}) async-start(), calls=%async_computation.14 | async-start | bytes 10485760 | tf_op jit(solution)/shard_map/reduce_scatter | solution.py:92
  650.1 241.1 %all-gather.19.cloned.1.call-start = ((), (), s32[]{:S(2)}) async-start(), calls=%async_computation.15 | async-start | bytes 5242880 | tf_op jit(solution)/shard_map/all_gather | solution.py:73
  811.5 1225.4 %all-reduce.9.cloned.1.call-start = ((), (), s32[]{:S(2)}) async-start(), calls=%async_computation.28 | async-start | bytes 134217728
  921.2 1283.3 %all-gather.21.cloned.1.call-start = ((), (), s32[]{:S(2)}) async-start(), calls=%async_computation.16 | async-start | bytes 20971520 | tf_op jit(solution)/shard_map/all_gather | solution.py:77
  2045.5 318.9 %reduce-scatter.14.cloned.1.call-start = ((), (), s32[]{:S(2)}) async-start(), calls=%async_computation.17 | async-start | bytes 10485760 | tf_op jit(solution)/shard_map/reduce_scatter | solution.py:92
  2219.3 145.1 %copy-start.13 = (bf16[1024,512]{1,0:T(8,128)(2,1)S(1)}, bf16[1024,512]{1,0:T(8,128)(2,1)}, u32[]{:S(2)}) copy-start(bf16[1024,512]{1,0:T(8,128)(2,1)} %param.16) | copy-start | bytes 3145732
  2219.3 230.3 %all-gather.23.cloned.1.call-start = ((), (), s32[]{:S(2)}) async-start(), calls=%async_computation.18 | async-start | bytes 5242880 | tf_op jit(solution)/shard_map/all_gather | solution.py:73
  2368.0 386.5 %reduce-scatter.16.cloned.1.call-start = ((), (), s32[]{:S(2)}) async-start(), calls=%async_computation.19 | async-start | bytes 41943040 | tf_op jit(solution)/shard_map/reduce_scatter | solution.py:81
  2467.2 605.7 %all-gather.25.cloned.1.call-start = ((), (), s32[]{:S(2)}) async-start(), calls=%async_computation.20 | async-start | bytes 41943040 | tf_op jit(solution)/shard_map/all_gather | solution.py:77
  2775.5 467.1 %reduce-scatter.18.cloned.1.call-start = ((), (), s32[]{:S(2)}) async-start(), calls=%async_computation.21 | async-start | bytes 10485760 | tf_op jit(solution)/shard_map/reduce_scatter | solution.py:92
  3097.9 242.5 %all-gather.27.cloned.1.call-start = ((), (), s32[]{:S(2)}) async-start(), calls=%async_computation.22 | async-start | bytes 5242880 | tf_op jit(solution)/shard_map/all_gather | solution.py:73
  3260.6 172.9 %reduce-scatter.20.cloned.1.call-start = ((), (), s32[]{:S(2)}) async-start(), calls=%async_computation.23 | async-start | bytes 10485760 | tf_op jit(solution)/shard_map/reduce_scatter | solution.py:81
  3348.5 418.7 %reduce-scatter.22.cloned.1.call-start = ((), (), s32[]{:S(2)}) async-start(), calls=%async_computation.24 | async-start | bytes 10485760 | tf_op jit(solution)/shard_map/reduce_scatter | solution.py:293
  3680.6 176.2 %reduce-scatter.24.cloned.1.call-start = ((), (), s32[]{:S(2)}) async-start(), calls=%async_computation.25 | async-start | bytes 10485760 | tf_op jit(solution)/shard_map/reduce_scatter | solution.py:296
  3681.1 301.9 %all-gather.29.cloned.1.call-start = ((), (), s32[]{:S(2)}) async-start(), calls=%async_computation.26 | async-start | bytes 15728640 | tf_op jit(solution)/shard_map/all_gather | solution.py:77
  3860.4 188.6 %all-reduce.11.cloned.1.call-start = ((), (), s32[]{:S(2)}) async-start(), calls=%async_computation.29 | async-start | bytes 16777216 | tf_op jit(solution)/shard_map/psum | solution.py:311
  3995.2 188.3 %reduce-scatter.26.cloned.1.call-start = ((), (), s32[]{:S(2)}) async-start(), calls=%async_computation.27 | async-start | bytes 10485760 | tf_op jit(solution)/shard_map/reduce_scatter | solution.py:92
  (54 other events, 1773.3 us)
Sparse Core Ops, SparseCore 0:
  23.8 80.1 all-gather.10
  117.9 220.3 reduce-scatter.9
  361.1 52.7 all-gather.12
  416.2 52.6 all-gather.14
  589.6 52.6 all-gather.16
  650.3 144.4 reduce-scatter.11
  811.6 79.5 all-gather.18
  921.3 1115.4 all-reduce.8
  2045.6 158.8 all-gather.20
  2219.4 144.9 reduce-scatter.13
  2368.1 81.4 all-gather.22
  2467.3 287.1 reduce-scatter.15
  2775.6 297.1 all-gather.24
  3098.1 144.4 reduce-scatter.17
  3260.7 79.6 all-gather.26
  3348.5 84.9 reduce-scatter.19
  3680.7 86.3 reduce-scatter.21
  3770.3 86.3 reduce-scatter.23
  3860.5 122.4 all-gather.28
  3995.3 40.0 all-reduce.10
  4037.8 145.6 reduce-scatter.25
where the time goes:
time: 4220 us; the launch traced here: 4210 us
  waiting for transfers between devices  3380 us (80%)
  matrix products  422 us (10%)
  other arithmetic  193 us (5%)
  blocking collectives  99.8 us (2%)
  local copies, waits for them, and re-layouts  83.2 us (2%)
    unnamed x22, waiting for transfers between devices  1110 us
    reduce_scatter x3, waiting for transfers between devices, row_product(): lax.psum_scatter(lax.dot_general(full, matrix, (((1,), (contract,)), ((),...  588 us
    all_gather x4, waiting for transfers between devices, collect(): return lax.all_gather(values, 'row', axis=0, tiled=True)  586 us
    reduce_scatter x4, waiting for transfers between devices, column_product(): lax.psum_scatter(lax.dot_general(full, matrix, (((1,), (contract,)), ((),...  534 us
    all_gather x4, waiting for transfers between devices, widen(): return lax.all_gather(values, 'col', axis=0, tiled=True)  313 us
    reduce_scatter x1, waiting for transfers between devices, shards(): lax.psum_scatter(key_sum.reshape(group_tokens, query_width), 'row', scatt...  85.9 us
  transfers between devices with their start and end apart: 21, of which 20 were waited for; matrix products, arithmetic and copies ran while one was open for 3% of the time, Pallas kernels for 0%

commit v1 on v0

--- a/solution.py
+++ b/solution.py
@@ -3,6 +3,8 @@
 import jax
 import jax.numpy as jnp
 from jax import lax
+from jax.experimental import pallas as pl
+from jax.experimental.pallas import tpu as pltpu
 from jax.sharding import PartitionSpec as P
 
 D = 2048
@@ -333,7 +335,532 @@
     )
 
 
+BF = jnp.bfloat16
+F32 = jnp.float32
+LOG2E = 1.4426950408889634
+SIDE = 4
+
+
+def fits_square(mesh):
+    return mesh.shape["dp"] == 2 and mesh.shape["row"] == SIDE and mesh.shape["col"] == SIDE
+
+
+def flip(values, axis, bit):
+    return lax.ppermute(values, axis, [(i, i ^ bit) for i in range(SIDE)])
+
+
+def flip_x(values):
+    return flip(values, "row", 1)
+
+
+def flip_y(values):
+    return flip(values, "row", 2)
+
+
+def flip_zl(values):
+    return flip(values, "col", 1)
+
+
+def flip_zh(values):
+    return flip(values, "col", 2)
+
+
+def flip_y_zh(values):
+    pairs = [
+        (r * SIDE + c, (r ^ 2) * SIDE + (c ^ 2)) for r in range(SIDE) for c in range(SIDE)
+    ]
+    return lax.ppermute(values, ("row", "col"), pairs)
+
+
+def flip_dp(values):
+    return lax.ppermute(values, "dp", [(0, 1), (1, 0)])
+
+
+def sum_all(value, with_row):
+    value = value + flip_dp(value)
+    value = value + flip_zl(value)
+    value = value + flip_zh(value)
+    if with_row:
+        value = value + flip_x(value)
+        value = value + flip_y(value)
+    return value
+
+
+def square_gather(block):
+    half = block.shape[0] // 2
+    top, bottom = block[:half], block[half:]
+    x_top, z_bottom = flip_x(top), flip_zl(bottom)
+    x_bottom, z_top = flip_x(bottom), flip_zl(top)
+    d_top, d_bottom = flip_zl(x_top), flip_x(z_bottom)
+    join = lambda a, b: jnp.concatenate((a, b), axis=0)
+    return [block, join(x_top, x_bottom), join(z_top, z_bottom), join(d_top, d_bottom)]
+
+
+def square_reduce(make):
+    far = make(3)
+    half = far.shape[0] // 2
+    far = far.astype(BF)
+    far_top, far_bottom = flip_zl(far[:half]), flip_x(far[half:])
+    by_x, by_z = make(1), make(2)
+    x_bottom = flip_x(by_x[half:].astype(BF))
+    z_top = flip_zl(by_z[:half].astype(BF))
+    x_top = flip_x((by_x[:half] + far_top.astype(F32)).astype(BF))
+    z_bottom = flip_zl((by_z[half:] + far_bottom.astype(F32)).astype(BF))
+    own = make(0)
+    top = own[:half] + x_top.astype(F32) + z_top.astype(F32)
+    bottom = own[half:] + x_bottom.astype(F32) + z_bottom.astype(F32)
+    return jnp.concatenate((top, bottom), axis=0)
+
+
+def ordered(flag, own, other, axis):
+    return jnp.where(
+        flag == 0,
+        jnp.concatenate((own, other), axis=axis),
+        jnp.concatenate((other, own), axis=axis),
+    )
+
+
+def pick(values, index, axis):
+    return lax.dynamic_index_in_dim(values, index, axis, keepdims=False)
+
+
+def gather_weights(matrices, place, lead):
+    x, y, dp = place
+    m, rows, n = matrices.shape
+    cut = matrices.reshape(m, rows, 2, 2, n // 4)
+    cut = pick(cut, dp, 3)
+    own, send = pick(cut, x, 2), pick(cut, 1 - x, 2)
+    tall = ordered(x, own, flip_x(send), 1)
+    pair = jnp.stack((tall, flip_zh(tall)), axis=2)
+    full = ordered(y, pair, flip_y(pair), 1)
+    other = flip_dp(full)
+    slots = ordered(lead, full[:, :, :, None], other[:, :, :, None], 3)
+    return slots.reshape(m, 4 * rows, n)
+
+
+def scatter_grads(grads, place, lead):
+    x, y, dp = place
+    m, depth, n = grads.shape
+    rows = depth // 4
+    cut = grads.astype(BF).reshape(m, depth, 2, 2, n // 4)
+    keep, send = pick(cut, lead, 3), pick(cut, 1 - lead, 3)
+    total = (keep.astype(F32) + flip_dp(send).astype(F32)).astype(BF)
+    total = total.reshape(m, 2, 2 * rows, 2, n // 4)
+    keep, send = pick(total, y, 1), pick(total, 1 - y, 1)
+    total = (keep.astype(F32) + flip_y(send).astype(F32)).astype(BF)
+    keep, send = total[:, :, 0], total[:, :, 1]
+    total = (keep.astype(F32) + flip_zh(send).astype(F32)).astype(BF)
+    total = total.reshape(m, 2, rows, n // 4)
+    keep, send = pick(total, x, 1), pick(total, 1 - x, 1)
+    both = ordered(x, keep[:, :, None], flip_x(send)[:, :, None], 2)
+    whole = ordered(dp, both[:, :, :, None], flip_dp(both)[:, :, :, None], 3)
+    return whole.reshape(m, rows, n).astype(F32)
+
+
+def local_norm(values):
+    average = jnp.mean(values, axis=1, keepdims=True)
+    square = jnp.mean(values * values, axis=1, keepdims=True)
+    inverse = lax.rsqrt(square - average * average + EPSILON)
+    return ((values - average) * inverse, inverse)
+
+
+def local_norm_backward(gradient, normed, inverse):
+    average = jnp.mean(gradient, axis=1, keepdims=True)
+    crossed = jnp.mean(gradient * normed, axis=1, keepdims=True)
+    return inverse * (gradient - average - normed * crossed)
+
+
+def dot(left, right, a, b):
+    return lax.dot_general(left, right, (((a,), (b,)), ((), ())), preferred_element_type=F32)
+
+
+BLOCK = 512
+PIECE = 256
+
+
+def allowed_pairs(starts, query0, key0, shape, query_axis):
+    query = query0 + lax.broadcasted_iota(jnp.int32, shape, query_axis)
+    key = key0 + lax.broadcasted_iota(jnp.int32, shape, 1 - query_axis)
+    first = jnp.zeros(shape, jnp.int32)
+    for s in range(CONT):
+        first = jnp.where(query >= starts[s], starts[s], first)
+    return (key <= query) & ((key < starts[0]) | (key >= first))
+
+
+def block_bounds(starts, n):
+    full = jnp.minimum(n, starts[0] // BLOCK)
+    first = jnp.int32(0)
+    for s in range(CONT):
+        first = jnp.where(n * BLOCK >= starts[s], starts[s], first)
+    return full, first
+
+
+def block_used(starts, first, m):
+    return (m * BLOCK < starts[0]) | ((m + 1) * BLOCK > first)
+
+
+def attention_forward(place_ref, starts_ref, *refs):
+    messages, refs = refs[:4], refs[4:]
+    outs, refs = refs[:4], refs[4:]
+    wide_ref, log_ref, q_s, k_s, v_s, score_s, acc_s, sum_s, max_s = refs
+    scale = LOG2E / math.sqrt(HD)
+    starts = [starts_ref[s] for s in range(CONT)]
+    for b in range(4):
+        for a in range(4):
+            rows = pl.ds(pl.multiple_of(place_ref[4 * b + a] * PIECE, PIECE), PIECE)
+            q_s[rows, :] = messages[b][0, a]
+            k_s[rows, :] = messages[b][1, a]
+            v_s[rows, :] = messages[b][2, a]
+
+    def one_block(n, carry):
+        rows = pl.ds(pl.multiple_of(n * BLOCK, BLOCK), BLOCK)
+        full, first = block_bounds(starts, n)
+        max_s[...] = jnp.full(max_s.shape, -1e30, F32)
+        acc_s[...] = jnp.zeros(acc_s.shape, F32)
+        sum_s[...] = jnp.zeros(sum_s.shape, F32)
+
+        def note(scores, m):
+            score_s[m] = scores
+            top = max_s[...]
+            for part in range(BLOCK // HD):
+                top = jnp.maximum(top, scores[:, part * HD : (part + 1) * HD])
+            max_s[...] = top
+
+        def product(m):
+            keys = pl.ds(pl.multiple_of(m * BLOCK, BLOCK), BLOCK)
+            return dot(q_s[rows, :], k_s[keys, :], 1, 1)
+
+        @pl.loop(0, full)
+        def _(m):
+            note(product(m), m)
+
+        @pl.loop(full, n + 1)
+        def _(m):
+            @pl.when(block_used(starts, first, m))
+            def _():
+                allowed = allowed_pairs(starts, n * BLOCK, m * BLOCK, (BLOCK, BLOCK), 0)
+                note(jnp.where(allowed, product(m), MASKED_SCORE), m)
+
+        highest = jnp.max(max_s[...], axis=1, keepdims=True) * scale
+
+        @pl.loop(0, n + 1)
+        def _(m):
+            @pl.when(block_used(starts, first, m))
+            def _():
+                keys = pl.ds(pl.multiple_of(m * BLOCK, BLOCK), BLOCK)
+                exponent = jnp.exp2(score_s[m] * scale - highest)
+                total = sum_s[...]
+                for part in range(BLOCK // HD):
+                    total = total + exponent[:, part * HD : (part + 1) * HD]
+                sum_s[...] = total
+                acc_s[...] += dot(exponent.astype(BF), v_s[keys, :], 1, 0)
+
+        total = jnp.sum(sum_s[...], axis=1, keepdims=True)
+        wide_ref[rows, :] = acc_s[...] / total
+        log_total = jnp.broadcast_to(highest + jnp.log2(total), (BLOCK, HD))
+        log_ref[n] = log_total.T[:8]
+        return carry
+
+    lax.fori_loop(0, k_s.shape[0] // BLOCK, one_block, 0)
+    for b in range(4):
+        for a in range(4):
+            rows = pl.ds(pl.multiple_of(place_ref[4 * b + a] * PIECE, PIECE), PIECE)
+            outs[b][a] = wide_ref[rows, :].astype(BF)
+
+
+def attention_backward(place_ref, starts_ref, *refs):
+    messages, refs = refs[:4], refs[4:]
+    grads, refs = refs[:4], refs[4:]
+    wide_ref, log_ref, cos_ref, sin_ref, *refs = refs
+    outs, refs = refs[:4], refs[4:]
+    q_s, k_s, v_s, g_s, dq_s, dk_s, dv_s = refs
+    scale = LOG2E / math.sqrt(HD)
+    starts = [starts_ref[s] for s in range(CONT)]
+    for b in range(4):
+        for a in range(4):
+            rows = pl.ds(pl.multiple_of(place_ref[4 * b + a] * PIECE, PIECE), PIECE)
+            q_s[rows, :] = messages[b][0, a]
+            k_s[rows, :] = messages[b][1, a]
+            v_s[rows, :] = messages[b][2, a]
+            g_s[rows, :] = grads[b][a]
+    dq_s[...] = jnp.zeros(dq_s.shape, F32)
+    dk_s[...] = jnp.zeros(dk_s.shape, F32)
+    dv_s[...] = jnp.zeros(dv_s.shape, F32)
+
+    def one_block(n, carry):
+        rows = pl.ds(pl.multiple_of(n * BLOCK, BLOCK), BLOCK)
+        full, first = block_bounds(starts, n)
+        crossed = g_s[rows, :].astype(F32) * wide_ref[rows, :]
+        row_dot = jnp.sum(crossed.T, axis=0, keepdims=True)
+        log_total = log_ref[n][:1]
+
+        def step(m, masked):
+            keys = pl.ds(pl.multiple_of(m * BLOCK, BLOCK), BLOCK)
+            query, key = q_s[rows, :], k_s[keys, :]
+            probability = jnp.exp2(dot(key, query, 1, 1) * scale - log_total)
+            if masked:
+                allowed = allowed_pairs(starts, n * BLOCK, m * BLOCK, (BLOCK, BLOCK), 1)
+                probability = jnp.where(allowed, probability, 0.0)
+            prob_grad = dot(v_s[keys, :], g_s[rows, :], 1, 1)
+            score_grad = (probability * (prob_grad - row_dot)).astype(BF)
+            dv_s[keys, :] += dot(probability.astype(BF), g_s[rows, :], 1, 0)
+            dk_s[keys, :] += dot(score_grad, query, 1, 0)
+            dq_s[rows, :] += dot(score_grad, key, 0, 0)
+
+        @pl.loop(0, full)
+        def _(m):
+            step(m, False)
+
+        @pl.loop(full, n + 1)
+        def _(m):
+            @pl.when(block_used(starts, first, m))
+            def _():
+                step(m, True)
+
+        return carry
+
+    lax.fori_loop(0, k_s.shape[0] // BLOCK, one_block, 0)
+    for b in range(4):
+        for a in range(4):
+            rows = pl.ds(pl.multiple_of(place_ref[4 * b + a] * PIECE, PIECE), PIECE)
+            for which, grad in ((0, dq_s), (1, dk_s)):
+                value = grad[rows, :] * (1.0 / math.sqrt(HD))
+                turned = value * cos_ref[rows, :] - pltpu.roll(value, HD // 2, 1) * sin_ref[rows, :]
+                outs[b][which, a] = turned.astype(BF)
+            outs[b][2, a] = dv_s[rows, :].astype(BF)
+
+
+SMEM_SPEC = pl.BlockSpec(memory_space=pltpu.SMEM)
+VMEM_SPEC = pl.BlockSpec(memory_space=pltpu.VMEM)
+
+
+def run_forward(place, starts, messages):
+    tokens = 16 * PIECE
+    blocks = tokens // BLOCK
+    out_shape = [jax.ShapeDtypeStruct((4, PIECE, HD), BF)] * 4
+    out_shape += [
+        jax.ShapeDtypeStruct((tokens, HD), F32),
+        jax.ShapeDtypeStruct((blocks, 8, BLOCK), F32),
+    ]
+    return pl.pallas_call(
+        attention_forward,
+        out_shape=out_shape,
+        in_specs=[SMEM_SPEC] * 2 + [VMEM_SPEC] * 4,
+        out_specs=[VMEM_SPEC] * 6,
+        scratch_shapes=[
+            pltpu.VMEM((tokens, HD), BF),
+            pltpu.VMEM((tokens, HD), BF),
+            pltpu.VMEM((tokens, HD), BF),
+            pltpu.VMEM((blocks, BLOCK, BLOCK), F32),
+            pltpu.VMEM((BLOCK, HD), F32),
+            pltpu.VMEM((BLOCK, HD), F32),
+            pltpu.VMEM((BLOCK, HD), F32),
+        ],
+        compiler_params=pltpu.CompilerParams(vmem_limit_bytes=48 * 2**20),
+        cost_estimate=pl.CostEstimate(
+            flops=2 * tokens * tokens * HD * 2,
+            bytes_accessed=8 * 2**20,
+            transcendentals=tokens * tokens // 2,
+        ),
+    )(place, starts, *messages)
+
+
+def run_backward(place, starts, messages, grads, wide, log_total, cosine, sine_table):
+    tokens = 16 * PIECE
+    return pl.pallas_call(
+        attention_backward,
+        out_shape=[jax.ShapeDtypeStruct((3, 4, PIECE, HD), BF)] * 4,
+        in_specs=[SMEM_SPEC] * 2 + [VMEM_SPEC] * 12,
+        out_specs=[VMEM_SPEC] * 4,
+        scratch_shapes=[pltpu.VMEM((tokens, HD), BF)] * 4 + [pltpu.VMEM((tokens, HD), F32)] * 3,
+        compiler_params=pltpu.CompilerParams(vmem_limit_bytes=52 * 2**20),
+        cost_estimate=pl.CostEstimate(
+            flops=5 * tokens * tokens * HD * 2,
+            bytes_accessed=16 * 2**20,
+            transcendentals=tokens * tokens // 2,
+        ),
+    )(place, starts, *messages, *grads, wide, log_total, cosine, sine_table)
+
+
+def swap_slots(messages):
+    return [messages[0], flip_y(messages[1]), flip_zh(messages[2]), flip_y_zh(messages[3])]
+
+
+def to_tokens(values):
+    return lax.all_to_all(values, "row", split_axis=0, concat_axis=1, tiled=True)
+
+
+def to_width(values):
+    return lax.all_to_all(values, "row", split_axis=1, concat_axis=0, tiled=True)
+
+
+def square_shards(
+    hidden_in,
+    teacher,
+    valid,
+    segment_ids,
+    query_weight,
+    key_weight,
+    value_weight,
+    output_weight,
+    gate_weight,
+    up_weight,
+    down_weight,
+):
+    row, col, dp = lax.axis_index("row"), lax.axis_index("col"), lax.axis_index("dp")
+    x, y = row % 2, row // 2
+    place = (x, y, dp)
+    own_piece = col * SIDE + row
+    segment = segment_ids[0]
+    group_tokens = segment.shape[0]
+    home_tokens = group_tokens // (SIDE * SIDE)
+    unit_width = gate_weight.shape[1]
+
+    hidden = to_tokens(hidden_in).astype(F32)
+    normed, inverse_one = local_norm(hidden)
+    normed_blocks = square_gather(normed.astype(BF))
+
+    lead = (dp + y) % 2
+    attn_weights = gather_weights(
+        jnp.stack((query_weight, key_weight, value_weight, output_weight.T)), place, lead
+    )
+    qkv_weight = jnp.concatenate((attn_weights[0], attn_weights[1], attn_weights[2]), axis=1)
+    out_weight = attn_weights[3]
+    mlp_weights = gather_weights(jnp.stack((gate_weight, up_weight)), place, 0)
+    gate_full, up_full = mlp_weights[0], mlp_weights[1]
+    down_full = gather_weights(down_weight.T[None], place, 0)[0]
+
+    labels = jnp.arange(1, CONT + 1, dtype=jnp.int32)
+    starts = jnp.sum((segment[None, :] < labels[:, None]).astype(jnp.int32), axis=1)
+    codes = jnp.arange(16, dtype=jnp.int32)
+    relative = (
+        (codes & 1) + ((codes >> 2) & 1) * 2 + ((codes >> 1) & 1) * 4 + ((codes >> 3) & 1) * 8
+    )
+    pieces = relative ^ own_piece
+    cosine, sine_table = rotary(positions(segment))
+    cos_wide = jnp.concatenate((cosine, cosine), axis=1)
+    sin_wide = jnp.concatenate((-sine_table, sine_table), axis=1)
+
+    def turn(values, cos_block, sin_block):
+        heads = values.reshape(home_tokens, 4, HD)
+        swapped = jnp.concatenate((heads[..., HD // 2 :], heads[..., : HD // 2]), axis=-1)
+        return heads * cos_block[:, None] + swapped * sin_block[:, None]
+
+    query_blocks, key_blocks, value_blocks = [], [], []
+    for a in range(4):
+        projected = dot(normed_blocks[a], qkv_weight, 1, 0)
+        cos_block = lax.dynamic_slice_in_dim(cos_wide, pieces[a] * home_tokens, home_tokens, 0)
+        sin_block = lax.dynamic_slice_in_dim(sin_wide, pieces[a] * home_tokens, home_tokens, 0)
+        width = 4 * HD
+        query_blocks.append(turn(projected[:, :width], cos_block, sin_block).astype(BF))
+        key_blocks.append(turn(projected[:, width : 2 * width], cos_block, sin_block).astype(BF))
+        value_blocks.append(projected[:, 2 * width :].reshape(home_tokens, 4, HD).astype(BF))
+    messages = [
+        jnp.stack(
+            [
+                jnp.stack([blocks[a][:, slot] for a in range(4)])
+                for blocks in (query_blocks, key_blocks, value_blocks)
+            ]
+        )
+        for slot in range(4)
+    ]
+    messages = swap_slots(messages)
+    *mixed, wide, log_total = run_forward(pieces, starts, messages)
+    mixed = swap_slots(mixed)
+    attended = [jnp.concatenate([mixed[b][a] for b in range(4)], axis=1) for a in range(4)]
+    after_attention = hidden + square_reduce(lambda a: dot(attended[a], out_weight, 1, 1))
+
+    normed_two, inverse_two = local_norm(after_attention)
+    normed_two_blocks = square_gather(normed_two.astype(BF))
+    gating = [dot(normed_two_blocks[a], gate_full, 1, 0) for a in range(4)]
+    upward = [dot(normed_two_blocks[a], up_full, 1, 0) for a in range(4)]
+    units = [(gating[a] * jax.nn.sigmoid(gating[a]) * upward[a]).astype(BF) for a in range(4)]
+    output = after_attention + square_reduce(lambda a: dot(units[a], down_full, 1, 1))
+
+    counted = valid.astype(F32)
+    total_count = jnp.maximum(sum_all(jnp.sum(counted).reshape(1), False), 1.0)
+    counted_home = lax.dynamic_slice_in_dim(counted, row * home_tokens, home_tokens, 0)[:, None]
+    differ = output - to_tokens(teacher).astype(F32)
+    local_loss = jnp.sum(counted_home * (differ * differ)) / D
+    mean_loss = sum_all(local_loss.reshape(1), True) / total_count
+    all_tokens = group_tokens * lax.axis_size("dp")
+    out_grad = counted_home * differ * (all_tokens / total_count)
+
+    out_blocks = square_gather(out_grad.astype(BF))
+    gate_low, up_low = [], []
+    for a in range(4):
+        units_grad = dot(out_blocks[a], down_full, 1, 0)
+        sigmoid = jax.nn.sigmoid(gating[a])
+        gate_low.append(
+            (units_grad * upward[a] * sigmoid * (1.0 + gating[a] * (1.0 - sigmoid))).astype(BF)
+        )
+        up_low.append((units_grad * (gating[a] * sigmoid)).astype(BF))
+    normed_two_grad = square_reduce(
+        lambda a: dot(gate_low[a], gate_full, 1, 1) + dot(up_low[a], up_full, 1, 1)
+    )
+    middle_grad = out_grad + local_norm_backward(normed_two_grad, normed_two, inverse_two)
+
+    join = lambda blocks: jnp.concatenate(blocks, axis=0)
+    out_wide = join(out_blocks)
+    down_grad = scatter_grads(dot(out_wide, join(units), 0, 0)[None], place, 0)
+    normed_two_wide = join(normed_two_blocks)
+    mlp_grads = scatter_grads(
+        jnp.stack(
+            (dot(normed_two_wide, join(gate_low), 0, 0), dot(normed_two_wide, join(up_low), 0, 0))
+        ),
+        place,
+        0,
+    )
+
+    middle_blocks = square_gather(middle_grad.astype(BF))
+    attended_grad = [dot(middle_blocks[a], out_weight, 1, 0).astype(BF) for a in range(4)]
+    grad_messages = [
+        jnp.stack([attended_grad[a][:, slot * HD : (slot + 1) * HD] for a in range(4)])
+        for slot in range(4)
+    ]
+    grad_messages = swap_slots(grad_messages)
+    back = run_backward(
+        pieces, starts, messages, grad_messages, wide, log_total, cos_wide, sin_wide
+    )
+    back = swap_slots(back)
+    projected_low = [
+        jnp.concatenate([back[b][which, a] for which in range(3) for b in range(4)], axis=1)
+        for a in range(4)
+    ]
+    normed_grad = square_reduce(lambda a: dot(projected_low[a], qkv_weight, 1, 1))
+    input_gradient = middle_grad + local_norm_backward(normed_grad, normed, inverse_one)
+
+    width = 4 * HD
+    qkv_grad = dot(join(normed_blocks), join(projected_low), 0, 0)
+    out_weight_grad = dot(join(middle_blocks), join(attended), 0, 0)
+    attn_grads = scatter_grads(
+        jnp.stack(
+            (
+                qkv_grad[:, :width],
+                qkv_grad[:, width : 2 * width],
+                qkv_grad[:, 2 * width :],
+                out_weight_grad,
+            )
+        ),
+        place,
+        lead,
+    )
+    return (
+        to_width(output.astype(BF)),
+        mean_loss,
+        to_width(input_gradient),
+        attn_grads[0],
+        attn_grads[1],
+        attn_grads[2],
+        attn_grads[3].T,
+        mlp_grads[0],
+        mlp_grads[1],
+        down_grad[0].T,
+    )
+
+
 def solution(mesh):
+    body = square_shards if fits_square(mesh) else shards
     in_specs = (
         P(("dp", "col"), "row"),
         P(("dp", "col"), "row"),
@@ -359,4 +886,4 @@
         P("row", "col"),
         P("col", "row"),
     )
-    return jax.shard_map(shards, mesh=mesh, in_specs=in_specs, out_specs=out_specs, check_vma=False)
+    return jax.shard_map(body, mesh=mesh, in_specs=in_specs, out_specs=out_specs, check_vma=False)

time: 4220 us -> 1620 us (0.38)
  waiting for transfers between devices: 3380 us -> 610 us
  local copies, waits for them, and re-layouts: 83.2 us -> 313 us
  matrix products: 422 us -> 203 us
  starting transfers between devices: 1.04 us -> 171 us
  blocking collectives: 99.8 us -> 0 us
  Pallas kernels: 0 us -> 70.3 us
    reduce_scatter x9 -> x0, waiting for transfers between devices: 1280 us -> none  [the longest x3 588 us: row_product(): lax.psum_scatter(lax.dot_general(full, matrix, (((1,), (contract,)), ((),...]
    unnamed x22 -> x0, waiting for transfers between devices: 1110 us -> none
    all_gather x10 -> x0, waiting for transfers between devices: 987 us -> none  [the longest x4 586 us: collect(): return lax.all_gather(values, 'row', axis=0, tiled=True)]
    ppermute x0 -> x95, waiting for transfers between devices: none -> 610 us  [the longest x80 567 us: flip(): return lax.ppermute(values, axis, [(i, i ^ bit) for i in range(SIDE)])]
    dot_general x26 -> x45, matrix products: 422 us -> 203 us  [dot(): lax.dot_general(left, right, (((a,), (b,)), ((), ())), preferred_element_...]
    ppermute x0 -> x95, starting transfers between devices: none -> 153 us  [the longest x80 142 us: flip(): return lax.ppermute(values, axis, [(i, i ^ bit) for i in range(SIDE)])]
    psum x6 -> x0, blocking collectives: 99.8 us -> none  [the longest x4 41.7 us: feature_sums(): return lax.psum((jnp.sum(left, axis=1), jnp.sum(right, axis=1)), 'row')]
    slice x6 -> x62, local copies, waits for them, and re-layouts: 20.2 us -> 94.6 us  [the longest x2 23.4 us: square_shards(): gate_full, up_full = (mlp_weights[0], mlp_weights[1])]
  transfers between devices with their start and end apart: 21 -> 99, of which waited for: 20 -> 48; matrix products, arithmetic and copies ran while one was open for 3% -> 37% of each run, Pallas kernels for 0% -> 4%
where the time goes in v1:
time: 1620 us; the launch traced here: 1600 us
  waiting for transfers between devices  610 us (38%)
  local copies, waits for them, and re-layouts  313 us (19%)
  other arithmetic  220 us (14%)
  matrix products  203 us (13%)
  starting transfers between devices  171 us (11%)
  Pallas kernels  70.3 us (4%)
    ppermute x80, waiting for transfers between devices, flip(): return lax.ppermute(values, axis, [(i, i ^ bit) for i in range(SIDE)])  567 us
    dot_general x45, matrix products, dot(): lax.dot_general(left, right, (((a,), (b,)), ((), ())), preferred_element_...  203 us
    ppermute x80, starting transfers between devices, flip(): return lax.ppermute(values, axis, [(i, i ^ bit) for i in range(SIDE)])  142 us
    unnamed x483, local copies, waits for them, and re-layouts  94.5 us
    select_n x20, other arithmetic, ordered(): jnp.where(flag == 0, jnp.concatenate((own, other), axis=axis), jnp.concat...  62.4 us
    ppermute x4, waiting for transfers between devices, flip_y_zh(): return lax.ppermute(values, ('row', 'col'), pairs)  42.6 us
    pallas_call x1, Pallas kernels, run_backward(): pl.pallas_call(attention_backward, out_shape=[jax.ShapeDtypeStruct((3, 4,...  40.3 us
  transfers between devices with their start and end apart: 99, of which 48 were waited for; matrix products, arithmetic and copies ran while one was open for 37% of the time, Pallas kernels for 4%

profile of v1, /device:TPU:0, one launch (start us, length us, event | category | flops | bytes accessed | tf_op | source)
XLA Modules:
  0.0 1601.8 jit_solution(10623542938114676482)
XLA Ops:
  40.1 38.6 %collective-permute-done.1 = bf16[4,1024,128]{1,2,0:T(8,128)(2,1)S(1)} collective-permute-done((bf16[4,1024,128]{1,2,0:T(8,128)(2,1)}, bf16[4,1024,128]{1,2,0:T(8,128)(2,1)S(1)}, u32[]{:S(2)}, u32[]{:S(2)}) %collective-permute-start.1) | collective-permute-done | bytes 1048608 | tf_op jit(solution)/shard_map/ppermute | solution.py:349
  114.1 21.5 %collective-permute-done.2 = bf16[4,1024,2,128]{1,3,2,0:T(8,128)(2,1)} collective-permute-done((bf16[4,1024,2,128]{1,3,2,0:T(8,128)(2,1)}, bf16[4,1024,2,128]{1,3,2,0:T(8,128)(2,1)}, u32[]{:S(2)}, u32[]{:S(2)}) %collective-permute-start.2) | collective-permute-done | bytes 2097184 | tf_op jit(solution)/shard_map/ppermute | solution.py:349
  154.9 47.0 %collective-permute-start.49 = (f32[1]{0:T(128)}, f32[1]{0:T(128)}, u32[]{:S(2)}, u32[]{:S(2)}) collective-permute-start(f32[1]{0:T(128)} %add.436), channel_id=1, source_target_pairs={{0,2},{1,3},{2,0},{3,1},{4,6},{5,7},{6,4},{7,5},{8,10},{9,11},{10,... | collective-permute-start | bytes 20 | tf_op jit(solution)/shard_map/ppermute | solution.py:349
  205.6 38.8 %collective-permute-done.49 = f32[1]{0:T(128)} collective-permute-done((f32[1]{0:T(128)}, f32[1]{0:T(128)}, u32[]{:S(2)}, u32[]{:S(2)}) %collective-permute-start.49) | collective-permute-done | bytes 36 | tf_op jit(solution)/shard_map/ppermute | solution.py:349
  398.2 34.5 %collective-permute-done.11.refs_2_ = bf16[3,4,256,128]{3,2,1,0:T(8,128)(2,1)S(1)} collective-permute-done((bf16[3,4,256,128]{3,2,1,0:T(8,128)(2,1)}, bf16[3,4,256,128]{3,2,1,0:T(8,128)(2,1)S(1)}, u32[]{:S(2)}, u32[]{:S(2)}) %collective-permute-start.11) | collective-permute-done | bytes 786464 | tf_op jit(solution)/shard_map/ppermute | solution.py:349
  432.7 16.4 %collective-permute-done.12.refs_3_ = bf16[3,4,256,128]{3,2,1,0:T(8,128)(2,1)S(1)} collective-permute-done((bf16[3,4,256,128]{3,2,1,0:T(8,128)(2,1)}, bf16[3,4,256,128]{3,2,1,0:T(8,128)(2,1)S(1)}, u32[]{:S(2)}, u32[]{:S(2)}) %collective-permute-start.12) | collective-permute-done | bytes 786464 | tf_op jit(solution)/shard_map/ppermute | solution.py:372
  449.2 30.0 %shard_map.186 = (bf16[4,256,128]{2,1,0:T(8,128)(2,1)S(1)}, bf16[4,256,128]{2,1,0:T(8,128)(2,1)S(1)}, bf16[4,256,128]{2,1,0:T(8,128)(2,1)S(1)}, bf16[4,256,128]{...) custom-call(s32[16]{0:T(128)S(1)} %fusion.206.place_ref, s32[8]{0:T(128)S(1)} %convert_reduce_fusion.2.starts_ref, ...), custom_call_target="tpu_custom_call" | custom-call | flops 8589934592 | bytes 8388608 | tf_op jit(solution)/shard_map/pallas_call | solution.py:645
  492.8 17.4 %collective-permute-done.14 = bf16[4,256,128]{2,1,0:T(8,128)(2,1)S(1)} collective-permute-done((bf16[4,256,128]{2,1,0:T(8,128)(2,1)S(1)}, bf16[4,256,128]{2,1,0:T(8,128)(2,1)S(1)}, u32[]{:S(2)}, u32[]{:S(2)}) %collective-permute-start.14) | collective-permute-done | bytes 262176 | tf_op jit(solution)/shard_map/ppermute | solution.py:349
  600.5 11.4 fusion.3
  611.9 11.5 copy.605
  642.1 11.9 copy.606
  817.6 13.8 convolution_convert_fusion.1
  831.4 13.1 convolution_convert_fusion.2
  853.3 11.9 convolution_convert_fusion
  884.5 11.4 copy.629
  981.8 14.1 collective-permute-done.69.refs_6_
  1001.0 40.3 %shard_map.187 = (bf16[3,4,256,128]{3,2,1,0:T(8,128)(2,1)S(1)}, bf16[3,4,256,128]{3,2,1,0:T(8,128)(2,1)}, bf16[3,4,256,128]{3,2,1,0:T(8,128)(2,1)}, bf16[3,4,256,128]{3,2,1,0:T(8,128)(2,1)}) custom-call(s32[16]{0:T(128)S(1)} %copy-done.2, s32[8]{0:T(128)S(1)} %copy-done.4, bf16[3,4,256,128]{3,2,1,0:T(8,128)(2,1)} %copy-done, ...), custom_call_target="tpu_custom_call" | custom-call | flops 21474836480 | bytes 16777216 | tf_op jit(solution)/shard_map/pallas_call | solution.py:670
  1061.5 33.7 %collective-permute-done.72 = bf16[3,4,256,128]{3,2,1,0:T(8,128)(2,1)} collective-permute-done((bf16[3,4,256,128]{3,2,1,0:T(8,128)(2,1)}, bf16[3,4,256,128]{3,2,1,0:T(8,128)(2,1)}, u32[]{:S(2)}, u32[]{:S(2)}) %collective-permute-start.72) | collective-permute-done | bytes 786464 | tf_op jit(solution)/shard_map/ppermute | solution.py:349
  1096.2 15.8 collective-permute-done.73
  1225.6 59.6 %collective-permute-done.91 = bf16[1,1024,2,512]{1,0,3,2:T(2,128)(2,1)} collective-permute-done((bf16[1,1024,2,512]{1,0,3,2:T(2,128)(2,1)}, bf16[1,1024,2,512]{1,0,3,2:T(2,128)(2,1)}, u32[]{:S(2)}, u32[]{:S(2)}) %collective-permute-start.91) | collective-permute-done | bytes 2097184 | tf_op jit(solution)/shard_map/ppermute | solution.py:349
  1314.1 61.0 %collective-permute-done.86 = bf16[2,1024,2,512]{3,1,2,0:T(8,128)(2,1)} collective-permute-done((bf16[2,1024,2,512]{3,1,2,0:T(8,128)(2,1)}, bf16[2,1024,2,512]{3,1,2,0:T(8,128)(2,1)}, u32[]{:S(2)}, u32[]{:S(2)}) %collective-permute-start.86) | collective-permute-done | bytes 4194336 | tf_op jit(solution)/shard_map/ppermute | solution.py:349
  1390.3 28.9 %collective-permute-done.81 = bf16[4,1024,2,128]{3,1,2,0:T(8,128)(2,1)} collective-permute-done((bf16[4,1024,2,128]{3,1,2,0:T(8,128)(2,1)}, bf16[4,1024,2,128]{3,1,2,0:T(8,128)(2,1)}, u32[]{:S(2)}, u32[]{:S(2)}) %collective-permute-start.81) | collective-permute-done | bytes 2097184 | tf_op jit(solution)/shard_map/ppermute | solution.py:349
  1434.2 61.6 %collective-permute-done.87 = bf16[2,1024,512]{2,1,0:T(8,128)(2,1)} collective-permute-done((bf16[2,1024,512]{2,1,0:T(8,128)(2,1)}, bf16[2,1024,512]{2,1,0:T(8,128)(2,1)}, u32[]{:S(2)}, u32[]{:S(2)}) %collective-permute-start.87) | collective-permute-done | bytes 2097184 | tf_op jit(solution)/shard_map/ppermute | solution.py:349
  1502.7 15.5 collective-permute-done.82
  (954 shorter events, 928.1 us)
Async XLA Ops:
  8.0 96.8 %all-to-all-start = ((bf16[4,256,512]{2,1,0:T(8,128)(2,1)}), bf16[4,256,512]{2,1,0:T(8,128)(2,1)S(1)}, u32[]{:S(2)}, u32[]{:S(2)}) async-start(bf16[4,256,512]{2,1,0:T(8,128)(2,1)} %bitcast), calls=%async_computation | async-start | bytes 2097152 | tf_op jit(solution)/shard_map/all_to_all | solution.py:690
  13.4 86.9 %collective-permute-start.26 = (bf16[1,512,512]{1,2,0:T(8,128)(2,1)}, bf16[1,512,512]{1,2,0:T(8,128)(2,1)}, u32[]{:S(2)}, u32[]{:S(2)}) collective-permute-start(bf16[1,512,512]{1,2,0:T(8,128)(2,1)} %get-tuple-element.142), channel_id=1, source_target_pairs={{0,4},{4,0},{8,12},{12,8},{1,5},{5,1},{9,13},{13,9},{2,6},{6,2},{1... | collective-permute-start | bytes 1572872 | tf_op jit(solution)/shard_map/ppermute | solution.py:349
  27.2 119.3 %collective-permute-start.22 = (bf16[2,512,512]{2,1,0:T(8,128)(2,1)}, bf16[2,512,512]{2,1,0:T(8,128)(2,1)}, u32[]{:S(2)}, u32[]{:S(2)}) collective-permute-start(bf16[2,512,512]{2,1,0:T(8,128)(2,1)} %bitcast.126), channel_id=1, source_target_pairs={{0,4},{4,0},{8,12},{12,8},{1,5},{5,1},{9,13},{13,9},{2,6},{6,2},{1... | collective-permute-start | bytes 3145736 | tf_op jit(solution)/shard_map/ppermute | solution.py:349
  104.9 144.9 %all-to-all-start.2 = ((bf16[4,256,512]{2,1,0:T(8,128)(2,1)}), bf16[4,256,512]{2,1,0:T(8,128)(2,1)}, u32[]{:S(2)}, u32[]{:S(2)}) async-start(bf16[4,256,512]{2,1,0:T(8,128)(2,1)} %bitcast.153), calls=%async_computation.2 | async-start | bytes 2097152 | tf_op jit(solution)/shard_map/all_to_all | solution.py:690
  140.7 162.3 %collective-permute-start.3 = (bf16[4,2048,2,128]{1,3,2,0:T(8,128)(2,1)}, bf16[4,2048,2,128]{1,3,2,0:T(8,128)(2,1)}, u32[]{:S(2)}, u32[]{:S(2)}) collective-permute-start(bf16[4,2048,2,128]{1,3,2,0:T(8,128)(2,1)} %maximum_select_fusion.3), channel_id=1, source_target_pairs={{0,16},{16,0},{1,17},{17,1},{2,18},{18,2},{3,19},{19,3},{4,20},{20... | collective-permute-start | bytes 12582920 | tf_op jit(solution)/shard_map/ppermute | solution.py:376
  144.0 103.5 %collective-permute-start.6 = (bf16[128,2048]{1,0:T(8,128)(2,1)}, bf16[128,2048]{1,0:T(8,128)(2,1)S(1)}, u32[]{:S(2)}, u32[]{:S(2)}) collective-permute-start(bf16[128,2048]{1,0:T(8,128)(2,1)} %get-tuple-element.183), channel_id=1, source_target_pairs={{0,1},{1,0},{2,3},{3,2},{4,5},{5,4},{6,7},{7,6},{8,9},{9,8},{10,11... | collective-permute-start | bytes 1572872 | tf_op jit(solution)/shard_map/ppermute | solution.py:349
  144.7 111.1 %collective-permute-start.4 = (bf16[128,2048]{1,0:T(8,128)(2,1)}, bf16[128,2048]{1,0:T(8,128)(2,1)}, u32[]{:S(2)}, u32[]{:S(2)}) collective-permute-start(bf16[128,2048]{1,0:T(8,128)(2,1)} %get-tuple-element.183), channel_id=1, source_target_pairs={{0,4},{4,0},{8,12},{12,8},{1,5},{5,1},{9,13},{13,9},{2,6},{6,2},{1... | collective-permute-start | bytes 1572872 | tf_op jit(solution)/shard_map/ppermute | solution.py:349
  150.1 133.1 %collective-permute-start.23 = (bf16[2,1024,512]{2,1,0:T(8,128)(2,1)}, bf16[2,1024,512]{2,1,0:T(8,128)(2,1)}, u32[]{:S(2)}, u32[]{:S(2)}) collective-permute-start(bf16[2,1024,512]{2,1,0:T(8,128)(2,1)} %maximum_select_fusion.8), channel_id=1, source_target_pairs={{0,2},{1,3},{2,0},{3,1},{4,6},{5,7},{6,4},{7,5},{8,10},{9,11},{10,... | collective-permute-start | bytes 6291464 | tf_op jit(solution)/shard_map/ppermute | solution.py:349
  154.9 89.5 %collective-permute-start.49 = (f32[1]{0:T(128)}, f32[1]{0:T(128)}, u32[]{:S(2)}, u32[]{:S(2)}) collective-permute-start(f32[1]{0:T(128)} %add.436), channel_id=1, source_target_pairs={{0,2},{1,3},{2,0},{3,1},{4,6},{5,7},{6,4},{7,5},{8,10},{9,11},{10,... | collective-permute-start | bytes 20 | tf_op jit(solution)/shard_map/ppermute | solution.py:349
  288.0 192.7 %collective-permute-start.24 = (bf16[2,1024,2,512]{3,1,0,2:T(8,128)(2,1)}, bf16[2,1024,2,512]{3,1,0,2:T(8,128)(2,1)}, u32[]{:S(2)}, u32[]{:S(2)}) collective-permute-start(bf16[2,1024,2,512]{3,1,0,2:T(8,128)(2,1)} %get-tuple-element.122), channel_id=1, source_target_pairs={{0,8},{4,12},{8,0},{12,4},{1,9},{5,13},{9,1},{13,5},{2,10},{6,14},... | collective-permute-start | bytes 12582920 | tf_op jit(solution)/shard_map/ppermute | solution.py:349
  299.1 266.2 %collective-permute-start.29 = (bf16[1,2048,2,512]{1,3,2,0:T(8,128)(2,1)}, bf16[1,2048,2,512]{1,3,2,0:T(8,128)(2,1)}, u32[]{:S(2)}, u32[]{:S(2)}) collective-permute-start(bf16[1,2048,2,512]{1,3,2,0:T(8,128)(2,1)} %maximum_select_fusion.5), channel_id=1, source_target_pairs={{0,16},{16,0},{1,17},{17,1},{2,18},{18,2},{3,19},{19,3},{4,20},{20... | collective-permute-start | bytes 12582920 | tf_op jit(solution)/shard_map/ppermute | solution.py:376
  489.6 110.9 %collective-permute-start.25 = (bf16[2,2048,2,512]{3,1,0,2:T(8,128)(2,1)}, bf16[2,2048,2,512]{3,1,0,2:T(8,128)(2,1)}, u32[]{:S(2)}, u32[]{:S(2)}) collective-permute-start(bf16[2,2048,2,512]{3,1,0,2:T(8,128)(2,1)} %maximum_select_fusion.2), channel_id=1, source_target_pairs={{0,16},{16,0},{1,17},{17,1},{2,18},{18,2},{3,19},{19,3},{4,20},{20... | collective-permute-start | bytes 25165832 | tf_op jit(solution)/shard_map/ppermute | solution.py:376
  766.7 136.8 %collective-permute-start.59 = (bf16[128,2048]{1,0:T(8,128)(2,1)}, bf16[128,2048]{1,0:T(8,128)(2,1)S(1)}, u32[]{:S(2)}, u32[]{:S(2)}) collective-permute-start(bf16[128,2048]{1,0:T(8,128)(2,1)} %slice.1384), channel_id=1, source_target_pairs={{0,4},{4,0},{8,12},{12,8},{1,5},{5,1},{9,13},{13,9},{2,6},{6,2},{1... | collective-permute-start | bytes 1572872 | tf_op jit(solution)/shard_map/ppermute | solution.py:349
  783.6 120.4 %collective-permute-start.58 = (bf16[128,2048]{1,0:T(8,128)(2,1)}, bf16[128,2048]{1,0:T(8,128)(2,1)}, u32[]{:S(2)}, u32[]{:S(2)}) collective-permute-start(bf16[128,2048]{1,0:T(8,128)(2,1)} %slice.1385), channel_id=1, source_target_pairs={{0,1},{1,0},{2,3},{3,2},{4,5},{5,4},{6,7},{7,6},{8,9},{9,8},{10,11... | collective-permute-start | bytes 1572872 | tf_op jit(solution)/shard_map/ppermute | solution.py:349
  895.9 272.5 %collective-permute-start.90 = (bf16[1,2048,2,512]{1,3,2,0:T(8,128)(2,1)}, bf16[1,2048,2,512]{1,3,2,0:T(8,128)(2,1)}, u32[]{:S(2)}, u32[]{:S(2)}) collective-permute-start(bf16[1,2048,2,512]{1,3,2,0:T(8,128)(2,1)} %slice_bitcast_fusion), channel_id=1, source_target_pairs={{0,16},{16,0},{1,17},{17,1},{2,18},{18,2},{3,19},{19,3},{4,20},{20... | collective-permute-start | bytes 12582920 | tf_op jit(solution)/shard_map/ppermute | solution.py:376
  903.5 287.9 %collective-permute-start.85 = (bf16[2,2048,2,512]{3,1,2,0:T(8,128)(2,1)}, bf16[2,2048,2,512]{3,1,2,0:T(8,128)(2,1)}, u32[]{:S(2)}, u32[]{:S(2)}) collective-permute-start(bf16[2,2048,2,512]{3,1,2,0:T(8,128)(2,1)} %fusion.4), channel_id=1, source_target_pairs={{0,16},{16,0},{1,17},{17,1},{2,18},{18,2},{3,19},{19,3},{4,20},{20... | collective-permute-start | bytes 25165832 | tf_op jit(solution)/shard_map/ppermute | solution.py:376
  927.0 502.6 %all-to-all-start.1 = ((bf16[256,4,512]{2,0,1:T(8,128)(2,1)}), bf16[256,4,512]{2,0,1:T(8,128)(2,1)}, u32[]{:S(2)}, u32[]{:S(2)}) async-start(bf16[256,4,512]{2,0,1:T(8,128)(2,1)} %copy.610), calls=%async_computation.1 | async-start | bytes 2097152 | tf_op jit(solution)/shard_map/all_to_all | solution.py:694
  1166.4 138.7 %collective-permute-start.80 = (bf16[4,2048,2,128]{3,1,2,0:T(8,128)(2,1)}, bf16[4,2048,2,128]{3,1,2,0:T(8,128)(2,1)}, u32[]{:S(2)}, u32[]{:S(2)}) collective-permute-start(bf16[4,2048,2,128]{3,1,2,0:T(8,128)(2,1)} %dynamic-slice_bitcast_fusion.2), channel_id=1, source_target_pairs={{0,16},{16,0},{1,17},{17,1},{2,18},{18,2},{3,19},{19,3},{4,20},{20... | collective-permute-start | bytes 12582920 | tf_op jit(solution)/shard_map/ppermute | solution.py:376
  1191.4 93.7 %collective-permute-start.91 = (bf16[1,1024,2,512]{1,0,3,2:T(2,128)(2,1)}, bf16[1,1024,2,512]{1,0,3,2:T(2,128)(2,1)}, u32[]{:S(2)}, u32[]{:S(2)}) collective-permute-start(bf16[1,1024,2,512]{1,0,3,2:T(2,128)(2,1)} %dynamic-slice_bitcast_fusion), channel_id=1, source_target_pairs={{0,8},{4,12},{8,0},{12,4},{1,9},{5,13},{9,1},{13,5},{2,10},{6,14},... | collective-permute-start | bytes 6291464 | tf_op jit(solution)/shard_map/ppermute | solution.py:349
  1206.0 169.0 %collective-permute-start.86 = (bf16[2,1024,2,512]{3,1,2,0:T(8,128)(2,1)}, bf16[2,1024,2,512]{3,1,2,0:T(8,128)(2,1)}, u32[]{:S(2)}, u32[]{:S(2)}) collective-permute-start(bf16[2,1024,2,512]{3,1,2,0:T(8,128)(2,1)} %dynamic-slice_bitcast_fusion.1), channel_id=1, source_target_pairs={{0,8},{4,12},{8,0},{12,4},{1,9},{5,13},{9,1},{13,5},{2,10},{6,14},... | collective-permute-start | bytes 12582920 | tf_op jit(solution)/shard_map/ppermute | solution.py:349
  1312.9 106.3 %collective-permute-start.81 = (bf16[4,1024,2,128]{3,1,2,0:T(8,128)(2,1)}, bf16[4,1024,2,128]{3,1,2,0:T(8,128)(2,1)}, u32[]{:S(2)}, u32[]{:S(2)}) collective-permute-start(bf16[4,1024,2,128]{3,1,2,0:T(8,128)(2,1)} %dynamic-slice_bitcast_fusion.3), channel_id=1, source_target_pairs={{0,8},{4,12},{8,0},{12,4},{1,9},{5,13},{9,1},{13,5},{2,10},{6,14},... | collective-permute-start | bytes 6291464 | tf_op jit(solution)/shard_map/ppermute | solution.py:349
  1381.1 114.7 %collective-permute-start.87 = (bf16[2,1024,512]{2,1,0:T(8,128)(2,1)}, bf16[2,1024,512]{2,1,0:T(8,128)(2,1)}, u32[]{:S(2)}, u32[]{:S(2)}) collective-permute-start(bf16[2,1024,512]{2,1,0:T(8,128)(2,1)} %slice_bitcast_fusion.2), channel_id=1, source_target_pairs={{0,2},{1,3},{2,0},{3,1},{4,6},{5,7},{6,4},{7,5},{8,10},{9,11},{10,... | collective-permute-start | bytes 6291464 | tf_op jit(solution)/shard_map/ppermute | solution.py:349
  1423.1 95.1 %collective-permute-start.82 = (bf16[4,1024,128]{2,1,0:T(8,128)(2,1)}, bf16[4,1024,128]{2,1,0:T(8,128)(2,1)}, u32[]{:S(2)}, u32[]{:S(2)}) collective-permute-start(bf16[4,1024,128]{2,1,0:T(8,128)(2,1)} %slice_bitcast_fusion.4), channel_id=1, source_target_pairs={{0,2},{1,3},{2,0},{3,1},{4,6},{5,7},{6,4},{7,5},{8,10},{9,11},{10,... | collective-permute-start | bytes 3145736 | tf_op jit(solution)/shard_map/ppermute | solution.py:349
  1429.6 121.3 %all-to-all-start.3 = ((f32[256,4,512]{2,0,1:T(8,128)}), f32[256,4,512]{2,0,1:T(8,128)}, u32[]{:S(2)}, u32[]{:S(2)}) async-start(f32[256,4,512]{2,0,1:T(8,128)} %copy.617), calls=%async_computation.3 | async-start | bytes 4194304 | tf_op jit(solution)/shard_map/all_to_all | solution.py:694
  (287 other events, 6215.1 us)

commit v2 on v1

--- a/solution.py
+++ b/solution.py
@@ -339,6 +339,10 @@
 F32 = jnp.float32
 LOG2E = 1.4426950408889634
 SIDE = 4
+HALF = D // 2
+PIECE = 256
+BLOCK = 512
+SLOTS = [(d, h) for h in range(2) for d in range(2)]
 
 
 def fits_square(mesh):
@@ -376,39 +380,29 @@
     return lax.ppermute(values, "dp", [(0, 1), (1, 0)])
 
 
-def sum_all(value, with_row):
-    value = value + flip_dp(value)
-    value = value + flip_zl(value)
-    value = value + flip_zh(value)
-    if with_row:
-        value = value + flip_x(value)
-        value = value + flip_y(value)
-    return value
-
-
-def square_gather(block):
+def flip_dp_y(values):
+    pairs = [(g * SIDE + r, (1 - g) * SIDE + (r ^ 2)) for g in range(2) for r in range(SIDE)]
+    return lax.ppermute(values, ("dp", "row"), pairs)
+
+
+def square_gather(block, *events):
     half = block.shape[0] // 2
-    top, bottom = block[:half], block[half:]
-    x_top, z_bottom = flip_x(top), flip_zl(bottom)
-    x_bottom, z_top = flip_x(bottom), flip_zl(top)
-    d_top, d_bottom = flip_zl(x_top), flip_x(z_bottom)
-    join = lambda a, b: jnp.concatenate((a, b), axis=0)
-    return [block, join(x_top, x_bottom), join(z_top, z_bottom), join(d_top, d_bottom)]
-
-
-def square_reduce(make):
-    far = make(3)
-    half = far.shape[0] // 2
-    far = far.astype(BF)
-    far_top, far_bottom = flip_zl(far[:half]), flip_x(far[half:])
-    by_x, by_z = make(1), make(2)
-    x_bottom = flip_x(by_x[half:].astype(BF))
-    z_top = flip_zl(by_z[:half].astype(BF))
-    x_top = flip_x((by_x[:half] + far_top.astype(F32)).astype(BF))
-    z_bottom = flip_zl((by_z[half:] + far_bottom.astype(F32)).astype(BF))
-    own = make(0)
-    top = own[:half] + x_top.astype(F32) + z_top.astype(F32)
-    bottom = own[half:] + x_bottom.astype(F32) + z_bottom.astype(F32)
+    by_x, by_z = flip_x(block), flip_zl(block)
+    next_x, next_z = after((by_x, by_z), *events) if events else (by_x, by_z)
+    return [block, by_x, by_z, flip_zl(next_x[:half]), flip_x(next_z[half:])]
+
+
+def square_reduce(far, sides, own, *events):
+    x_top, x_bottom, z_top, z_bottom = sides
+    far_top, far_bottom = flip_zl(far[0]), flip_x(far[1])
+    got_x_bottom, got_z_top = flip_x(x_bottom), flip_zl(z_top)
+    if events:
+        far_top, far_bottom = after((far_top, far_bottom), *events)
+    got_x_top = flip_x((x_top + far_top.astype(F32)).astype(BF))
+    got_z_bottom = flip_zl((z_bottom + far_bottom.astype(F32)).astype(BF))
+    half = far_top.shape[0]
+    top = own[:half] + got_x_top.astype(F32) + got_z_top.astype(F32)
+    bottom = own[half:] + got_x_bottom.astype(F32) + got_z_bottom.astype(F32)
     return jnp.concatenate((top, bottom), axis=0)
 
 
@@ -420,41 +414,62 @@
     )
 
 
-def pick(values, index, axis):
-    return lax.dynamic_index_in_dim(values, index, axis, keepdims=False)
-
-
-def gather_weights(matrices, place, lead):
-    x, y, dp = place
-    m, rows, n = matrices.shape
-    cut = matrices.reshape(m, rows, 2, 2, n // 4)
-    cut = pick(cut, dp, 3)
-    own, send = pick(cut, x, 2), pick(cut, 1 - x, 2)
-    tall = ordered(x, own, flip_x(send), 1)
-    pair = jnp.stack((tall, flip_zh(tall)), axis=2)
-    full = ordered(y, pair, flip_y(pair), 1)
-    other = flip_dp(full)
-    slots = ordered(lead, full[:, :, :, None], other[:, :, :, None], 3)
-    return slots.reshape(m, 4 * rows, n)
-
-
-def scatter_grads(grads, place, lead):
-    x, y, dp = place
-    m, depth, n = grads.shape
-    rows = depth // 4
-    cut = grads.astype(BF).reshape(m, depth, 2, 2, n // 4)
-    keep, send = pick(cut, lead, 3), pick(cut, 1 - lead, 3)
-    total = (keep.astype(F32) + flip_dp(send).astype(F32)).astype(BF)
-    total = total.reshape(m, 2, 2 * rows, 2, n // 4)
-    keep, send = pick(total, y, 1), pick(total, 1 - y, 1)
-    total = (keep.astype(F32) + flip_y(send).astype(F32)).astype(BF)
-    keep, send = total[:, :, 0], total[:, :, 1]
-    total = (keep.astype(F32) + flip_zh(send).astype(F32)).astype(BF)
-    total = total.reshape(m, 2, rows, n // 4)
-    keep, send = pick(total, x, 1), pick(total, 1 - x, 1)
-    both = ordered(x, keep[:, :, None], flip_x(send)[:, :, None], 2)
-    whole = ordered(dp, both[:, :, :, None], flip_dp(both)[:, :, :, None], 3)
-    return whole.reshape(m, rows, n).astype(F32)
+def after(values, *events):
+    return lax.optimization_barrier((values, events))[0]
+
+
+def other_core(quarter):
+    return [flip_dp(piece) for piece in quarter]
+
+
+def piece_list(tall, high, by_y, by_y_high, others):
+    other_tall, other_y, other_high, other_y_high = others
+    return [tall, by_y, other_tall, other_y, high, by_y_high, other_high, other_y_high]
+
+
+def wide(values):
+    return values.astype(F32)
+
+
+class Spread:
+    def __init__(self, grads):
+        self.keep, self.send = grads
+
+    def to_core(self, *events):
+        self.got = flip_dp(after(self.send, *events))
+        return self.got
+
+    def here(self, y, h):
+        return wide(self.keep[y, h]) + wide(self.got[y, h])
+
+    def to_y(self, h, *events):
+        by_y = flip_dp_y(after(self.here(1, h).astype(BF), *events))
+        setattr(self, "by_y%d" % h, by_y)
+        return by_y
+
+    def to_high(self, *events):
+        send = (self.here(0, 1) + wide(self.by_y1)).astype(BF)
+        self.high = flip_zh(after(send, *events))
+        return self.high
+
+    def to_x(self, x, axis, *events):
+        total = self.here(0, 0) + wide(self.by_y0) + wide(self.high)
+        total = after(total.astype(BF), *events)
+        size = total.shape[axis] // 2
+        own = lax.dynamic_slice_in_dim(total, x * size, size, axis)
+        other = flip_x(lax.dynamic_slice_in_dim(total, (1 - x) * size, size, axis))
+        self.parts = (own, other)
+        return self.parts
+
+
+def unite(own, by_x, x, q, axis):
+    other_own, other_x = flip_dp(own), flip_dp(by_x)
+    first = jnp.where(x == 0, own, by_x), jnp.where(x == 0, other_own, other_x)
+    second = jnp.where(x == 0, by_x, own), jnp.where(x == 0, other_x, other_own)
+    parts = []
+    for mine, theirs in (first, second):
+        parts += [jnp.where(q == 0, mine, theirs), jnp.where(q == 0, theirs, mine)]
+    return jnp.concatenate(parts, axis=axis).astype(F32)
 
 
 def local_norm(values):
@@ -474,8 +489,431 @@
     return lax.dot_general(left, right, (((a,), (b,)), ((), ())), preferred_element_type=F32)
 
 
-BLOCK = 512
-PIECE = 256
+SMEM_SPEC = pl.BlockSpec(memory_space=pltpu.SMEM)
+VMEM_SPEC = pl.BlockSpec(memory_space=pltpu.VMEM)
+
+
+def shape(dims, kind):
+    return jax.ShapeDtypeStruct(dims, kind)
+
+
+def params(megabytes):
+    return pltpu.CompilerParams(vmem_limit_bytes=megabytes * 2**20)
+
+
+def cost(flops, moved, transcendentals=0):
+    return pl.CostEstimate(
+        flops=int(flops), bytes_accessed=int(moved), transcendentals=int(transcendentals)
+    )
+
+
+def y_half(y):
+    return slice(y * HALF, (y + 1) * HALF)
+
+
+def columns(index, width):
+    return slice(index * width, (index + 1) * width)
+
+
+FAR_SHAPES = [shape((PIECE // 2, D), BF)] * 2
+SIDE_SHAPES = [
+    shape((PIECE // 2, D), F32),
+    shape((PIECE // 2, D), BF),
+    shape((PIECE // 2, D), BF),
+    shape((PIECE // 2, D), F32),
+]
+OWN_SHAPES = [shape((PIECE, D), F32)]
+SUM_SHAPES = {"far": FAR_SHAPES, "sides": SIDE_SHAPES, "own": OWN_SHAPES}
+SUM_BLOCKS = {"far": (3,), "sides": (1, 2), "own": (0,)}
+
+
+def store_sum(kind, index, part, value, outs):
+    half = PIECE // 2
+    if kind == "own":
+        outs[0][:, y_half(part)] = value
+        return
+    for low in range(2):
+        out = outs[2 * index + low]
+        out[:, y_half(part)] = value[low * half : (low + 1) * half].astype(out.dtype)
+
+
+def qkv_kernel(place_ref, *refs):
+    acts, refs = refs[:5], refs[5:]
+    weights, refs = refs[:8], refs[8:]
+    cos_ref, sin_ref, *refs = refs
+    outs, weight_s = refs[:4], refs[4]
+    for b in range(4):
+        for y in range(2):
+            for which in range(3):
+                weight_s[y_half(y), columns(which * 4 + b, HD)] = weights[2 * b + y][which]
+    for a in range(4):
+        rows = pl.ds(pl.multiple_of(place_ref[a] * PIECE, PIECE), PIECE)
+        cos_block, sin_block = cos_ref[rows, :], sin_ref[rows, :]
+        act = acts[a][...] if a < 3 else jnp.concatenate((acts[3][...], acts[4][...]), axis=0)
+        projected = dot(act, weight_s[...], 1, 0)
+        for which in range(3):
+            for b in range(4):
+                tile = projected[:, columns(which * 4 + b, HD)]
+                if which < 2:
+                    tile = tile * cos_block + pltpu.roll(tile, HD // 2, 1) * sin_block
+                outs[b][which, a] = tile.astype(BF)
+
+
+def run_qkv(place, acts, weights, cos_wide, sin_wide):
+    return pl.pallas_call(
+        qkv_kernel,
+        out_shape=[shape((3, 4, PIECE, HD), BF)] * 4,
+        in_specs=[SMEM_SPEC] + [VMEM_SPEC] * 15,
+        out_specs=[VMEM_SPEC] * 4,
+        scratch_shapes=[pltpu.VMEM((D, 12 * HD), BF)],
+        compiler_params=params(40),
+        cost_estimate=cost(2 * 4 * PIECE * D * 12 * HD, 20 * 2**20),
+    )(place, *acts, *weights, cos_wide, sin_wide)
+
+
+def out_kernel(*refs):
+    mixed, refs = refs[:4], refs[4:]
+    weights, refs = refs[:8], refs[8:]
+    outs, weight_s = refs[:7], refs[7]
+    for b in range(4):
+        for y in range(2):
+            weight_s[y_half(y), columns(b, HD)] = weights[2 * b + y][...]
+    at = 0
+    for kind in ("far", "sides", "own"):
+        for index, a in enumerate(SUM_BLOCKS[kind]):
+            act = jnp.concatenate([mixed[b][a] for b in range(4)], axis=1)
+            for y in range(2):
+                value = dot(act, weight_s[y_half(y), :], 1, 1)
+                store_sum(kind, index, y, value, outs[at:])
+        at += len(SUM_SHAPES[kind])
+
+
+def run_out(mixed, weights):
+    outs = pl.pallas_call(
+        out_kernel,
+        out_shape=FAR_SHAPES + SIDE_SHAPES + OWN_SHAPES,
+        in_specs=[VMEM_SPEC] * 12,
+        out_specs=[VMEM_SPEC] * 7,
+        scratch_shapes=[pltpu.VMEM((D, 4 * HD), BF)],
+        compiler_params=params(36),
+        cost_estimate=cost(2 * 4 * PIECE * D * 4 * HD, 16 * 2**20),
+    )(*mixed, *weights)
+    return outs[:2], outs[2:6], outs[6]
+
+
+def input_kernel(*refs):
+    back, refs = refs[:4], refs[4:]
+    weights, refs = refs[:8], refs[8:]
+    outs, weight_s = refs[:7], refs[7]
+    for b in range(4):
+        for y in range(2):
+            for which in range(3):
+                weight_s[y_half(y), columns(which * 4 + b, HD)] = weights[2 * b + y][which]
+    at = 0
+    for kind in ("far", "sides", "own"):
+        for index, a in enumerate(SUM_BLOCKS[kind]):
+            act = jnp.concatenate(
+                [back[b][which, a] for which in range(3) for b in range(4)], axis=1
+            )
+            for y in range(2):
+                value = dot(act, weight_s[y_half(y), :], 1, 1)
+                store_sum(kind, index, y, value, outs[at:])
+        at += len(SUM_SHAPES[kind])
+
+
+def run_input(back, weights):
+    outs = pl.pallas_call(
+        input_kernel,
+        out_shape=FAR_SHAPES + SIDE_SHAPES + OWN_SHAPES,
+        in_specs=[VMEM_SPEC] * 12,
+        out_specs=[VMEM_SPEC] * 7,
+        scratch_shapes=[pltpu.VMEM((D, 12 * HD), BF)],
+        compiler_params=params(40),
+        cost_estimate=cost(2 * 4 * PIECE * D * 12 * HD, 20 * 2**20),
+    )(*back, *weights)
+    return outs[:2], outs[2:6], outs[6]
+
+
+def attended_grad_kernel(*refs):
+    acts, refs = refs[:5], refs[5:]
+    weights, refs = refs[:8], refs[8:]
+    outs, weight_s = refs[:4], refs[4]
+    for b in range(4):
+        for y in range(2):
+            weight_s[y_half(y), columns(b, HD)] = weights[2 * b + y][...]
+    for a in range(4):
+        act = acts[a][...] if a < 3 else jnp.concatenate((acts[3][...], acts[4][...]), axis=0)
+        value = dot(act, weight_s[...], 1, 0)
+        for b in range(4):
+            outs[b][a] = value[:, columns(b, HD)].astype(BF)
+
+
+def run_attended_grad(acts, weights):
+    return pl.pallas_call(
+        attended_grad_kernel,
+        out_shape=[shape((4, PIECE, HD), BF)] * 4,
+        in_specs=[VMEM_SPEC] * 13,
+        out_specs=[VMEM_SPEC] * 4,
+        scratch_shapes=[pltpu.VMEM((D, 4 * HD), BF)],
+        compiler_params=params(36),
+        cost_estimate=cost(2 * 4 * PIECE * D * 4 * HD, 16 * 2**20),
+    )(*acts, *weights)
+
+
+CHUNK = 256
+
+
+def up_kernel(count, *refs):
+    acts, refs = refs[:count], refs[count:]
+    gates, refs = refs[:8], refs[8:]
+    ups, refs = refs[:8], refs[8:]
+    gating_ref, upward_ref, units_ref = refs
+    start = 0
+    for act_ref in acts:
+        size = act_ref.shape[0]
+        rows = slice(start, start + size)
+        start += size
+        low, high = act_ref[:, y_half(0)], act_ref[:, y_half(1)]
+        for b in range(4):
+            gate = dot(low, gates[2 * b][...], 1, 0) + dot(high, gates[2 * b + 1][...], 1, 0)
+            up = dot(low, ups[2 * b][...], 1, 0) + dot(high, ups[2 * b + 1][...], 1, 0)
+            gating_ref[b, rows] = gate
+            upward_ref[b, rows] = up
+            units_ref[b, rows] = (gate * jax.nn.sigmoid(gate) * up).astype(BF)
+
+
+def run_up(acts, gates, ups):
+    rows = sum(act.shape[0] for act in acts)
+    width = gates[0].shape[1]
+    whole = lambda act: pl.BlockSpec(act.shape, lambda j: (0, 0))
+    piece = pl.BlockSpec((HALF, CHUNK), lambda j: (0, j))
+    out = pl.BlockSpec((4, rows, CHUNK), lambda j: (0, 0, j))
+    return pl.pallas_call(
+        lambda *refs: up_kernel(len(acts), *refs),
+        grid=(width // CHUNK,),
+        out_shape=[shape((4, rows, width), kind) for kind in (F32, F32, BF)],
+        in_specs=[whole(act) for act in acts] + [piece] * 16,
+        out_specs=[out] * 3,
+        compiler_params=params(48),
+        cost_estimate=cost(2 * rows * D * 8 * width, 16 * 2**20, 4 * rows * width),
+    )(*acts, *gates, *ups)
+
+
+def down_kernel(kind, units_ref, *refs):
+    weights, outs = refs[:8], refs[8:]
+    for index in range(len(SUM_BLOCKS[kind])):
+        rows = slice(index * PIECE, (index + 1) * PIECE)
+        for y in range(2):
+            value = dot(units_ref[0, rows], weights[y][...], 1, 0)
+            for b in range(1, 4):
+                value += dot(units_ref[b, rows], weights[2 * b + y][...], 1, 0)
+            store_sum(kind, index, y, value, outs)
+
+
+def run_down(kind, units, weights):
+    rows, width = units.shape[1], units.shape[2]
+    shapes = SUM_SHAPES[kind]
+    return pl.pallas_call(
+        lambda *refs: down_kernel(kind, *refs),
+        out_shape=shapes,
+        in_specs=[VMEM_SPEC] * 9,
+        out_specs=[VMEM_SPEC] * len(shapes),
+        compiler_params=params(36),
+        cost_estimate=cost(2 * rows * D * 4 * width, 12 * 2**20),
+    )(units, *weights)
+
+
+def gated_kernel(count, *refs):
+    acts, refs = refs[:count], refs[count:]
+    gating_ref, upward_ref, *refs = refs
+    weights, refs = refs[:8], refs[8:]
+    gate_ref, up_ref = refs
+    start = 0
+    for act_ref in acts:
+        size = act_ref.shape[0]
+        rows = slice(start, start + size)
+        start += size
+        low, high = act_ref[:, y_half(0)], act_ref[:, y_half(1)]
+        for b in range(4):
+            grad = dot(low, weights[2 * b][...], 1, 1) + dot(high, weights[2 * b + 1][...], 1, 1)
+            gate = gating_ref[b, rows]
+            sigmoid = jax.nn.sigmoid(gate)
+            gate_ref[b, rows] = (
+                grad * upward_ref[b, rows] * sigmoid * (1.0 + gate * (1.0 - sigmoid))
+            ).astype(BF)
+            up_ref[b, rows] = (grad * (gate * sigmoid)).astype(BF)
+
+
+def run_gated(acts, gating, upward, weights):
+    rows, width = gating.shape[1], gating.shape[2]
+    return pl.pallas_call(
+        lambda *refs: gated_kernel(len(acts), *refs),
+        out_shape=[shape((4, rows, width), BF)] * 2,
+        in_specs=[VMEM_SPEC] * (len(acts) + 10),
+        out_specs=[VMEM_SPEC] * 2,
+        compiler_params=params(44),
+        cost_estimate=cost(2 * rows * D * 4 * width, 16 * 2**20, 4 * rows * width),
+    )(*acts, gating, upward, *weights)
+
+
+def normed_two_kernel(kind, gate_ref, up_ref, *refs):
+    gates, refs = refs[:8], refs[8:]
+    ups, refs = refs[:8], refs[8:]
+    outs, total_s = refs[:-1], refs[-1]
+    step, last = pl.program_id(0), pl.num_programs(0) - 1
+    for y in range(2):
+        value = dot(gate_ref[0], gates[y][...], 1, 1)
+        for b in range(4):
+            if b > 0:
+                value += dot(gate_ref[b], gates[2 * b + y][...], 1, 1)
+            value += dot(up_ref[b], ups[2 * b + y][...], 1, 1)
+
+        @pl.when(step == 0)
+        def _():
+            total_s[:, y_half(y)] = value
+
+        @pl.when(step == last)
+        def _():
+            whole = total_s[:, y_half(y)] + value
+            for index in range(len(SUM_BLOCKS[kind])):
+                rows = slice(index * PIECE, (index + 1) * PIECE)
+                store_sum(kind, index, y, whole[rows], outs)
+
+
+def run_normed_two(kind, gate_low, up_low, gates, ups):
+    rows, width = gate_low.shape[1], gate_low.shape[2]
+    shapes = SUM_SHAPES[kind]
+    low = pl.BlockSpec((4, rows, width // 2), lambda j: (0, 0, j))
+    piece = pl.BlockSpec((HALF, width // 2), lambda j: (0, j))
+    return pl.pallas_call(
+        lambda *refs: normed_two_kernel(kind, *refs),
+        grid=(2,),
+        out_shape=shapes,
+        in_specs=[low] * 2 + [piece] * 16,
+        out_specs=[pl.BlockSpec(s.shape, lambda j: (0, 0)) for s in shapes],
+        scratch_shapes=[pltpu.VMEM((rows, D), F32)],
+        compiler_params=params(48),
+        cost_estimate=cost(2 * rows * D * 8 * width, 18 * 2**20),
+    )(gate_low, up_low, *gates, *ups)
+
+
+def wide_grad_kernel(*refs):
+    acts, refs = refs[:5], refs[5:]
+    lows, refs = refs[:3], refs[3:]
+    outs, turned_s = refs[:2], refs[2]
+
+    @pl.when(pl.program_id(1) == 0)
+    def _():
+        start = 0
+        for act_ref in acts:
+            size = act_ref.shape[0]
+            turned_s[:, start : start + size] = act_ref[...].T
+            start += size
+
+    for d in range(2):
+        total, start = None, 0
+        for low_ref in lows:
+            size = low_ref.shape[1]
+            value = dot(turned_s[:, start : start + size], low_ref[d], 1, 0)
+            total = value if total is None else total + value
+            start += size
+        outs[d][0, 0] = total.astype(BF)
+
+
+def run_wide_grad(acts, lows):
+    width = lows[0].shape[2]
+    return pl.pallas_call(
+        wide_grad_kernel,
+        grid=(2, 2),
+        out_shape=[shape((2, 2, HALF, width), BF)] * 2,
+        in_specs=[pl.BlockSpec((act.shape[0], HALF), lambda y, h: (0, y)) for act in acts]
+        + [pl.BlockSpec((2, low.shape[1], width), lambda y, h: (h, 0, 0)) for low in lows],
+        out_specs=[pl.BlockSpec((1, 1, HALF, width), lambda y, h: (y, h, 0, 0))] * 2,
+        scratch_shapes=[pltpu.VMEM((HALF, 4 * PIECE), BF)],
+        compiler_params=params(36),
+        cost_estimate=cost(2 * 4 * PIECE * D * 4 * width, 16 * 2**20),
+    )(*acts, *lows)
+
+
+def down_grad_kernel(*refs):
+    units, refs = refs[:3], refs[3:]
+    acts, refs = refs[:5], refs[5:]
+    outs, turned_s = refs[:2], refs[2]
+
+    @pl.when(pl.program_id(1) == 0)
+    def _():
+        start = 0
+        for unit_ref in units:
+            size = unit_ref.shape[1]
+            for d in range(2):
+                turned_s[d, :, start : start + size] = unit_ref[d].T
+            start += size
+
+    for d in range(2):
+        total, start = None, 0
+        for act_ref in acts:
+            size = act_ref.shape[0]
+            value = dot(turned_s[d, :, start : start + size], act_ref[...], 1, 0)
+            total = value if total is None else total + value
+            start += size
+        outs[d][0, 0] = total.astype(BF)
+
+
+def run_down_grad(units, acts):
+    width = units[0].shape[2]
+    return pl.pallas_call(
+        down_grad_kernel,
+        grid=(2, 2),
+        out_shape=[shape((2, 2, width, HALF), BF)] * 2,
+        in_specs=[pl.BlockSpec((2, unit.shape[1], width), lambda h, y: (h, 0, 0)) for unit in units]
+        + [pl.BlockSpec((act.shape[0], HALF), lambda h, y: (0, y)) for act in acts],
+        out_specs=[pl.BlockSpec((1, 1, width, HALF), lambda h, y: (y, h, 0, 0))] * 2,
+        scratch_shapes=[pltpu.VMEM((2, width, 4 * PIECE), BF)],
+        compiler_params=params(36),
+        cost_estimate=cost(2 * 4 * PIECE * D * 4 * width, 16 * 2**20),
+    )(*units, *acts)
+
+
+def head_grad_kernel(kinds, *refs):
+    acts, refs = refs[:5], refs[5:]
+    messages, refs = refs[:4], refs[4:]
+    outs, turned_s, right_s = refs[:2], refs[2], refs[3]
+    start = 0
+    for act_ref in acts:
+        size = act_ref.shape[0]
+        turned_s[:, start : start + size] = act_ref[...].T
+        start += size
+
+    @pl.when(pl.program_id(0) == 0)
+    def _():
+        for which in range(kinds):
+            for b in range(4):
+                for a in range(4):
+                    value = messages[b][which, a] if kinds > 1 else messages[b][a]
+                    right_s[columns(a, PIECE), columns(which * 4 + b, HD)] = value
+
+    for which in range(kinds):
+        value = dot(turned_s[...], right_s[:, columns(which, 4 * HD)], 1, 0)
+        for b, (d, h) in enumerate(SLOTS):
+            outs[d][0, h, which] = value[:, columns(b, HD)].astype(BF)
+
+
+def run_head_grad(kinds, acts, messages):
+    whole = lambda dims: pl.BlockSpec(dims, lambda y: (0,) * len(dims))
+    return pl.pallas_call(
+        lambda *refs: head_grad_kernel(kinds, *refs),
+        grid=(2,),
+        out_shape=[shape((2, 2, kinds, HALF, HD), BF)] * 2,
+        in_specs=[pl.BlockSpec((act.shape[0], HALF), lambda y: (0, y)) for act in acts]
+        + [whole(message.shape) for message in messages],
+        out_specs=[pl.BlockSpec((1, 2, kinds, HALF, HD), lambda y: (y, 0, 0, 0, 0))] * 2,
+        scratch_shapes=[
+            pltpu.VMEM((HALF, 4 * PIECE), BF),
+            pltpu.VMEM((4 * PIECE, kinds * 4 * HD), BF),
+        ],
+        compiler_params=params(40),
+        cost_estimate=cost(2 * 4 * PIECE * D * kinds * 4 * HD, 12 * 2**20),
+    )(*acts, *messages)
 
 
 def allowed_pairs(starts, query0, key0, shape, query_axis):
@@ -628,10 +1066,6 @@
                 turned = value * cos_ref[rows, :] - pltpu.roll(value, HD // 2, 1) * sin_ref[rows, :]
                 outs[b][which, a] = turned.astype(BF)
             outs[b][2, a] = dv_s[rows, :].astype(BF)
-
-
-SMEM_SPEC = pl.BlockSpec(memory_space=pltpu.SMEM)
-VMEM_SPEC = pl.BlockSpec(memory_space=pltpu.VMEM)
 
 
 def run_forward(place, starts, messages):
@@ -709,153 +1143,215 @@
 ):
     row, col, dp = lax.axis_index("row"), lax.axis_index("col"), lax.axis_index("dp")
     x, y = row % 2, row // 2
-    place = (x, y, dp)
+    q = (dp + y) % 2
     own_piece = col * SIDE + row
     segment = segment_ids[0]
     group_tokens = segment.shape[0]
     home_tokens = group_tokens // (SIDE * SIDE)
-    unit_width = gate_weight.shape[1]
-
-    hidden = to_tokens(hidden_in).astype(F32)
-    normed, inverse_one = local_norm(hidden)
-    normed_blocks = square_gather(normed.astype(BF))
-
-    lead = (dp + y) % 2
-    attn_weights = gather_weights(
-        jnp.stack((query_weight, key_weight, value_weight, output_weight.T)), place, lead
-    )
-    qkv_weight = jnp.concatenate((attn_weights[0], attn_weights[1], attn_weights[2]), axis=1)
-    out_weight = attn_weights[3]
-    mlp_weights = gather_weights(jnp.stack((gate_weight, up_weight)), place, 0)
-    gate_full, up_full = mlp_weights[0], mlp_weights[1]
-    down_full = gather_weights(down_weight.T[None], place, 0)[0]
+
+    def swap_y(values):
+        return jnp.where(
+            y == 0, values, jnp.concatenate((values[:, HALF:], values[:, :HALF]), axis=1)
+        )
+
+    def cut(matrix, at, axis):
+        size = matrix.shape[axis] // 4
+        return lax.dynamic_slice_in_dim(matrix, (2 * at + q) * size, size, axis)
+
+    def head_cut(at):
+        parts = [cut(matrix, at, 1) for matrix in (query_weight, key_weight, value_weight)]
+        return jnp.stack(parts + [cut(output_weight, at, 0).T])
 
     labels = jnp.arange(1, CONT + 1, dtype=jnp.int32)
     starts = jnp.sum((segment[None, :] < labels[:, None]).astype(jnp.int32), axis=1)
     codes = jnp.arange(16, dtype=jnp.int32)
     relative = (
-        (codes & 1) + ((codes >> 2) & 1) * 2 + ((codes >> 1) & 1) * 4 + ((codes >> 3) & 1) * 8
+        (codes & 1) + ((codes >> 1) & 1) * 4 + ((codes >> 2) & 1) * 2 + ((codes >> 3) & 1) * 8
     )
     pieces = relative ^ own_piece
-    cosine, sine_table = rotary(positions(segment))
-    cos_wide = jnp.concatenate((cosine, cosine), axis=1)
-    sin_wide = jnp.concatenate((-sine_table, sine_table), axis=1)
-
-    def turn(values, cos_block, sin_block):
-        heads = values.reshape(home_tokens, 4, HD)
-        swapped = jnp.concatenate((heads[..., HD // 2 :], heads[..., : HD // 2]), axis=-1)
-        return heads * cos_block[:, None] + swapped * sin_block[:, None]
-
-    query_blocks, key_blocks, value_blocks = [], [], []
-    for a in range(4):
-        projected = dot(normed_blocks[a], qkv_weight, 1, 0)
-        cos_block = lax.dynamic_slice_in_dim(cos_wide, pieces[a] * home_tokens, home_tokens, 0)
-        sin_block = lax.dynamic_slice_in_dim(sin_wide, pieces[a] * home_tokens, home_tokens, 0)
-        width = 4 * HD
-        query_blocks.append(turn(projected[:, :width], cos_block, sin_block).astype(BF))
-        key_blocks.append(turn(projected[:, width : 2 * width], cos_block, sin_block).astype(BF))
-        value_blocks.append(projected[:, 2 * width :].reshape(home_tokens, 4, HD).astype(BF))
-    messages = [
-        jnp.stack(
-            [
-                jnp.stack([blocks[a][:, slot] for a in range(4)])
-                for blocks in (query_blocks, key_blocks, value_blocks)
-            ]
-        )
-        for slot in range(4)
-    ]
+    frequency = jnp.power(10000.0, jnp.arange(HD // 2, dtype=F32) * (-2.0 / HD))
+    angles = positions(segment).astype(F32)[:, None] * jnp.tile(frequency, 2)[None, :]
+    sign = jnp.where(jnp.arange(HD) < HD // 2, -1.0, 1.0)
+    cos_wide, sin_wide = jnp.cos(angles), jnp.sin(angles) * sign[None, :]
+
+    heads_x = after(flip_x(head_cut(1 - x)), cos_wide, sin_wide)
+    gates_x = flip_x(after(cut(gate_weight, 1 - x, 1), heads_x))
+    hidden = swap_y(to_tokens(after(hidden_in, heads_x))).astype(F32)
+    all_heads = ordered(x, head_cut(x), heads_x, 1)
+    heads_tall, outs_tall = all_heads[:3], all_heads[3]
+    heads_high = flip_zh(heads_tall)
+    heads_y = flip_dp_y(heads_tall)
+    hidden = after(hidden, gates_x)
+    gates_tall = ordered(x, cut(gate_weight, x, 1), gates_x, 0)
+    row_half = gates_tall.shape[0] // 2
+    normed, inverse_one = local_norm(hidden)
+    normed_acts = square_gather(normed.astype(BF), heads_high)
+    gates_first = flip_zh(after(gates_tall[:row_half], heads_high))
+    heads_y_high = flip_dp_y(heads_high)
+    gates_second = flip_zh(after(gates_tall[row_half:], gates_first))
+    heads_other = other_core(
+        (heads_tall, heads_y, heads_high, after(heads_y_high, gates_first))
+    )
+    heads = piece_list(heads_tall, heads_high, heads_y, heads_y_high, heads_other)
+
+    heads, normed_acts = after((heads, normed_acts), gates_second)
+    gates_high = jnp.concatenate((gates_first, gates_second), axis=0)
+    messages = run_qkv(pieces, normed_acts, heads, cos_wide, sin_wide)
+    ups_x = flip_x(after(cut(up_weight, 1 - x, 1), messages[0]))
+    downs_x = flip_x(after(cut(down_weight, 1 - x, 0), messages[0]))
+    outs_high = flip_zh(after(outs_tall, messages[0]))
+    outs_y = flip_dp_y(after(outs_tall, messages[0]))
+    gates_y = flip_dp_y(after(gates_tall, outs_y))
     messages = swap_slots(messages)
-    *mixed, wide, log_total = run_forward(pieces, starts, messages)
+    messages = after(messages, ups_x, downs_x, outs_high, outs_y, gates_y)
+
+    ups_tall = ordered(x, cut(up_weight, x, 1), after(ups_x, messages), 0)
+    ups_high = flip_zh(ups_tall)
+    outs_y_high = flip_dp_y(after(outs_high, messages))
+    gates_y_high = flip_dp_y(after(gates_high, messages))
+    *mixed, wide_mixed, log_total = run_forward(pieces, starts, messages)
+    mixed = after(mixed, ups_high, outs_y_high, gates_y_high)
+    outs_other = other_core(after((outs_tall, outs_y, outs_high, outs_y_high), mixed))
+    outs = piece_list(outs_tall, outs_high, outs_y, outs_y_high, outs_other)
     mixed = swap_slots(mixed)
-    attended = [jnp.concatenate([mixed[b][a] for b in range(4)], axis=1) for a in range(4)]
-    after_attention = hidden + square_reduce(lambda a: dot(attended[a], out_weight, 1, 1))
+
+    downs_tall = ordered(x, cut(down_weight, x, 0), after(downs_x, mixed), 1)
+    middle_row = downs_tall.shape[0] // 2
+    downs_first = flip_zh(downs_tall[:middle_row])
+    downs_second = flip_zh(after(downs_tall[middle_row:], downs_first))
+    ups_y = flip_dp_y(after(ups_tall, mixed))
+    ups_y_high = flip_dp_y(after(ups_high, ups_y))
+    gates_other = other_core(after((gates_tall, gates_y, gates_high, gates_y_high), mixed))
+    gates = piece_list(gates_tall, gates_high, gates_y, gates_y_high, gates_other)
+    sums = run_out(mixed, outs)
+    after_attention = hidden + square_reduce(*sums, downs_first, ups_y)
+    after_attention = after(after_attention, downs_second, ups_y_high, gates_other)
 
     normed_two, inverse_two = local_norm(after_attention)
-    normed_two_blocks = square_gather(normed_two.astype(BF))
-    gating = [dot(normed_two_blocks[a], gate_full, 1, 0) for a in range(4)]
-    upward = [dot(normed_two_blocks[a], up_full, 1, 0) for a in range(4)]
-    units = [(gating[a] * jax.nn.sigmoid(gating[a]) * upward[a]).astype(BF) for a in range(4)]
-    output = after_attention + square_reduce(lambda a: dot(units[a], down_full, 1, 1))
-
-    counted = valid.astype(F32)
-    total_count = jnp.maximum(sum_all(jnp.sum(counted).reshape(1), False), 1.0)
-    counted_home = lax.dynamic_slice_in_dim(counted, row * home_tokens, home_tokens, 0)[:, None]
-    differ = output - to_tokens(teacher).astype(F32)
+    ups_other = other_core(after((ups_tall, ups_y, ups_high, ups_y_high), normed_two))
+    ups = piece_list(ups_tall, ups_high, ups_y, ups_y_high, ups_other)
+    downs_high = jnp.concatenate((downs_first, downs_second), axis=0)
+    low_two = normed_two.astype(BF)
+    downs_y = flip_dp_y(after(downs_tall, normed_two))
+    up_own = run_up([low_two], gates, ups)
+    two_acts = square_gather(low_two, up_own)
+    downs_y_high = flip_dp_y(after(downs_high, downs_y))
+    count = jnp.sum(valid.astype(F32)).reshape(1)
+    count = count + flip_dp(after(count, low_two))
+    up_sides = run_up(after(two_acts[1:3], up_own[2], downs_y, count), gates, ups)
+    downs_other = other_core(
+        after((downs_tall, downs_y, downs_high, downs_y_high), up_own[2])
+    )
+    count = count + flip_zh(after(count, two_acts[1:3]))
+    up_far = run_up(after(two_acts[3:], up_sides[2], downs_y_high, count), gates, ups)
+    count = count + flip_zl(after(count, two_acts))
+    downs = piece_list(downs_tall, downs_high, downs_y, downs_y_high, downs_other)
+    ups_out = [up_own, up_sides, up_far]
+    units = [out[2] for out in ups_out]
+    down_far = run_down("far", after(units[2], count), downs)
+    down_sides = run_down("sides", after(units[1], down_far), downs)
+    down_own = run_down("own", after(units[0], down_sides), downs)
+    output = after_attention + square_reduce(down_far, down_sides, down_own[0])
+
+    total_count = jnp.maximum(count, 1.0)
+    counted_home = lax.dynamic_slice_in_dim(
+        valid.astype(F32), row * home_tokens, home_tokens, 0
+    )[:, None]
+    target = swap_y(to_tokens(after(teacher, mixed)))
+    differ = output - target.astype(F32)
     local_loss = jnp.sum(counted_home * (differ * differ)) / D
-    mean_loss = sum_all(local_loss.reshape(1), True) / total_count
     all_tokens = group_tokens * lax.axis_size("dp")
     out_grad = counted_home * differ * (all_tokens / total_count)
 
-    out_blocks = square_gather(out_grad.astype(BF))
-    gate_low, up_low = [], []
-    for a in range(4):
-        units_grad = dot(out_blocks[a], down_full, 1, 0)
-        sigmoid = jax.nn.sigmoid(gating[a])
-        gate_low.append(
-            (units_grad * upward[a] * sigmoid * (1.0 + gating[a] * (1.0 - sigmoid))).astype(BF)
-        )
-        up_low.append((units_grad * (gating[a] * sigmoid)).astype(BF))
-    normed_two_grad = square_reduce(
-        lambda a: dot(gate_low[a], gate_full, 1, 1) + dot(up_low[a], up_full, 1, 1)
-    )
+    low_out = out_grad.astype(BF)
+    loss = local_loss.reshape(1)
+    loss = loss + flip_dp(after(loss, low_out))
+    low_own = run_gated([low_out], up_own[0], up_own[1], downs)
+    out_acts = square_gather(low_out, low_own)
+    low_sides = run_gated(after(out_acts[1:3], low_own, loss), up_sides[0], up_sides[1], downs)
+    loss = loss + flip_y(after(loss, out_acts[1:3]))
+    low_far = run_gated(after(out_acts[3:], low_sides, loss), up_far[0], up_far[1], downs)
+    loss = loss + flip_zl(after(loss, low_sides))
+    lows = [low_own, low_sides, low_far]
+    two_far = run_normed_two("far", *after(low_far, loss), gates, ups)
+    loss = loss + flip_x(after(loss, low_far))
+    two_sides = run_normed_two("sides", *after(low_sides, two_far, loss), gates, ups)
+    loss = loss + flip_zh(after(loss, two_far))
+
+    down_grads = Spread(run_down_grad(after(units, two_sides), after(out_acts, loss)))
+    down_core = down_grads.to_core()
+    two_own = run_normed_two("own", *after(low_own, down_grads.keep), gates, ups)
+    gate_pair = run_wide_grad(two_acts, after([low[0] for low in lows], two_own, down_core))
+    gate_grads = Spread(gate_pair)
+    down_y1 = down_grads.to_y(1)
+    normed_two_grad = square_reduce(two_far, two_sides, two_own[0])
+    normed_two_grad = after(normed_two_grad, down_y1, gate_pair)
     middle_grad = out_grad + local_norm_backward(normed_two_grad, normed_two, inverse_two)
-
-    join = lambda blocks: jnp.concatenate(blocks, axis=0)
-    out_wide = join(out_blocks)
-    down_grad = scatter_grads(dot(out_wide, join(units), 0, 0)[None], place, 0)
-    normed_two_wide = join(normed_two_blocks)
-    mlp_grads = scatter_grads(
-        jnp.stack(
-            (dot(normed_two_wide, join(gate_low), 0, 0), dot(normed_two_wide, join(up_low), 0, 0))
-        ),
-        place,
-        0,
-    )
-
-    middle_blocks = square_gather(middle_grad.astype(BF))
-    attended_grad = [dot(middle_blocks[a], out_weight, 1, 0).astype(BF) for a in range(4)]
-    grad_messages = [
-        jnp.stack([attended_grad[a][:, slot * HD : (slot + 1) * HD] for a in range(4)])
-        for slot in range(4)
-    ]
+    low_middle = middle_grad.astype(BF)
+    gate_core = gate_grads.to_core(low_middle)
+    down_y0 = down_grads.to_y(0, low_middle)
+    up_pair = run_wide_grad(two_acts, after([low[1] for low in lows], gate_pair))
+    up_grads = Spread(up_pair)
+    middle_acts = square_gather(low_middle, down_y0, gate_core)
+    down_grads.to_high(down_y0)
+    gate_y1 = gate_grads.to_y(1, down_y0)
+    middle_acts = after(middle_acts, up_pair, gate_y1)
+    grad_messages = run_attended_grad(middle_acts, outs)
+    grad_messages = after(grad_messages, down_grads.high)
+    up_core = up_grads.to_core(grad_messages)
+    gate_y0 = gate_grads.to_y(0, grad_messages)
+    out_grads = Spread(run_head_grad(1, after(middle_acts, grad_messages), mixed))
     grad_messages = swap_slots(grad_messages)
+    grad_messages = after(grad_messages, up_core, out_grads.keep, gate_y0)
+    gate_grads.to_high(grad_messages)
+    up_y1 = up_grads.to_y(1, grad_messages)
+    up_y0 = up_grads.to_y(0, grad_messages)
     back = run_backward(
-        pieces, starts, messages, grad_messages, wide, log_total, cos_wide, sin_wide
-    )
+        pieces, starts, messages, grad_messages, wide_mixed, log_total, cos_wide, sin_wide
+    )
+    back = after(back, gate_grads.high, up_y1, up_y0)
+    layer_output = to_width(swap_y(after(output, back).astype(BF)))
+    gate_grads.to_x(x, 0, back)
+    down_grads.to_x(x, 1, back)
+    out_core = out_grads.to_core(back)
+    out_y1 = out_grads.to_y(1, back)
+    out_y0 = out_grads.to_y(0, back)
     back = swap_slots(back)
-    projected_low = [
-        jnp.concatenate([back[b][which, a] for which in range(3) for b in range(4)], axis=1)
-        for a in range(4)
-    ]
-    normed_grad = square_reduce(lambda a: dot(projected_low[a], qkv_weight, 1, 1))
+    back = after(back, out_y1, out_y0, gate_grads.parts, down_grads.parts, layer_output)
+    up_grads.to_high(back)
+    head_pair = run_head_grad(3, normed_acts, back)
+    head_grads = Spread(head_pair)
+    head_core = head_grads.to_core()
+    input_sums = run_input(after(back, head_pair), heads)
+    input_sums = after(input_sums, head_core)
+    head_y1 = head_grads.to_y(1)
+    normed_grad = square_reduce(*input_sums, head_y1)
+    head_y0 = head_grads.to_y(0, head_y1)
+    out_grads.to_high(up_grads.high)
+    head_grads.to_high(head_y1)
+    normed_grad = after(normed_grad, head_y0, up_grads.high)
+    up_grads.to_x(x, 0, normed_grad)
+    out_grads.to_x(x, 1, normed_grad)
     input_gradient = middle_grad + local_norm_backward(normed_grad, normed, inverse_one)
-
-    width = 4 * HD
-    qkv_grad = dot(join(normed_blocks), join(projected_low), 0, 0)
-    out_weight_grad = dot(join(middle_blocks), join(attended), 0, 0)
-    attn_grads = scatter_grads(
-        jnp.stack(
-            (
-                qkv_grad[:, :width],
-                qkv_grad[:, width : 2 * width],
-                qkv_grad[:, 2 * width :],
-                out_weight_grad,
-            )
-        ),
-        place,
-        lead,
-    )
+    head_grads.to_x(x, 1, normed_grad)
+    mean_loss = loss / total_count
+
+    down_grad = unite(*down_grads.parts, x, q, 0)
+    gate_grad = unite(*gate_grads.parts, x, q, 1)
+    up_grad = unite(*up_grads.parts, x, q, 1)
+    out_weight_grad = unite(*out_grads.parts, x, q, 2)
+    head_grads = unite(*head_grads.parts, x, q, 2)
     return (
-        to_width(output.astype(BF)),
+        layer_output,
         mean_loss,
-        to_width(input_gradient),
-        attn_grads[0],
-        attn_grads[1],
-        attn_grads[2],
-        attn_grads[3].T,
-        mlp_grads[0],
-        mlp_grads[1],
-        down_grad[0].T,
+        to_width(swap_y(input_gradient)),
+        head_grads[0],
+        head_grads[1],
+        head_grads[2],
+        out_weight_grad[0].T,
+        gate_grad,
+        up_grad,
+        down_grad,
     )
 
 

time: 1620 us -> 1170 us (0.72)
  local copies, waits for them, and re-layouts: 313 us -> 96.1 us
  matrix products: 203 us -> 0 us
  Pallas kernels: 70.3 us -> 257 us
  other arithmetic: 220 us -> 81.8 us
  waiting for transfers between devices: 610 us -> 575 us
  starting transfers between devices: 171 us -> 142 us
    dot_general x45 -> x0, matrix products: 203 us -> none  [dot(): lax.dot_general(left, right, (((a,), (b,)), ((), ())), preferred_element_...]
    pallas_call x0 -> x21, Pallas kernels: none -> 186 us  [the longest x3 33.8 us: run_normed_two(): pl.pallas_call(lambda *refs: normed_two_kernel(kind, *refs), grid=(2,), o...]
    ppermute x80 -> x75, waiting for transfers between devices: 567 us -> 427 us  [flip(): return lax.ppermute(values, axis, [(i, i ^ bit) for i in range(SIDE)])]
    slice x62 -> x15, local copies, waits for them, and re-layouts: 94.6 us -> 5.08 us  [the longest x8 3.55 us: square_gather(): return [block, by_x, by_z, flip_zl(next_x[:half]), flip_x(next_z[half:])]]
    ppermute x0 -> x20, waiting for transfers between devices: none -> 82.2 us  [flip_dp_y(): return lax.ppermute(values, ('dp', 'row'), pairs)]
    select_n x20 -> x4, other arithmetic: 62.4 us -> 3.08 us  [ordered(): jnp.where(flag == 0, jnp.concatenate((own, other), axis=axis), jnp.concat...]
    ppermute x80 -> x75, starting transfers between devices: 142 us -> 92.2 us  [flip(): return lax.ppermute(values, axis, [(i, i ^ bit) for i in range(SIDE)])]
    another operation x21 -> x3, local copies, waits for them, and re-layouts: 43.9 us -> 2.15 us  [the longest x2 2.15 us: head_cut(): return jnp.stack(parts + [cut(output_weight, at, 0).T])]
  transfers between devices with their start and end apart: 99 -> 140, of which waited for: 48 -> 58; matrix products, arithmetic and copies ran while one was open for 37% -> 8% of each run, Pallas kernels for 4% -> 18%
where the time goes in v2:
time: 1170 us; the launch traced here: 1160 us
  waiting for transfers between devices  575 us (49%)
  Pallas kernels  257 us (22%)
  starting transfers between devices  142 us (12%)
  local copies, waits for them, and re-layouts  96.1 us (8%)
  other arithmetic  81.8 us (7%)
    ppermute x75, waiting for transfers between devices, flip(): return lax.ppermute(values, axis, [(i, i ^ bit) for i in range(SIDE)])  427 us
    ppermute x75, starting transfers between devices, flip(): return lax.ppermute(values, axis, [(i, i ^ bit) for i in range(SIDE)])  92.2 us
    ppermute x20, waiting for transfers between devices, flip_dp_y(): return lax.ppermute(values, ('dp', 'row'), pairs)  82.2 us
    unnamed x391, local copies, waits for them, and re-layouts  72.7 us
    pallas_call x1, Pallas kernels, run_backward(): pl.pallas_call(attention_backward, out_shape=[jax.ShapeDtypeStruct((3, 4,...  40.2 us
    ppermute x4, waiting for transfers between devices, flip_y_zh(): return lax.ppermute(values, ('row', 'col'), pairs)  39.7 us
    pallas_call x3, Pallas kernels, run_normed_two(): pl.pallas_call(lambda *refs: normed_two_kernel(kind, *refs), grid=(2,), o...  33.8 us
    pallas_call x3, Pallas kernels, run_up(): pl.pallas_call(lambda *refs: up_kernel(len(acts), *refs), grid=(width //...  33.6 us
  transfers between devices with their start and end apart: 140, of which 58 were waited for; matrix products, arithmetic and copies ran while one was open for 8% of the time, Pallas kernels for 18%

profile of v2, /device:TPU:0, one launch (start us, length us, event | category | flops | bytes accessed | tf_op | source)
XLA Modules:
  0.0 1163.2 jit_solution(1348616823006246557)
XLA Ops:
  38.4 19.7 %collective-permute-done.5.refs_9_.refs_8_ = bf16[3,1024,128]{2,1,0:T(8,128)(2,1)} collective-permute-done((bf16[3,1024,128]{2,1,0:T(8,128)(2,1)S(1)}, bf16[3,1024,128]{2,1,0:T(8,128)(2,1)}, u32[]{:S(2)}, u32[]{:S(2)}) %collective-permute-start.5) | collective-permute-done | bytes 786464 | tf_op jit(solution)/shard_map/ppermute | solution.py:353
  67.0 16.4 %collective-permute-done.8 = bf16[512,512]{1,0:T(8,128)(2,1)} collective-permute-done((bf16[512,512]{1,0:T(8,128)(2,1)}, bf16[512,512]{1,0:T(8,128)(2,1)}, u32[]{:S(2)}, u32[]{:S(2)}) %collective-permute-start.8) | collective-permute-done | bytes 524320 | tf_op jit(solution)/shard_map/ppermute | solution.py:353
  107.4 15.2 %collective-permute-done.14 = bf16[512,512]{1,0:T(8,128)(2,1)} collective-permute-done((bf16[512,512]{1,0:T(8,128)(2,1)}, bf16[512,512]{1,0:T(8,128)(2,1)}, u32[]{:S(2)}, u32[]{:S(2)}) %collective-permute-start.14) | collective-permute-done | bytes 524320 | tf_op jit(solution)/shard_map/ppermute | solution.py:353
  152.3 22.2 %collective-permute-done.20.refs_8_.refs_9_ = bf16[1024,128]{1,0:T(8,128)(2,1)S(1)} collective-permute-done((bf16[1024,128]{1,0:T(8,128)(2,1)S(1)}, bf16[1024,128]{1,0:T(8,128)(2,1)S(1)}, u32[]{:S(2)}, u32[]{:S(2)}) %collective-permute-start.20) | collective-permute-done | bytes 262176 | tf_op jit(solution)/shard_map/ppermute | solution.py:353
  192.5 15.7 %collective-permute-done.16.refs_2_ = bf16[3,4,256,128]{3,2,1,0:T(8,128)(2,1)S(1)} collective-permute-done((bf16[3,4,256,128]{3,2,1,0:T(8,128)(2,1)S(1)}, bf16[3,4,256,128]{3,2,1,0:T(8,128)(2,1)S(1)}, u32[]{:S(2)}, u32[]{:S(2)}) %collective-permute-start.16) | collective-permute-done | bytes 786464 | tf_op jit(solution)/shard_map/ppermute | solution.py:353
  208.2 17.4 %collective-permute-done.17.refs_3_ = bf16[3,4,256,128]{3,2,1,0:T(8,128)(2,1)S(1)} collective-permute-done((bf16[3,4,256,128]{3,2,1,0:T(8,128)(2,1)S(1)}, bf16[3,4,256,128]{3,2,1,0:T(8,128)(2,1)S(1)}, u32[]{:S(2)}, u32[]{:S(2)}) %collective-permute-start.17) | collective-permute-done | bytes 786464 | tf_op jit(solution)/shard_map/ppermute | solution.py:376
  228.3 30.3 %shard_map.187 = (bf16[4,256,128]{2,1,0:T(8,128)(2,1)S(1)}, bf16[4,256,128]{2,1,0:T(8,128)(2,1)S(1)}, bf16[4,256,128]{2,1,0:T(8,128)(2,1)S(1)}, bf16[4,256,128]{...) custom-call(s32[16]{0:T(128)S(1)} %fusion.40.place_ref, s32[8]{0:T(128)S(1)} %convert_reduce_fusion.1.starts_ref, ...), custom_call_target="tpu_custom_call" | custom-call | flops 8589934592 | bytes 8388608 | tf_op jit(solution)/shard_map/pallas_call | solution.py:1079
  258.7 16.2 %collective-permute-done.23.refs_13_.refs_14_ = bf16[1024,512]{1,0:T(8,128)(2,1)S(1)} collective-permute-done((bf16[1024,512]{1,0:T(8,128)(2,1)S(1)}, bf16[1024,512]{1,0:T(8,128)(2,1)S(1)}, u32[]{:S(2)}, u32[]{:S(2)}) %collective-permute-start.23) | collective-permute-done | bytes 1048608 | tf_op jit(solution)/shard_map/ppermute | solution.py:353
  308.9 19.3 %collective-permute-done.35 = bf16[256,1024]{1,0:T(8,128)(2,1)S(1)} collective-permute-done((bf16[256,1024]{1,0:T(8,128)(2,1)S(1)}, bf16[256,1024]{1,0:T(8,128)(2,1)S(1)}, u32[]{:S(2)}, u32[]{:S(2)}) %collective-permute-start.35) | collective-permute-done | bytes 524320 | tf_op jit(solution)/shard_map/ppermute | solution.py:353
  368.0 21.7 %collective-permute-done.42.refs_14_.refs_15_ = bf16[1024,512]{1,0:T(8,128)(2,1)S(1)} collective-permute-done((bf16[1024,512]{1,0:T(8,128)(2,1)S(1)}, bf16[1024,512]{1,0:T(8,128)(2,1)S(1)}, u32[]{:S(2)}, u32[]{:S(2)}) %collective-permute-start.42) | collective-permute-done | bytes 1048608 | tf_op jit(solution)/shard_map/ppermute | solution.py:385
  394.0 22.7 %collective-permute-done.53.refs_2_.refs_4_.refs_5_ = bf16[512,1024]{1,0:T(8,128)(2,1)S(1)} collective-permute-done((bf16[512,1024]{1,0:T(8,128)(2,1)S(1)}, bf16[512,1024]{1,0:T(8,128)(2,1)S(1)}, u32[]{:S(2)}, u32[]{:S(2)}) %collective-permute-start.53) | collective-permute-done | bytes 1048608 | tf_op jit(solution)/shard_map/ppermute | solution.py:385
  456.5 15.1 %shard_map.190 = (f32[4,512,512]{2,1,0:T(8,128)}, f32[4,512,512]{2,1,0:T(8,128)}, bf16[4,512,512]{2,1,0:T(8,128)(2,1)}) custom-call(bf16[256,2048]{1,0:T(8,128)(2,1)S(1)} %collective-permute-done.51.refs_0_.refs_1_, bf16[256,2048]{1,0:T(8,128)(2,1)S(1)} %collective-permute-done.52.refs_1_.refs_2_, ...), custom_call_target="tpu_custom_call" | custom-call | flops 8589934592 | bytes 16777216 | tf_op jit(solution)/shard_map/pallas_call | solution.py:691
  552.8 14.0 %collective-permute-done.70.refs_0_.refs_4_ = bf16[256,2048]{1,0:T(8,128)(2,1)S(1)} collective-permute-done((bf16[256,2048]{1,0:T(8,128)(2,1)S(1)}, bf16[256,2048]{1,0:T(8,128)(2,1)S(1)}, u32[]{:S(2)}, u32[]{:S(2)}) %collective-permute-start.70) | collective-permute-done | bytes 1048608 | tf_op jit(solution)/shard_map/ppermute | solution.py:353
  626.3 15.2 %shard_map.199 = (f32[128,2048]{1,0:T(8,128)S(1)}, bf16[128,2048]{1,0:T(8,128)(2,1)}, bf16[128,2048]{1,0:T(8,128)(2,1)}, f32[128,2048]{1,0:T(8,128)S(1)}) custom-call(bf16[4,512,512]{2,1,0:T(8,128)(2,1)} %get-tuple-element.395.refs_0_.refs_6_, bf16[4,512,512]{2,1,0:T(8,128)(2,1)} %get-tuple-element.405.refs_1_.refs_6_, ...), custom_call_target="tpu_custom_call" | custom-call | flops 8589934592 | bytes 18874368 | tf_op jit(solution)/shard_map/pallas_call | solution.py:788
  646.6 15.4 %shard_map.200 = (bf16[2,2,512,1024]{3,2,1,0:T(8,128)(2,1)S(1)}, bf16[2,2,512,1024]{3,2,1,0:T(8,128)(2,1)}) custom-call(bf16[4,256,512]{2,1,0:T(8,128)(2,1)S(1)} %copy-done.62, bf16[4,512,512]{2,1,0:T(8,128)(2,1)S(1)} %copy-done.136, bf16[4,256,512]{2,1,0:T(8,128)(2,1)S(1)} %copy-done.45, bf16[256,2048]{1,0:T(8,128)(2,1)S(1)} %copy-done.35, ...), custom_call_target="tpu_custom_call" | custom-call | flops 8589934592 | bytes 16777216 | tf_op jit(solution)/shard_map/pallas_call | solution.py:864
  744.4 15.6 %collective-permute-done.89 = bf16[512,1024]{1,0:T(8,128)(2,1)S(1)} collective-permute-done((bf16[512,1024]{1,0:T(8,128)(2,1)}, bf16[512,1024]{1,0:T(8,128)(2,1)S(1)}, u32[]{:S(2)}, u32[]{:S(2)}) %collective-permute-start.89) | collective-permute-done | bytes 1048608 | tf_op jit(solution)/shard_map/ppermute | solution.py:385
  781.8 17.7 %collective-permute-done.91.refs_3_ = bf16[128,2048]{1,0:T(8,128)(2,1)S(1)} collective-permute-done((bf16[128,2048]{1,0:T(8,128)(2,1)S(1)}, bf16[128,2048]{1,0:T(8,128)(2,1)S(1)}, u32[]{:S(2)}, u32[]{:S(2)}) %collective-permute-start.91) | collective-permute-done | bytes 524320 | tf_op jit(solution)/shard_map/ppermute | solution.py:353
  831.4 19.4 %collective-permute-done.95.refs_5_ = bf16[4,256,128]{2,1,0:T(8,128)(2,1)S(1)} collective-permute-done((bf16[4,256,128]{2,1,0:T(8,128)(2,1)}, bf16[4,256,128]{2,1,0:T(8,128)(2,1)S(1)}, u32[]{:S(2)}, u32[]{:S(2)}) %collective-permute-start.95) | collective-permute-done | bytes 262176 | tf_op jit(solution)/shard_map/ppermute | solution.py:353
  858.8 40.2 %shard_map.206 = (bf16[3,4,256,128]{3,2,1,0:T(8,128)(2,1)S(1)}, bf16[3,4,256,128]{3,2,1,0:T(8,128)(2,1)}, bf16[3,4,256,128]{3,2,1,0:T(8,128)(2,1)}, bf16[3,4,256,128]{3,2,1,0:T(8,128)(2,1)}) custom-call(s32[16]{0:T(128)S(1)} %fusion.40.place_ref, s32[8]{0:T(128)S(1)} %convert_reduce_fusion.1.starts_ref, bf16[3,4,256,128]{3,2,1,0:T(8,128)(2,1)} %copy-done.139, ...), custom_call_target="tpu_custom_call" | custom-call | flops 21474836480 | bytes 16777216 | tf_op jit(solution)/shard_map/pallas_call | solution.py:1104
  923.1 21.3 %collective-permute-done.109 = bf16[512,512]{1,0:T(8,128)(2,1)S(1)} collective-permute-done((bf16[512,512]{1,0:T(8,128)(2,1)}, bf16[512,512]{1,0:T(8,128)(2,1)S(1)}, u32[]{:S(2)}, u32[]{:S(2)}) %collective-permute-start.109) | collective-permute-done | bytes 524320 | tf_op jit(solution)/shard_map/ppermute | solution.py:353
  958.6 16.4 %collective-permute-done.105.refs_8_.refs_3_ = bf16[3,4,256,128]{3,2,1,0:T(8,128)(2,1)} collective-permute-done((bf16[3,4,256,128]{3,2,1,0:T(8,128)(2,1)}, bf16[3,4,256,128]{3,2,1,0:T(8,128)(2,1)}, u32[]{:S(2)}, u32[]{:S(2)}) %collective-permute-start.105) | collective-permute-done | bytes 786464 | tf_op jit(solution)/shard_map/ppermute | solution.py:376
  1027.7 30.7 %collective-permute-done.120 = bf16[1024,512]{1,0:T(8,128)(2,1)S(1)} collective-permute-done((bf16[1024,512]{1,0:T(8,128)(2,1)S(1)}, bf16[1024,512]{1,0:T(8,128)(2,1)S(1)}, u32[]{:S(2)}, u32[]{:S(2)}) %collective-permute-start.120) | collective-permute-done | bytes 1048608 | tf_op jit(solution)/shard_map/ppermute | solution.py:353
  1081.5 16.6 %collective-permute-done.118 = bf16[128,2048]{1,0:T(8,128)(2,1)S(1)} collective-permute-done((bf16[128,2048]{1,0:T(8,128)(2,1)S(1)}, bf16[128,2048]{1,0:T(8,128)(2,1)S(1)}, u32[]{:S(2)}, u32[]{:S(2)}) %collective-permute-start.118) | collective-permute-done | bytes 524320 | tf_op jit(solution)/shard_map/ppermute | solution.py:353
  1143.1 15.3 %all-to-all-done.3 = f32[256,4,512]{2,0,1:T(8,128)S(1)} async-done(((f32[256,4,512]{2,0,1:T(8,128)}), f32[256,4,512]{2,0,1:T(8,128)S(1)}, u32[]{:S(2)}, u32[]{:S(2)}) %all-to-all-start.3) | async-done | bytes 2097184 | tf_op jit(solution)/shard_map/all_to_all | solution.py:1128
  (783 shorter events, 682.7 us)
Async XLA Ops:
  28.5 37.2 %collective-permute-start.2 = (bf16[3,1024,128]{2,1,0:T(8,128)(2,1)S(1)}, bf16[3,1024,128]{2,1,0:T(8,128)(2,1)}, u32[]{:S(2)}, u32[]{:S(2)}) collective-permute-start(bf16[3,1024,128]{2,1,0:T(8,128)(2,1)S(1)} %slice.298.refs_5_.refs_4_), channel_id=1, source_target_pairs={{0,24},{4,28},{8,16},{12,20},{16,8},{20,12},{24,0},{28,4},{1,25},{... | collective-permute-start | bytes 2359304 | tf_op jit(solution)/shard_map/ppermute | solution.py:385
  85.6 40.6 %collective-permute-start.9 = (bf16[3,1024,128]{2,1,0:T(8,128)(2,1)}, bf16[3,1024,128]{2,1,0:T(8,128)(2,1)}, u32[]{:S(2)}, u32[]{:S(2)}) collective-permute-start(bf16[3,1024,128]{2,1,0:T(8,128)(2,1)} %collective-permute-done.6.refs_10_.refs_9_), channel_id=1, source_target_pairs={{0,16},{16,0},{1,17},{17,1},{2,18},{18,2},{3,19},{19,3},{4,20},{20... | collective-permute-start | bytes 2359304 | tf_op jit(solution)/shard_map/ppermute | solution.py:380
  150.2 75.4 %collective-permute-start.22 = (bf16[1024,512]{1,0:T(8,128)(2,1)S(1)}, bf16[1024,512]{1,0:T(8,128)(2,1)S(1)}, u32[]{:S(2)}, u32[]{:S(2)}) collective-permute-start(bf16[1024,512]{1,0:T(8,128)(2,1)S(1)} %maximum_select_fusion.3.refs_1_.refs_2_), channel_id=1, source_target_pairs={{0,24},{4,28},{8,16},{12,20},{16,8},{20,12},{24,0},{28,4},{1,25},{... | collective-permute-start | bytes 3145736 | tf_op jit(solution)/shard_map/ppermute | solution.py:385
  150.2 42.3 %collective-permute-start.15 = (bf16[3,4,256,128]{3,2,1,0:T(8,128)(2,1)S(1)}, bf16[3,4,256,128]{3,2,1,0:T(8,128)(2,1)S(1)}, u32[]{:S(2)}, u32[]{:S(2)}) collective-permute-start(bf16[3,4,256,128]{3,2,1,0:T(8,128)(2,1)S(1)} %get-tuple-element.273), channel_id=1, source_target_pairs={{0,8},{4,12},{8,0},{12,4},{1,9},{5,13},{9,1},{13,5},{2,10},{6,14},... | collective-permute-start | bytes 2359304 | tf_op jit(solution)/shard_map/ppermute | solution.py:353
  152.0 56.2 %collective-permute-start.16 = (bf16[3,4,256,128]{3,2,1,0:T(8,128)(2,1)S(1)}, bf16[3,4,256,128]{3,2,1,0:T(8,128)(2,1)S(1)}, u32[]{:S(2)}, u32[]{:S(2)}) collective-permute-start(bf16[3,4,256,128]{3,2,1,0:T(8,128)(2,1)S(1)} %get-tuple-element.274), channel_id=1, source_target_pairs={{0,2},{1,3},{2,0},{3,1},{4,6},{5,7},{6,4},{7,5},{8,10},{9,11},{10,... | collective-permute-start | bytes 2359304 | tf_op jit(solution)/shard_map/ppermute | solution.py:353
  174.5 51.2 %collective-permute-start.17 = (bf16[3,4,256,128]{3,2,1,0:T(8,128)(2,1)S(1)}, bf16[3,4,256,128]{3,2,1,0:T(8,128)(2,1)S(1)}, u32[]{:S(2)}, u32[]{:S(2)}) collective-permute-start(bf16[3,4,256,128]{3,2,1,0:T(8,128)(2,1)S(1)} %get-tuple-element.275), channel_id=1, source_target_pairs={{0,10},{1,11},{2,8},{3,9},{4,14},{5,15},{6,12},{7,13},{8,2},{9,3},... | collective-permute-start | bytes 2359304 | tf_op jit(solution)/shard_map/ppermute | solution.py:376
  226.8 48.2 %collective-permute-start.23 = (bf16[1024,512]{1,0:T(8,128)(2,1)S(1)}, bf16[1024,512]{1,0:T(8,128)(2,1)S(1)}, u32[]{:S(2)}, u32[]{:S(2)}) collective-permute-start(bf16[1024,512]{1,0:T(8,128)(2,1)S(1)} %maximum_select_fusion.4.refs_9_.refs_10_), channel_id=1, source_target_pairs={{0,2},{1,3},{2,0},{3,1},{4,6},{5,7},{6,4},{7,5},{8,10},{9,11},{10,... | collective-permute-start | bytes 3145736 | tf_op jit(solution)/shard_map/ppermute | solution.py:353
  308.9 39.0 %collective-permute-start.38 = (bf16[128,2048]{1,0:T(8,128)(2,1)S(1)}, bf16[128,2048]{1,0:T(8,128)(2,1)S(1)}, u32[]{:S(2)}, u32[]{:S(2)}) collective-permute-start(bf16[128,2048]{1,0:T(8,128)(2,1)S(1)} %get-tuple-element.306), channel_id=1, source_target_pairs={{0,1},{1,0},{2,3},{3,2},{4,5},{5,4},{6,7},{7,6},{8,9},{9,8},{10,11... | collective-permute-start | bytes 1572872 | tf_op jit(solution)/shard_map/ppermute | solution.py:353
  418.2 37.2 %collective-permute-start.57 = (bf16[512,1024]{1,0:T(8,128)(2,1)S(1)}, bf16[512,1024]{1,0:T(8,128)(2,1)S(1)}, u32[]{:S(2)}, u32[]{:S(2)}) collective-permute-start(bf16[512,1024]{1,0:T(8,128)(2,1)S(1)} %constant_dynamic-update-slice_fusion.2.refs_5_.refs_7_.refs_8_), channel_id=1, source_target_pairs={{0,24},{4,28},{8,16},{12,20},{16,8},{20,12},{24,0},{28,4},{1,25},{... | collective-permute-start | bytes 3145736 | tf_op jit(solution)/shard_map/ppermute | solution.py:385
  662.0 40.2 %collective-permute-start.85 = (bf16[2,2,512,1024]{3,2,1,0:T(8,128)(2,1)}, bf16[2,2,512,1024]{3,2,1,0:T(8,128)(2,1)}, u32[]{:S(2)}, u32[]{:S(2)}) collective-permute-start(bf16[2,2,512,1024]{3,2,1,0:T(8,128)(2,1)} %get-tuple-element.393), channel_id=1, source_target_pairs={{0,16},{16,0},{1,17},{17,1},{2,18},{18,2},{3,19},{19,3},{4,20},{20... | collective-permute-start | bytes 12582920 | tf_op jit(solution)/shard_map/ppermute | solution.py:380
  760.9 38.7 %collective-permute-start.93 = (bf16[1024,512]{1,0:T(8,128)(2,1)}, bf16[1024,512]{1,0:T(8,128)(2,1)S(1)}, u32[]{:S(2)}, u32[]{:S(2)}) collective-permute-start(bf16[1024,512]{1,0:T(8,128)(2,1)} %get-tuple-element.409), channel_id=1, source_target_pairs={{0,24},{4,28},{8,16},{12,20},{16,8},{20,12},{24,0},{28,4},{1,25},{... | collective-permute-start | bytes 3145736 | tf_op jit(solution)/shard_map/ppermute | solution.py:385
  764.6 48.2 %collective-permute-start.94 = (bf16[512,1024]{1,0:T(8,128)(2,1)S(1)}, bf16[512,1024]{1,0:T(8,128)(2,1)S(1)}, u32[]{:S(2)}, u32[]{:S(2)}) collective-permute-start(bf16[512,1024]{1,0:T(8,128)(2,1)S(1)} %fusion.9), channel_id=1, source_target_pairs={{0,2},{1,3},{2,0},{3,1},{4,6},{5,7},{6,4},{7,5},{8,10},{9,11},{10,... | collective-permute-start | bytes 3145736 | tf_op jit(solution)/shard_map/ppermute | solution.py:353
  813.8 36.9 %collective-permute-start.98 = (bf16[2,2,1024,512]{3,2,1,0:T(8,128)(2,1)}, bf16[2,2,1024,512]{3,2,1,0:T(8,128)(2,1)}, u32[]{:S(2)}, u32[]{:S(2)}) collective-permute-start(bf16[2,2,1024,512]{3,2,1,0:T(8,128)(2,1)} %get-tuple-element.424), channel_id=1, source_target_pairs={{0,16},{16,0},{1,17},{17,1},{2,18},{18,2},{3,19},{19,3},{4,20},{20... | collective-permute-start | bytes 12582920 | tf_op jit(solution)/shard_map/ppermute | solution.py:380
  854.2 45.8 %collective-permute-start.102 = (bf16[1024,512]{1,0:T(8,128)(2,1)}, bf16[1024,512]{1,0:T(8,128)(2,1)S(1)}, u32[]{:S(2)}, u32[]{:S(2)}) collective-permute-start(bf16[1024,512]{1,0:T(8,128)(2,1)} %get-tuple-element.444), channel_id=1, source_target_pairs={{0,24},{4,28},{8,16},{12,20},{16,8},{20,12},{24,0},{28,4},{1,25},{... | collective-permute-start | bytes 3145736 | tf_op jit(solution)/shard_map/ppermute | solution.py:385
  854.3 47.8 %collective-permute-start.101 = (bf16[1024,512]{1,0:T(8,128)(2,1)S(1)}, bf16[1024,512]{1,0:T(8,128)(2,1)S(1)}, u32[]{:S(2)}, u32[]{:S(2)}) collective-permute-start(bf16[1024,512]{1,0:T(8,128)(2,1)S(1)} %get-tuple-element.443), channel_id=1, source_target_pairs={{0,24},{4,28},{8,16},{12,20},{16,8},{20,12},{24,0},{28,4},{1,25},{... | collective-permute-start | bytes 3145736 | tf_op jit(solution)/shard_map/ppermute | solution.py:385
  856.0 47.2 %collective-permute-start.100 = (bf16[1024,512]{1,0:T(8,128)(2,1)}, bf16[1024,512]{1,0:T(8,128)(2,1)S(1)}, u32[]{:S(2)}, u32[]{:S(2)}) collective-permute-start(bf16[1024,512]{1,0:T(8,128)(2,1)} %fusion.8), channel_id=1, source_target_pairs={{0,2},{1,3},{2,0},{3,1},{4,6},{5,7},{6,4},{7,5},{8,10},{9,11},{10,... | collective-permute-start | bytes 3145736 | tf_op jit(solution)/shard_map/ppermute | solution.py:353
  903.2 41.5 %collective-permute-start.103 = (bf16[3,4,256,128]{3,2,1,0:T(8,128)(2,1)}, bf16[3,4,256,128]{3,2,1,0:T(8,128)(2,1)S(1)}, u32[]{:S(2)}, u32[]{:S(2)}) collective-permute-start(bf16[3,4,256,128]{3,2,1,0:T(8,128)(2,1)} %get-tuple-element.446), channel_id=1, source_target_pairs={{0,8},{4,12},{8,0},{12,4},{1,9},{5,13},{9,1},{13,5},{2,10},{6,14},... | collective-permute-start | bytes 2359304 | tf_op jit(solution)/shard_map/ppermute | solution.py:353
  904.2 53.6 %collective-permute-start.104 = (bf16[3,4,256,128]{3,2,1,0:T(8,128)(2,1)}, bf16[3,4,256,128]{3,2,1,0:T(8,128)(2,1)S(1)}, u32[]{:S(2)}, u32[]{:S(2)}) collective-permute-start(bf16[3,4,256,128]{3,2,1,0:T(8,128)(2,1)} %get-tuple-element.447), channel_id=1, source_target_pairs={{0,2},{1,3},{2,0},{3,1},{4,6},{5,7},{6,4},{7,5},{8,10},{9,11},{10,... | collective-permute-start | bytes 2359304 | tf_op jit(solution)/shard_map/ppermute | solution.py:353
  904.2 70.9 %collective-permute-start.105 = (bf16[3,4,256,128]{3,2,1,0:T(8,128)(2,1)}, bf16[3,4,256,128]{3,2,1,0:T(8,128)(2,1)}, u32[]{:S(2)}, u32[]{:S(2)}) collective-permute-start(bf16[3,4,256,128]{3,2,1,0:T(8,128)(2,1)} %get-tuple-element.448), channel_id=1, source_target_pairs={{0,10},{1,11},{2,8},{3,9},{4,14},{5,15},{6,12},{7,13},{8,2},{9,3},... | collective-permute-start | bytes 2359304 | tf_op jit(solution)/shard_map/ppermute | solution.py:376
  922.3 52.7 %collective-permute-start.108 = (bf16[1,1024,128]{2,1,0:T(8,128)(2,1)}, bf16[1,1024,128]{2,1,0:T(8,128)(2,1)S(1)}, u32[]{:S(2)}, u32[]{:S(2)}) collective-permute-start(bf16[1,1024,128]{2,1,0:T(8,128)(2,1)} %get-tuple-element.453), channel_id=1, source_target_pairs={{0,24},{4,28},{8,16},{12,20},{16,8},{20,12},{24,0},{28,4},{1,25},{... | collective-permute-start | bytes 786440 | tf_op jit(solution)/shard_map/ppermute | solution.py:385
  1010.6 47.7 %collective-permute-start.120 = (bf16[1024,512]{1,0:T(8,128)(2,1)S(1)}, bf16[1024,512]{1,0:T(8,128)(2,1)S(1)}, u32[]{:S(2)}, u32[]{:S(2)}) collective-permute-start(bf16[1024,512]{1,0:T(8,128)(2,1)S(1)} %fusion.3), channel_id=1, source_target_pairs={{0,2},{1,3},{2,0},{3,1},{4,6},{5,7},{6,4},{7,5},{8,10},{9,11},{10,... | collective-permute-start | bytes 3145736 | tf_op jit(solution)/shard_map/ppermute | solution.py:353
  1012.6 51.2 %collective-permute-start.114 = (bf16[3,1024,128]{2,1,0:T(8,128)(2,1)S(1)}, bf16[3,1024,128]{2,1,0:T(8,128)(2,1)S(1)}, u32[]{:S(2)}, u32[]{:S(2)}) collective-permute-start(bf16[3,1024,128]{2,1,0:T(8,128)(2,1)S(1)} %get-tuple-element.542), channel_id=1, source_target_pairs={{0,24},{4,28},{8,16},{12,20},{16,8},{20,12},{24,0},{28,4},{1,25},{... | collective-permute-start | bytes 2359304 | tf_op jit(solution)/shard_map/ppermute | solution.py:385
  1023.9 39.4 %collective-permute-start.112 = (bf16[128,2048]{1,0:T(8,128)(2,1)S(1)}, bf16[128,2048]{1,0:T(8,128)(2,1)S(1)}, u32[]{:S(2)}, u32[]{:S(2)}) collective-permute-start(bf16[128,2048]{1,0:T(8,128)(2,1)S(1)} %get-tuple-element.475), channel_id=1, source_target_pairs={{0,1},{1,0},{2,3},{3,2},{4,5},{5,4},{6,7},{7,6},{8,9},{9,8},{10,11... | collective-permute-start | bytes 1572872 | tf_op jit(solution)/shard_map/ppermute | solution.py:353
  1026.1 37.8 %collective-permute-start.113 = (bf16[128,2048]{1,0:T(8,128)(2,1)S(1)}, bf16[128,2048]{1,0:T(8,128)(2,1)S(1)}, u32[]{:S(2)}, u32[]{:S(2)}) collective-permute-start(bf16[128,2048]{1,0:T(8,128)(2,1)S(1)} %get-tuple-element.476), channel_id=1, source_target_pairs={{0,4},{4,0},{8,12},{12,8},{1,5},{5,1},{9,13},{13,9},{2,6},{6,2},{1... | collective-permute-start | bytes 1572872 | tf_op jit(solution)/shard_map/ppermute | solution.py:353
  (308 other events, 6118.1 us)

commit v3 on v2

--- a/solution.py
+++ b/solution.py
@@ -361,19 +361,23 @@
     return flip(values, "row", 2)
 
 
-def flip_zl(values):
+def flip_far(values):
+    return flip(values, "col", 2)
+
+
+def flip_near(values):
     return flip(values, "col", 1)
 
 
-def flip_zh(values):
-    return flip(values, "col", 2)
-
-
-def flip_y_zh(values):
+def flip_y_near(values):
     pairs = [
-        (r * SIDE + c, (r ^ 2) * SIDE + (c ^ 2)) for r in range(SIDE) for c in range(SIDE)
+        (r * SIDE + c, (r ^ 2) * SIDE + (c ^ 1)) for r in range(SIDE) for c in range(SIDE)
     ]
     return lax.ppermute(values, ("row", "col"), pairs)
+
+
+def flip_z(values):
+    return flip(values, "col", 3)
 
 
 def flip_dp(values):
@@ -385,25 +389,51 @@
     return lax.ppermute(values, ("dp", "row"), pairs)
 
 
+def near_gather(block, *events):
+    half = block.shape[0] // 2
+    by_x, by_z = flip_x(block), flip_near(block)
+    next_x, next_z = after((by_x, by_z), *events)
+    return [block, by_x, by_z, flip_near(next_x[:half]), flip_x(next_z[half:])]
+
+
+def near_reduce(far, sides, own):
+    first = near_reduce_far(far)
+    return near_reduce_end(near_reduce_sides(first, sides), own)
+
+
+def near_reduce_far(far):
+    return flip_near(far[0]), flip_x(far[1])
+
+
+def near_reduce_sides(first, sides):
+    far_top, far_bottom = first
+    x_top, x_bottom, z_top, z_bottom = sides
+    return (
+        flip_x((x_top + wide(far_top)).astype(BF)),
+        flip_x(x_bottom),
+        flip_near(z_top),
+        flip_near((z_bottom + wide(far_bottom)).astype(BF)),
+    )
+
+
+def near_reduce_end(got, own):
+    x_top, x_bottom, z_top, z_bottom = got
+    half = x_top.shape[0]
+    top = own[:half] + wide(x_top) + wide(z_top)
+    bottom = own[half:] + wide(x_bottom) + wide(z_bottom)
+    return jnp.concatenate((top, bottom), axis=0)
+
+
 def square_gather(block, *events):
-    half = block.shape[0] // 2
-    by_x, by_z = flip_x(block), flip_zl(block)
-    next_x, next_z = after((by_x, by_z), *events) if events else (by_x, by_z)
-    return [block, by_x, by_z, flip_zl(next_x[:half]), flip_x(next_z[half:])]
-
-
-def square_reduce(far, sides, own, *events):
-    x_top, x_bottom, z_top, z_bottom = sides
-    far_top, far_bottom = flip_zl(far[0]), flip_x(far[1])
-    got_x_bottom, got_z_top = flip_x(x_bottom), flip_zl(z_top)
-    if events:
-        far_top, far_bottom = after((far_top, far_bottom), *events)
-    got_x_top = flip_x((x_top + far_top.astype(F32)).astype(BF))
-    got_z_bottom = flip_zl((z_bottom + far_bottom.astype(F32)).astype(BF))
-    half = far_top.shape[0]
-    top = own[:half] + got_x_top.astype(F32) + got_z_top.astype(F32)
-    bottom = own[half:] + got_x_bottom.astype(F32) + got_z_bottom.astype(F32)
-    return jnp.concatenate((top, bottom), axis=0)
+    by_z, by_x = flip_far(block), flip_x(block)
+    return [block, by_x, by_z, flip_x(after(by_z, *events) if events else by_z)]
+
+
+def square_reduce(far, by_x, by_z, own):
+    got_far = flip_x(far)
+    got_x = flip_x(after(by_x, got_far))
+    got_z = flip_far((by_z + wide(got_far)).astype(BF))
+    return own + wide(got_x) + wide(got_z)
 
 
 def ordered(flag, own, other, axis):
@@ -418,13 +448,13 @@
     return lax.optimization_barrier((values, events))[0]
 
 
-def other_core(quarter):
-    return [flip_dp(piece) for piece in quarter]
-
-
-def piece_list(tall, high, by_y, by_y_high, others):
-    other_tall, other_y, other_high, other_y_high = others
-    return [tall, by_y, other_tall, other_y, high, by_y_high, other_high, other_y_high]
+def both_cores(tall, by_y, high, by_y_high, *events):
+    own = jnp.stack((tall, by_y, high, by_y_high))
+    return own, flip_dp(after(own, *events) if events else own)
+
+
+def piece(pair, slot, y):
+    return pair[slot % 2].at[2 * (slot // 2) + y]
 
 
 def wide(values):
@@ -447,29 +477,37 @@
         setattr(self, "by_y%d" % h, by_y)
         return by_y
 
-    def to_high(self, *events):
+    def to_high(self, flip_z, *events):
         send = (self.here(0, 1) + wide(self.by_y1)).astype(BF)
-        self.high = flip_zh(after(send, *events))
+        self.high = flip_z(after(send, *events))
         return self.high
 
-    def to_x(self, x, axis, *events):
-        total = self.here(0, 0) + wide(self.by_y0) + wide(self.high)
-        total = after(total.astype(BF), *events)
-        size = total.shape[axis] // 2
-        own = lax.dynamic_slice_in_dim(total, x * size, size, axis)
-        other = flip_x(lax.dynamic_slice_in_dim(total, (1 - x) * size, size, axis))
-        self.parts = (own, other)
-        return self.parts
-
-
-def unite(own, by_x, x, q, axis):
-    other_own, other_x = flip_dp(own), flip_dp(by_x)
-    first = jnp.where(x == 0, own, by_x), jnp.where(x == 0, other_own, other_x)
-    second = jnp.where(x == 0, by_x, own), jnp.where(x == 0, other_x, other_own)
+    def total(self, *events):
+        value = self.here(0, 0) + wide(self.by_y0) + wide(self.high)
+        return after(value.astype(BF), *events) if events else value.astype(BF)
+
+
+def to_x(total, x, axis):
+    size = total.shape[axis] // 2
+    own = lax.dynamic_slice_in_dim(total, x * size, size, axis)
+    return own, lax.dynamic_slice_in_dim(total, (1 - x) * size, size, axis)
+
+
+def pair_up(own, by_x, x):
+    return jnp.where(x == 0, jnp.stack((own, by_x)), jnp.stack((by_x, own)))
+
+
+def unite(mine, theirs, q, axis):
     parts = []
-    for mine, theirs in (first, second):
-        parts += [jnp.where(q == 0, mine, theirs), jnp.where(q == 0, theirs, mine)]
+    for at in range(2):
+        parts += [jnp.where(q == 0, mine[at], theirs[at]), jnp.where(q == 0, theirs[at], mine[at])]
     return jnp.concatenate(parts, axis=axis).astype(F32)
+
+
+def exchanged_sum(value, axes, count):
+    tiles = jnp.broadcast_to(value, (count, 8, HD))
+    tiles = lax.all_to_all(tiles, axes, split_axis=0, concat_axis=0, tiled=True)
+    return jnp.sum(tiles[:, 0, 0]).reshape(1)
 
 
 def local_norm(values):
@@ -517,39 +555,55 @@
 
 FAR_SHAPES = [shape((PIECE // 2, D), BF)] * 2
 SIDE_SHAPES = [
+    shape((PIECE, D), BF),
+    shape((PIECE // 2, D), F32),
+    shape((PIECE // 2, D), F32),
+]
+OWN_SHAPES = [shape((PIECE, D), F32)]
+NEAR_SHAPES = [
     shape((PIECE // 2, D), F32),
     shape((PIECE // 2, D), BF),
     shape((PIECE // 2, D), BF),
     shape((PIECE // 2, D), F32),
 ]
-OWN_SHAPES = [shape((PIECE, D), F32)]
-SUM_SHAPES = {"far": FAR_SHAPES, "sides": SIDE_SHAPES, "own": OWN_SHAPES}
+SUM_SHAPES = {"far": FAR_SHAPES, "sides": NEAR_SHAPES, "own": OWN_SHAPES}
 SUM_BLOCKS = {"far": (3,), "sides": (1, 2), "own": (0,)}
 
 
+def store_halves(part, value, outs):
+    half = PIECE // 2
+    for low in range(2):
+        rows = value[low * half : (low + 1) * half]
+        outs[low][:, y_half(part)] = rows.astype(outs[low].dtype)
+
+
 def store_sum(kind, index, part, value, outs):
-    half = PIECE // 2
     if kind == "own":
         outs[0][:, y_half(part)] = value
-        return
-    for low in range(2):
-        out = outs[2 * index + low]
-        out[:, y_half(part)] = value[low * half : (low + 1) * half].astype(out.dtype)
+    else:
+        store_halves(part, value, outs[2 * index : 2 * index + 2])
+
+
+ALL_SHAPES = [shape((PIECE, D), kind) for kind in (F32, BF, F32, BF)]
+
+
+def store_any(a, part, value, outs):
+    outs[a][:, y_half(part)] = value.astype(outs[a].dtype)
 
 
 def qkv_kernel(place_ref, *refs):
-    acts, refs = refs[:5], refs[5:]
-    weights, refs = refs[:8], refs[8:]
+    acts, refs = refs[:4], refs[4:]
+    weights, refs = refs[:2], refs[2:]
     cos_ref, sin_ref, *refs = refs
     outs, weight_s = refs[:4], refs[4]
     for b in range(4):
         for y in range(2):
             for which in range(3):
-                weight_s[y_half(y), columns(which * 4 + b, HD)] = weights[2 * b + y][which]
+                weight_s[y_half(y), columns(which * 4 + b, HD)] = piece(weights, b, y)[which]
     for a in range(4):
         rows = pl.ds(pl.multiple_of(place_ref[a] * PIECE, PIECE), PIECE)
         cos_block, sin_block = cos_ref[rows, :], sin_ref[rows, :]
-        act = acts[a][...] if a < 3 else jnp.concatenate((acts[3][...], acts[4][...]), axis=0)
+        act = acts[a][...]
         projected = dot(act, weight_s[...], 1, 0)
         for which in range(3):
             for b in range(4):
@@ -563,7 +617,7 @@
     return pl.pallas_call(
         qkv_kernel,
         out_shape=[shape((3, 4, PIECE, HD), BF)] * 4,
-        in_specs=[SMEM_SPEC] + [VMEM_SPEC] * 15,
+        in_specs=[SMEM_SPEC] + [VMEM_SPEC] * 8,
         out_specs=[VMEM_SPEC] * 4,
         scratch_shapes=[pltpu.VMEM((D, 12 * HD), BF)],
         compiler_params=params(40),
@@ -573,76 +627,68 @@
 
 def out_kernel(*refs):
     mixed, refs = refs[:4], refs[4:]
-    weights, refs = refs[:8], refs[8:]
-    outs, weight_s = refs[:7], refs[7]
+    weights, refs = refs[:2], refs[2:]
+    outs, weight_s = refs[:4], refs[4]
     for b in range(4):
         for y in range(2):
-            weight_s[y_half(y), columns(b, HD)] = weights[2 * b + y][...]
-    at = 0
-    for kind in ("far", "sides", "own"):
-        for index, a in enumerate(SUM_BLOCKS[kind]):
-            act = jnp.concatenate([mixed[b][a] for b in range(4)], axis=1)
-            for y in range(2):
-                value = dot(act, weight_s[y_half(y), :], 1, 1)
-                store_sum(kind, index, y, value, outs[at:])
-        at += len(SUM_SHAPES[kind])
+            weight_s[y_half(y), columns(b, HD)] = piece(weights, b, y)[3]
+    for a in range(4):
+        act = jnp.concatenate([mixed[b][a] for b in range(4)], axis=1)
+        for y in range(2):
+            store_any(a, y, dot(act, weight_s[y_half(y), :], 1, 1), outs)
 
 
 def run_out(mixed, weights):
     outs = pl.pallas_call(
         out_kernel,
-        out_shape=FAR_SHAPES + SIDE_SHAPES + OWN_SHAPES,
-        in_specs=[VMEM_SPEC] * 12,
-        out_specs=[VMEM_SPEC] * 7,
+        out_shape=ALL_SHAPES,
+        in_specs=[VMEM_SPEC] * 6,
+        out_specs=[VMEM_SPEC] * 4,
         scratch_shapes=[pltpu.VMEM((D, 4 * HD), BF)],
         compiler_params=params(36),
         cost_estimate=cost(2 * 4 * PIECE * D * 4 * HD, 16 * 2**20),
     )(*mixed, *weights)
-    return outs[:2], outs[2:6], outs[6]
+    return outs[3], outs[1], outs[2], outs[0]
 
 
 def input_kernel(*refs):
     back, refs = refs[:4], refs[4:]
-    weights, refs = refs[:8], refs[8:]
-    outs, weight_s = refs[:7], refs[7]
+    weights, refs = refs[:2], refs[2:]
+    outs, weight_s = refs[:4], refs[4]
     for b in range(4):
         for y in range(2):
             for which in range(3):
-                weight_s[y_half(y), columns(which * 4 + b, HD)] = weights[2 * b + y][which]
-    at = 0
-    for kind in ("far", "sides", "own"):
-        for index, a in enumerate(SUM_BLOCKS[kind]):
-            act = jnp.concatenate(
-                [back[b][which, a] for which in range(3) for b in range(4)], axis=1
-            )
-            for y in range(2):
-                value = dot(act, weight_s[y_half(y), :], 1, 1)
-                store_sum(kind, index, y, value, outs[at:])
-        at += len(SUM_SHAPES[kind])
+                weight_s[y_half(y), columns(which * 4 + b, HD)] = piece(weights, b, y)[which]
+    for a in range(4):
+        act = jnp.concatenate(
+            [back[b][which, a] for which in range(3) for b in range(4)], axis=1
+        )
+        for y in range(2):
+            store_any(a, y, dot(act, weight_s[y_half(y), :], 1, 1), outs)
 
 
 def run_input(back, weights):
     outs = pl.pallas_call(
         input_kernel,
-        out_shape=FAR_SHAPES + SIDE_SHAPES + OWN_SHAPES,
-        in_specs=[VMEM_SPEC] * 12,
-        out_specs=[VMEM_SPEC] * 7,
+        out_shape=ALL_SHAPES,
+        in_specs=[VMEM_SPEC] * 6,
+        out_specs=[VMEM_SPEC] * 4,
         scratch_shapes=[pltpu.VMEM((D, 12 * HD), BF)],
         compiler_params=params(40),
         cost_estimate=cost(2 * 4 * PIECE * D * 12 * HD, 20 * 2**20),
     )(*back, *weights)
-    return outs[:2], outs[2:6], outs[6]
+    return outs[3], outs[1], outs[2], outs[0]
 
 
 def attended_grad_kernel(*refs):
-    acts, refs = refs[:5], refs[5:]
-    weights, refs = refs[:8], refs[8:]
+    acts, refs = refs[:4], refs[4:]
+    weights, refs = refs[:2], refs[2:]
     outs, weight_s = refs[:4], refs[4]
     for b in range(4):
         for y in range(2):
-            weight_s[y_half(y), columns(b, HD)] = weights[2 * b + y][...]
+            weight_s[y_half(y), columns(b, HD)] = piece(weights, b, y)[3]
     for a in range(4):
-        act = acts[a][...] if a < 3 else jnp.concatenate((acts[3][...], acts[4][...]), axis=0)
+        act = acts[a][...]
         value = dot(act, weight_s[...], 1, 0)
         for b in range(4):
             outs[b][a] = value[:, columns(b, HD)].astype(BF)
@@ -652,7 +698,7 @@
     return pl.pallas_call(
         attended_grad_kernel,
         out_shape=[shape((4, PIECE, HD), BF)] * 4,
-        in_specs=[VMEM_SPEC] * 13,
+        in_specs=[VMEM_SPEC] * 6,
         out_specs=[VMEM_SPEC] * 4,
         scratch_shapes=[pltpu.VMEM((D, 4 * HD), BF)],
         compiler_params=params(36),
@@ -665,8 +711,8 @@
 
 def up_kernel(count, *refs):
     acts, refs = refs[:count], refs[count:]
-    gates, refs = refs[:8], refs[8:]
-    ups, refs = refs[:8], refs[8:]
+    gates, refs = refs[:2], refs[2:]
+    ups, refs = refs[:2], refs[2:]
     gating_ref, upward_ref, units_ref = refs
     start = 0
     for act_ref in acts:
@@ -675,8 +721,9 @@
         start += size
         low, high = act_ref[:, y_half(0)], act_ref[:, y_half(1)]
         for b in range(4):
-            gate = dot(low, gates[2 * b][...], 1, 0) + dot(high, gates[2 * b + 1][...], 1, 0)
-            up = dot(low, ups[2 * b][...], 1, 0) + dot(high, ups[2 * b + 1][...], 1, 0)
+            gate = dot(low, piece(gates, b, 0)[...], 1, 0)
+            gate += dot(high, piece(gates, b, 1)[...], 1, 0)
+            up = dot(low, piece(ups, b, 0)[...], 1, 0) + dot(high, piece(ups, b, 1)[...], 1, 0)
             gating_ref[b, rows] = gate
             upward_ref[b, rows] = up
             units_ref[b, rows] = (gate * jax.nn.sigmoid(gate) * up).astype(BF)
@@ -684,15 +731,15 @@
 
 def run_up(acts, gates, ups):
     rows = sum(act.shape[0] for act in acts)
-    width = gates[0].shape[1]
+    width = gates[0].shape[2]
     whole = lambda act: pl.BlockSpec(act.shape, lambda j: (0, 0))
-    piece = pl.BlockSpec((HALF, CHUNK), lambda j: (0, j))
+    part = pl.BlockSpec((4, HALF, CHUNK), lambda j: (0, 0, j))
     out = pl.BlockSpec((4, rows, CHUNK), lambda j: (0, 0, j))
     return pl.pallas_call(
         lambda *refs: up_kernel(len(acts), *refs),
         grid=(width // CHUNK,),
         out_shape=[shape((4, rows, width), kind) for kind in (F32, F32, BF)],
-        in_specs=[whole(act) for act in acts] + [piece] * 16,
+        in_specs=[whole(act) for act in acts] + [part] * 4,
         out_specs=[out] * 3,
         compiler_params=params(48),
         cost_estimate=cost(2 * rows * D * 8 * width, 16 * 2**20, 4 * rows * width),
@@ -700,13 +747,13 @@
 
 
 def down_kernel(kind, units_ref, *refs):
-    weights, outs = refs[:8], refs[8:]
+    weights, outs = refs[:2], refs[2:]
     for index in range(len(SUM_BLOCKS[kind])):
         rows = slice(index * PIECE, (index + 1) * PIECE)
         for y in range(2):
-            value = dot(units_ref[0, rows], weights[y][...], 1, 0)
+            value = dot(units_ref[0, rows], piece(weights, 0, y)[...], 1, 0)
             for b in range(1, 4):
-                value += dot(units_ref[b, rows], weights[2 * b + y][...], 1, 0)
+                value += dot(units_ref[b, rows], piece(weights, b, y)[...], 1, 0)
             store_sum(kind, index, y, value, outs)
 
 
@@ -716,7 +763,7 @@
     return pl.pallas_call(
         lambda *refs: down_kernel(kind, *refs),
         out_shape=shapes,
-        in_specs=[VMEM_SPEC] * 9,
+        in_specs=[VMEM_SPEC] * 3,
         out_specs=[VMEM_SPEC] * len(shapes),
         compiler_params=params(36),
         cost_estimate=cost(2 * rows * D * 4 * width, 12 * 2**20),
@@ -726,7 +773,7 @@
 def gated_kernel(count, *refs):
     acts, refs = refs[:count], refs[count:]
     gating_ref, upward_ref, *refs = refs
-    weights, refs = refs[:8], refs[8:]
+    weights, refs = refs[:2], refs[2:]
     gate_ref, up_ref = refs
     start = 0
     for act_ref in acts:
@@ -735,7 +782,8 @@
         start += size
         low, high = act_ref[:, y_half(0)], act_ref[:, y_half(1)]
         for b in range(4):
-            grad = dot(low, weights[2 * b][...], 1, 1) + dot(high, weights[2 * b + 1][...], 1, 1)
+            grad = dot(low, piece(weights, b, 0)[...], 1, 1)
+            grad += dot(high, piece(weights, b, 1)[...], 1, 1)
             gate = gating_ref[b, rows]
             sigmoid = jax.nn.sigmoid(gate)
             gate_ref[b, rows] = (
@@ -749,7 +797,7 @@
     return pl.pallas_call(
         lambda *refs: gated_kernel(len(acts), *refs),
         out_shape=[shape((4, rows, width), BF)] * 2,
-        in_specs=[VMEM_SPEC] * (len(acts) + 10),
+        in_specs=[VMEM_SPEC] * (len(acts) + 4),
         out_specs=[VMEM_SPEC] * 2,
         compiler_params=params(44),
         cost_estimate=cost(2 * rows * D * 4 * width, 16 * 2**20, 4 * rows * width),
@@ -757,16 +805,16 @@
 
 
 def normed_two_kernel(kind, gate_ref, up_ref, *refs):
-    gates, refs = refs[:8], refs[8:]
-    ups, refs = refs[:8], refs[8:]
+    gates, refs = refs[:2], refs[2:]
+    ups, refs = refs[:2], refs[2:]
     outs, total_s = refs[:-1], refs[-1]
     step, last = pl.program_id(0), pl.num_programs(0) - 1
     for y in range(2):
-        value = dot(gate_ref[0], gates[y][...], 1, 1)
+        value = dot(gate_ref[0], piece(gates, 0, y)[...], 1, 1)
         for b in range(4):
             if b > 0:
-                value += dot(gate_ref[b], gates[2 * b + y][...], 1, 1)
-            value += dot(up_ref[b], ups[2 * b + y][...], 1, 1)
+                value += dot(gate_ref[b], piece(gates, b, y)[...], 1, 1)
+            value += dot(up_ref[b], piece(ups, b, y)[...], 1, 1)
 
         @pl.when(step == 0)
         def _():
@@ -784,12 +832,12 @@
     rows, width = gate_low.shape[1], gate_low.shape[2]
     shapes = SUM_SHAPES[kind]
     low = pl.BlockSpec((4, rows, width // 2), lambda j: (0, 0, j))
-    piece = pl.BlockSpec((HALF, width // 2), lambda j: (0, j))
+    part = pl.BlockSpec((4, HALF, width // 2), lambda j: (0, 0, j))
     return pl.pallas_call(
         lambda *refs: normed_two_kernel(kind, *refs),
         grid=(2,),
         out_shape=shapes,
-        in_specs=[low] * 2 + [piece] * 16,
+        in_specs=[low] * 2 + [part] * 4,
         out_specs=[pl.BlockSpec(s.shape, lambda j: (0, 0)) for s in shapes],
         scratch_shapes=[pltpu.VMEM((rows, D), F32)],
         compiler_params=params(48),
@@ -875,8 +923,9 @@
 
 
 def head_grad_kernel(kinds, *refs):
-    acts, refs = refs[:5], refs[5:]
+    acts, refs = refs[:4], refs[4:]
     messages, refs = refs[:4], refs[4:]
+    passed, refs = (refs[:2], refs[2:]) if kinds > 1 else (None, refs)
     outs, turned_s, right_s = refs[:2], refs[2], refs[3]
     start = 0
     for act_ref in acts:
@@ -896,24 +945,30 @@
         value = dot(turned_s[...], right_s[:, columns(which, 4 * HD)], 1, 0)
         for b, (d, h) in enumerate(SLOTS):
             outs[d][0, h, which] = value[:, columns(b, HD)].astype(BF)
-
-
-def run_head_grad(kinds, acts, messages):
+    if passed:
+        for d in range(2):
+            outs[d][0, :, kinds] = passed[d][0, :, 0]
+
+
+def run_head_grad(kinds, acts, messages, passed=()):
     whole = lambda dims: pl.BlockSpec(dims, lambda y: (0,) * len(dims))
+    rows = lambda count: pl.BlockSpec((1, 2, count, HALF, HD), lambda y: (y, 0, 0, 0, 0))
+    made = kinds + 1 if passed else kinds
     return pl.pallas_call(
         lambda *refs: head_grad_kernel(kinds, *refs),
         grid=(2,),
-        out_shape=[shape((2, 2, kinds, HALF, HD), BF)] * 2,
+        out_shape=[shape((2, 2, made, HALF, HD), BF)] * 2,
         in_specs=[pl.BlockSpec((act.shape[0], HALF), lambda y: (0, y)) for act in acts]
-        + [whole(message.shape) for message in messages],
-        out_specs=[pl.BlockSpec((1, 2, kinds, HALF, HD), lambda y: (y, 0, 0, 0, 0))] * 2,
+        + [whole(message.shape) for message in messages]
+        + [rows(1)] * len(passed),
+        out_specs=[rows(made)] * 2,
         scratch_shapes=[
             pltpu.VMEM((HALF, 4 * PIECE), BF),
             pltpu.VMEM((4 * PIECE, kinds * 4 * HD), BF),
         ],
-        compiler_params=params(40),
+        compiler_params=params(44),
         cost_estimate=cost(2 * 4 * PIECE * D * kinds * 4 * HD, 12 * 2**20),
-    )(*acts, *messages)
+    )(*acts, *messages, *passed)
 
 
 def allowed_pairs(starts, query0, key0, shape, query_axis):
@@ -1117,7 +1172,7 @@
 
 
 def swap_slots(messages):
-    return [messages[0], flip_y(messages[1]), flip_zh(messages[2]), flip_y_zh(messages[3])]
+    return [messages[0], flip_y(messages[1]), flip_near(messages[2]), flip_y_near(messages[3])]
 
 
 def to_tokens(values):
@@ -1166,7 +1221,7 @@
     starts = jnp.sum((segment[None, :] < labels[:, None]).astype(jnp.int32), axis=1)
     codes = jnp.arange(16, dtype=jnp.int32)
     relative = (
-        (codes & 1) + ((codes >> 1) & 1) * 4 + ((codes >> 2) & 1) * 2 + ((codes >> 3) & 1) * 8
+        (codes & 1) + ((codes >> 1) & 1) * 8 + ((codes >> 2) & 1) * 2 + ((codes >> 3) & 1) * 4
     )
     pieces = relative ^ own_piece
     frequency = jnp.power(10000.0, jnp.arange(HD // 2, dtype=F32) * (-2.0 / HD))
@@ -1174,181 +1229,159 @@
     sign = jnp.where(jnp.arange(HD) < HD // 2, -1.0, 1.0)
     cos_wide, sin_wide = jnp.cos(angles), jnp.sin(angles) * sign[None, :]
 
-    heads_x = after(flip_x(head_cut(1 - x)), cos_wide, sin_wide)
+    heads_x = flip_x(head_cut(1 - x))
+    count = exchanged_sum(jnp.sum(valid.astype(F32)), ("dp", "col"), 2 * SIDE)
+    heads_x = after(heads_x, count)
     gates_x = flip_x(after(cut(gate_weight, 1 - x, 1), heads_x))
     hidden = swap_y(to_tokens(after(hidden_in, heads_x))).astype(F32)
-    all_heads = ordered(x, head_cut(x), heads_x, 1)
-    heads_tall, outs_tall = all_heads[:3], all_heads[3]
-    heads_high = flip_zh(heads_tall)
+    heads_tall = ordered(x, head_cut(x), heads_x, 1)
+    heads_high = flip_near(heads_tall)
     heads_y = flip_dp_y(heads_tall)
-    hidden = after(hidden, gates_x)
+    normed, inverse_one = local_norm(after(hidden, gates_x))
+    low_normed = normed.astype(BF)
+    normed_acts = square_gather(low_normed)
+    heads_y_high = flip_dp_y(after(heads_high, low_normed))
     gates_tall = ordered(x, cut(gate_weight, x, 1), gates_x, 0)
-    row_half = gates_tall.shape[0] // 2
-    normed, inverse_one = local_norm(hidden)
-    normed_acts = square_gather(normed.astype(BF), heads_high)
-    gates_first = flip_zh(after(gates_tall[:row_half], heads_high))
-    heads_y_high = flip_dp_y(heads_high)
-    gates_second = flip_zh(after(gates_tall[row_half:], gates_first))
-    heads_other = other_core(
-        (heads_tall, heads_y, heads_high, after(heads_y_high, gates_first))
-    )
-    heads = piece_list(heads_tall, heads_high, heads_y, heads_y_high, heads_other)
-
-    heads, normed_acts = after((heads, normed_acts), gates_second)
-    gates_high = jnp.concatenate((gates_first, gates_second), axis=0)
+    gates_high = flip_far(after(gates_tall, heads_high, normed_acts[1:3]))
+    cos_wide, sin_wide = after((cos_wide, sin_wide), heads_tall)
+    heads = both_cores(
+        heads_tall, heads_y, heads_high, after(heads_y_high, normed_acts[1:3], cos_wide, sin_wide)
+    )
+    gates_y = flip_dp_y(after(gates_tall, normed_acts))
+
     messages = run_qkv(pieces, normed_acts, heads, cos_wide, sin_wide)
-    ups_x = flip_x(after(cut(up_weight, 1 - x, 1), messages[0]))
-    downs_x = flip_x(after(cut(down_weight, 1 - x, 0), messages[0]))
-    outs_high = flip_zh(after(outs_tall, messages[0]))
-    outs_y = flip_dp_y(after(outs_tall, messages[0]))
-    gates_y = flip_dp_y(after(gates_tall, outs_y))
+    mlp_x = jnp.stack((cut(up_weight, 1 - x, 1), cut(down_weight, 1 - x, 0)))
+    mlp_x = flip_x(after(mlp_x, messages[0]))
+    target = to_tokens(after(teacher, messages[0]))
     messages = swap_slots(messages)
-    messages = after(messages, ups_x, downs_x, outs_high, outs_y, gates_y)
-
-    ups_tall = ordered(x, cut(up_weight, x, 1), after(ups_x, messages), 0)
-    ups_high = flip_zh(ups_tall)
-    outs_y_high = flip_dp_y(after(outs_high, messages))
+    messages = after(messages, mlp_x, gates_high, gates_y, target)
+
+    ups_tall = ordered(x, cut(up_weight, x, 1), after(mlp_x[0], messages), 0)
+    ups_high = flip_far(after(ups_tall, gates_high))
     gates_y_high = flip_dp_y(after(gates_high, messages))
+    ups_y = flip_dp_y(ups_tall)
     *mixed, wide_mixed, log_total = run_forward(pieces, starts, messages)
-    mixed = after(mixed, ups_high, outs_y_high, gates_y_high)
-    outs_other = other_core(after((outs_tall, outs_y, outs_high, outs_y_high), mixed))
-    outs = piece_list(outs_tall, outs_high, outs_y, outs_y_high, outs_other)
+    mixed = after(mixed, gates_y_high)
+    downs_tall = ordered(x, cut(down_weight, x, 0), after(mlp_x[1], mixed), 1)
     mixed = swap_slots(mixed)
-
-    downs_tall = ordered(x, cut(down_weight, x, 0), after(downs_x, mixed), 1)
-    middle_row = downs_tall.shape[0] // 2
-    downs_first = flip_zh(downs_tall[:middle_row])
-    downs_second = flip_zh(after(downs_tall[middle_row:], downs_first))
-    ups_y = flip_dp_y(after(ups_tall, mixed))
-    ups_y_high = flip_dp_y(after(ups_high, ups_y))
-    gates_other = other_core(after((gates_tall, gates_y, gates_high, gates_y_high), mixed))
-    gates = piece_list(gates_tall, gates_high, gates_y, gates_y_high, gates_other)
-    sums = run_out(mixed, outs)
-    after_attention = hidden + square_reduce(*sums, downs_first, ups_y)
-    after_attention = after(after_attention, downs_second, ups_y_high, gates_other)
+    mixed = after(mixed, ups_high, ups_y)
+    gates = both_cores(gates_tall, gates_y, gates_high, gates_y_high, mixed)
+
+    ups_y_high = flip_dp_y(after(ups_high, mixed))
+    downs_y = flip_dp_y(after(downs_tall, ups_y_high))
+    after_attention = hidden + square_reduce(*run_out(mixed, heads))
+    after_attention = after(after_attention, ups_y_high, gates, downs_y)
 
     normed_two, inverse_two = local_norm(after_attention)
-    ups_other = other_core(after((ups_tall, ups_y, ups_high, ups_y_high), normed_two))
-    ups = piece_list(ups_tall, ups_high, ups_y, ups_y_high, ups_other)
-    downs_high = jnp.concatenate((downs_first, downs_second), axis=0)
+    ups = both_cores(ups_tall, ups_y, ups_high, ups_y_high, normed_two)
     low_two = normed_two.astype(BF)
-    downs_y = flip_dp_y(after(downs_tall, normed_two))
     up_own = run_up([low_two], gates, ups)
-    two_acts = square_gather(low_two, up_own)
-    downs_y_high = flip_dp_y(after(downs_high, downs_y))
-    count = jnp.sum(valid.astype(F32)).reshape(1)
-    count = count + flip_dp(after(count, low_two))
-    up_sides = run_up(after(two_acts[1:3], up_own[2], downs_y, count), gates, ups)
-    downs_other = other_core(
-        after((downs_tall, downs_y, downs_high, downs_y_high), up_own[2])
-    )
-    count = count + flip_zh(after(count, two_acts[1:3]))
-    up_far = run_up(after(two_acts[3:], up_sides[2], downs_y_high, count), gates, ups)
-    count = count + flip_zl(after(count, two_acts))
-    downs = piece_list(downs_tall, downs_high, downs_y, downs_y_high, downs_other)
+    two_acts = near_gather(low_two, up_own)
+    downs_high = flip_far(after(downs_tall, low_two))
+    downs_y_high = flip_dp_y(after(downs_high, two_acts[1:3], up_own[2]))
+    up_sides = run_up(after(two_acts[1:3], up_own[2]), gates, ups)
+    up_far = run_up(after(two_acts[3:], up_sides[2], downs_y_high), gates, ups)
+    downs = both_cores(downs_tall, downs_y, downs_high, downs_y_high, two_acts, up_sides[2])
     ups_out = [up_own, up_sides, up_far]
     units = [out[2] for out in ups_out]
-    down_far = run_down("far", after(units[2], count), downs)
+    down_far = run_down("far", units[2], downs)
     down_sides = run_down("sides", after(units[1], down_far), downs)
     down_own = run_down("own", after(units[0], down_sides), downs)
-    output = after_attention + square_reduce(down_far, down_sides, down_own[0])
+    output = after_attention + near_reduce(down_far, down_sides, down_own[0])
 
     total_count = jnp.maximum(count, 1.0)
     counted_home = lax.dynamic_slice_in_dim(
         valid.astype(F32), row * home_tokens, home_tokens, 0
     )[:, None]
-    target = swap_y(to_tokens(after(teacher, mixed)))
-    differ = output - target.astype(F32)
+    differ = output - swap_y(target).astype(F32)
     local_loss = jnp.sum(counted_home * (differ * differ)) / D
     all_tokens = group_tokens * lax.axis_size("dp")
     out_grad = counted_home * differ * (all_tokens / total_count)
 
     low_out = out_grad.astype(BF)
-    loss = local_loss.reshape(1)
-    loss = loss + flip_dp(after(loss, low_out))
+    loss = exchanged_sum(after(local_loss, low_out), ("dp", "row", "col"), 2 * SIDE * SIDE)
     low_own = run_gated([low_out], up_own[0], up_own[1], downs)
-    out_acts = square_gather(low_out, low_own)
-    low_sides = run_gated(after(out_acts[1:3], low_own, loss), up_sides[0], up_sides[1], downs)
-    loss = loss + flip_y(after(loss, out_acts[1:3]))
+    out_acts = near_gather(low_out, low_own)
+    low_sides = run_gated(after(out_acts[1:3], low_own), up_sides[0], up_sides[1], downs)
     low_far = run_gated(after(out_acts[3:], low_sides, loss), up_far[0], up_far[1], downs)
-    loss = loss + flip_zl(after(loss, low_sides))
     lows = [low_own, low_sides, low_far]
-    two_far = run_normed_two("far", *after(low_far, loss), gates, ups)
-    loss = loss + flip_x(after(loss, low_far))
-    two_sides = run_normed_two("sides", *after(low_sides, two_far, loss), gates, ups)
-    loss = loss + flip_zh(after(loss, two_far))
-
-    down_grads = Spread(run_down_grad(after(units, two_sides), after(out_acts, loss)))
+    two_far = run_normed_two("far", *low_far, gates, ups)
+    two_sides = run_normed_two("sides", *after(low_sides, two_far), gates, ups)
+
+    first = near_reduce_far(two_far)
+    down_grads = Spread(run_down_grad(after(units, two_sides, first), out_acts))
+    got = near_reduce_sides(first, two_sides)
     down_core = down_grads.to_core()
-    two_own = run_normed_two("own", *after(low_own, down_grads.keep), gates, ups)
+    two_own = run_normed_two("own", *after(low_own, down_grads.keep, got[1:3]), gates, ups)
+    normed_two_grad = near_reduce_end(got, two_own[0])
     gate_pair = run_wide_grad(two_acts, after([low[0] for low in lows], two_own, down_core))
     gate_grads = Spread(gate_pair)
     down_y1 = down_grads.to_y(1)
-    normed_two_grad = square_reduce(two_far, two_sides, two_own[0])
-    normed_two_grad = after(normed_two_grad, down_y1, gate_pair)
     middle_grad = out_grad + local_norm_backward(normed_two_grad, normed_two, inverse_two)
     low_middle = middle_grad.astype(BF)
     gate_core = gate_grads.to_core(low_middle)
     down_y0 = down_grads.to_y(0, low_middle)
     up_pair = run_wide_grad(two_acts, after([low[1] for low in lows], gate_pair))
     up_grads = Spread(up_pair)
-    middle_acts = square_gather(low_middle, down_y0, gate_core)
-    down_grads.to_high(down_y0)
-    gate_y1 = gate_grads.to_y(1, down_y0)
-    middle_acts = after(middle_acts, up_pair, gate_y1)
-    grad_messages = run_attended_grad(middle_acts, outs)
-    grad_messages = after(grad_messages, down_grads.high)
+    middle_acts = square_gather(low_middle, gate_pair, down_y1)
+    gate_y1 = gate_grads.to_y(1, down_y0, middle_acts[1:3])
+    middle_acts = after(middle_acts, up_pair, down_y0, gate_y1)
+    grad_messages = run_attended_grad(middle_acts, heads)
     up_core = up_grads.to_core(grad_messages)
-    gate_y0 = gate_grads.to_y(0, grad_messages)
-    out_grads = Spread(run_head_grad(1, after(middle_acts, grad_messages), mixed))
+    gate_y0 = gate_grads.to_y(0, gate_y1)
+    down_grads.to_high(flip_far, middle_acts[1:3])
+    out_pair = run_head_grad(1, after(middle_acts, grad_messages), mixed)
     grad_messages = swap_slots(grad_messages)
-    grad_messages = after(grad_messages, up_core, out_grads.keep, gate_y0)
-    gate_grads.to_high(grad_messages)
+    grad_messages = after(grad_messages, up_core, out_pair, gate_y0)
+    layer_output = to_width(swap_y(after(output, grad_messages).astype(BF)))
+    up_y0 = up_grads.to_y(0, grad_messages)
     up_y1 = up_grads.to_y(1, grad_messages)
-    up_y0 = up_grads.to_y(0, grad_messages)
     back = run_backward(
         pieces, starts, messages, grad_messages, wide_mixed, log_total, cos_wide, sin_wide
     )
-    back = after(back, gate_grads.high, up_y1, up_y0)
-    layer_output = to_width(swap_y(after(output, back).astype(BF)))
-    gate_grads.to_x(x, 0, back)
-    down_grads.to_x(x, 1, back)
-    out_core = out_grads.to_core(back)
-    out_y1 = out_grads.to_y(1, back)
-    out_y0 = out_grads.to_y(0, back)
+    back = after(back, down_grads.high, up_y1, up_y0)
+    gate_grads.to_high(flip_far, back)
+    own_down, send_down = to_x(down_grads.total(back), x, 1)
+    down_x = flip_x(send_down)
     back = swap_slots(back)
-    back = after(back, out_y1, out_y0, gate_grads.parts, down_grads.parts, layer_output)
-    up_grads.to_high(back)
-    head_pair = run_head_grad(3, normed_acts, back)
+    back = after(back, down_x, gate_grads.high, layer_output)
+    up_grads.to_high(flip_far, back)
+    head_pair = run_head_grad(3, normed_acts, back, out_pair)
     head_grads = Spread(head_pair)
     head_core = head_grads.to_core()
     input_sums = run_input(after(back, head_pair), heads)
     input_sums = after(input_sums, head_core)
     head_y1 = head_grads.to_y(1)
-    normed_grad = square_reduce(*input_sums, head_y1)
+    normed_grad = square_reduce(*input_sums)
     head_y0 = head_grads.to_y(0, head_y1)
-    out_grads.to_high(up_grads.high)
-    head_grads.to_high(head_y1)
-    normed_grad = after(normed_grad, head_y0, up_grads.high)
-    up_grads.to_x(x, 0, normed_grad)
-    out_grads.to_x(x, 1, normed_grad)
+    head_grads.to_high(flip_near, head_y1)
+    down_mine = pair_up(own_down, down_x, x)
+    down_theirs = flip_dp(after(down_mine, input_sums))
+    normed_grad = after(normed_grad, head_y0, head_grads.high, down_theirs, up_grads.high)
     input_gradient = middle_grad + local_norm_backward(normed_grad, normed, inverse_one)
-    head_grads.to_x(x, 1, normed_grad)
+    own_head, send_head = to_x(head_grads.total(normed_grad), x, 1)
+    own_gate, send_gate = to_x(gate_grads.total(input_sums), x, 0)
+    own_up, send_up = to_x(up_grads.total(normed_grad), x, 0)
+    head_x = flip_x(send_head)
+    last_x = flip_x(jnp.stack((send_gate, send_up)))
+    last_mine = jnp.stack((pair_up(own_gate, last_x[0], x), pair_up(own_up, last_x[1], x)))
+    last_theirs = flip_dp(last_mine)
+    head_mine = pair_up(own_head, head_x, x)
+    head_theirs = flip_dp(head_mine)
     mean_loss = loss / total_count
 
-    down_grad = unite(*down_grads.parts, x, q, 0)
-    gate_grad = unite(*gate_grads.parts, x, q, 1)
-    up_grad = unite(*up_grads.parts, x, q, 1)
-    out_weight_grad = unite(*out_grads.parts, x, q, 2)
-    head_grads = unite(*head_grads.parts, x, q, 2)
+    gate_grad = unite(last_mine[0], last_theirs[0], q, 1)
+    down_grad = unite(down_mine, down_theirs, q, 0)
+    up_grad = unite(last_mine[1], last_theirs[1], q, 1)
+    head_grads = unite(head_mine, head_theirs, q, 2)
     return (
         layer_output,
         mean_loss,
-        to_width(swap_y(input_gradient)),
+        to_width(swap_y(input_gradient.astype(BF))).astype(F32),
         head_grads[0],
         head_grads[1],
         head_grads[2],
-        out_weight_grad[0].T,
+        head_grads[3].T,
         gate_grad,
         up_grad,
         down_grad,

time: 1170 us -> 1070 us (0.915)
  waiting for transfers between devices: 575 us -> 526 us
  starting transfers between devices: 142 us -> 97.9 us
  local copies, waits for them, and re-layouts: 96.1 us -> 68.5 us
  Pallas kernels: 257 us -> 279 us
    ppermute x20 -> x16, waiting for transfers between devices: 82.2 us -> 7.34 us  [flip_dp_y(): return lax.ppermute(values, ('dp', 'row'), pairs)]
    ppermute x75 -> x54, starting transfers between devices: 92.2 us -> 53.6 us  [flip(): return lax.ppermute(values, axis, [(i, i ^ bit) for i in range(SIDE)])]
    all_to_all x2, waiting for transfers between devices: 0.01 us -> 32.7 us  [to_tokens(): lax.all_to_all(values, 'row', split_axis=0, concat_axis=1, tiled=True)]
    unnamed x391 -> x268, local copies, waits for them, and re-layouts: 72.7 us -> 41.1 us
    ppermute x4, waiting for transfers between devices: 39.7 us -> 26.5 us  [flip_y_near(): return lax.ppermute(values, ('row', 'col'), pairs)]
    pallas_call x3, Pallas kernels: 33.6 us -> 45.7 us  [run_up(): pl.pallas_call(lambda *refs: up_kernel(len(acts), *refs), grid=(width //...]
    ppermute x75 -> x54, waiting for transfers between devices: 427 us -> 438 us  [flip(): return lax.ppermute(values, axis, [(i, i ^ bit) for i in range(SIDE)])]
  transfers between devices with their start and end apart: 140 -> 91, of which waited for: 58 -> 46; matrix products, arithmetic and copies ran while one was open for 8% -> 9% of each run, Pallas kernels for 18% -> 20%
where the time goes in v3:
time: 1070 us
  waiting for transfers between devices  526 us (49%)
  Pallas kernels  279 us (26%)
  starting transfers between devices  97.9 us (9%)
  other arithmetic  87.9 us (8%)
  local copies, waits for them, and re-layouts  68.5 us (6%)
    ppermute x54, waiting for transfers between devices, flip(): return lax.ppermute(values, axis, [(i, i ^ bit) for i in range(SIDE)])  438 us
    ppermute x54, starting transfers between devices, flip(): return lax.ppermute(values, axis, [(i, i ^ bit) for i in range(SIDE)])  53.6 us
    pallas_call x3, Pallas kernels, run_up(): pl.pallas_call(lambda *refs: up_kernel(len(acts), *refs), grid=(width //...  45.7 us
    unnamed x268, local copies, waits for them, and re-layouts  41.1 us
    pallas_call x1, Pallas kernels, run_backward(): pl.pallas_call(attention_backward, out_shape=[jax.ShapeDtypeStruct((3, 4,...  40.8 us
    all_to_all x2, waiting for transfers between devices, to_tokens(): lax.all_to_all(values, 'row', split_axis=0, concat_axis=1, tiled=True)  32.7 us
    pallas_call x3, Pallas kernels, run_normed_two(): pl.pallas_call(lambda *refs: normed_two_kernel(kind, *refs), grid=(2,), o...  32.4 us
    pallas_call x1, Pallas kernels, run_forward(): pl.pallas_call(attention_forward, out_shape=out_shape, in_specs=[SMEM_SPE...  30.3 us
  transfers between devices with their start and end apart: 91, of which 46 were waited for; matrix products, arithmetic and copies ran while one was open for 9% of the time, Pallas kernels for 20%

profile of v3, /device:TPU:0, one launch (start us, length us, event | category | flops | bytes accessed | tf_op | source)
XLA Modules:
  0.0 1065.1 jit_solution(629302701011508736)
XLA Ops:
  63.7 34.4 %collective-permute-done.3.refs_2_ = bf16[256,2048]{1,0:T(8,128)(2,1)} collective-permute-done((bf16[256,2048]{1,0:T(8,128)(2,1)S(1)}, bf16[256,2048]{1,0:T(8,128)(2,1)}, u32[]{:S(2)}, u32[]{:S(2)}) %collective-permute-start.3) | collective-permute-done | bytes 1048608 | tf_op jit(solution)/shard_map/ppermute | solution.py:353
  108.4 20.0 %collective-permute-done.4.refs_3_ = bf16[256,2048]{1,0:T(8,128)(2,1)} collective-permute-done((bf16[256,2048]{1,0:T(8,128)(2,1)}, bf16[256,2048]{1,0:T(8,128)(2,1)}, u32[]{:S(2)}, u32[]{:S(2)}) %collective-permute-start.4) | collective-permute-done | bytes 1048608 | tf_op jit(solution)/shard_map/ppermute | solution.py:353
  129.2 12.1 %shard_map.186 = (bf16[3,4,256,128]{3,2,1,0:T(8,128)(2,1)S(1)}, bf16[3,4,256,128]{3,2,1,0:T(8,128)(2,1)S(1)}, bf16[3,4,256,128]{3,2,1,0:T(8,128)(2,1)}, bf16[3,4,256,128]{3,2,1,0:T(8,128)(2,1)}) custom-call(s32[16]{0:T(128)S(1)} %fusion.36.place_ref, bf16[256,2048]{1,0:T(8,128)(2,1)S(1)} %fusion.14.refs_0_, bf16[256,2048]{1,0:T(8,128)(2,1)S(1)} %copy-done.53, ...), custom_call_target="tpu_custom_call" | custom-call | flops 6442450944 | bytes 20971520 | tf_op jit(solution)/shard_map/pallas_call | solution.py:617
  158.4 25.2 %all-to-all-done.2 = bf16[4,256,512]{2,1,0:T(8,128)(2,1)} async-done(((bf16[4,256,512]{2,1,0:T(8,128)(2,1)}), bf16[4,256,512]{2,1,0:T(8,128)(2,1)}, u32[]{:S(2)}, u32[]{:S(2)}) %all-to-all-start.2) | async-done | bytes 1048608 | tf_op jit(solution)/shard_map/all_to_all | solution.py:1179
  202.7 30.3 %shard_map.187 = (bf16[4,256,128]{2,1,0:T(8,128)(2,1)S(1)}, bf16[4,256,128]{2,1,0:T(8,128)(2,1)S(1)}, bf16[4,256,128]{2,1,0:T(8,128)(2,1)S(1)}, bf16[4,256,128]{...) custom-call(s32[16]{0:T(128)S(1)} %fusion.36.place_ref, s32[8]{0:T(128)S(1)} %convert_reduce_fusion.1.starts_ref, ...), custom_call_target="tpu_custom_call" | custom-call | flops 8589934592 | bytes 8388608 | tf_op jit(solution)/shard_map/pallas_call | solution.py:1134
  268.0 24.3 %collective-permute-done.21 = bf16[256,2048]{1,0:T(8,128)(2,1)S(1)} collective-permute-done((bf16[256,2048]{1,0:T(8,128)(2,1)S(1)}, bf16[256,2048]{1,0:T(8,128)(2,1)S(1)}, u32[]{:S(2)}, u32[]{:S(2)}) %collective-permute-start.21) | collective-permute-done | bytes 1048608 | tf_op jit(solution)/shard_map/ppermute | solution.py:353
  295.4 21.6 %collective-permute-done.22 = bf16[256,2048]{1,0:T(8,128)(2,1)S(1)} collective-permute-done((bf16[256,2048]{1,0:T(8,128)(2,1)S(1)}, bf16[256,2048]{1,0:T(8,128)(2,1)S(1)}, u32[]{:S(2)}, u32[]{:S(2)}) %collective-permute-start.22) | collective-permute-done | bytes 1048608 | tf_op jit(solution)/shard_map/ppermute | solution.py:353
  317.1 23.9 %collective-permute-done.23 = bf16[256,2048]{1,0:T(8,128)(2,1)S(1)} collective-permute-done((bf16[256,2048]{1,0:T(8,128)(2,1)S(1)}, bf16[256,2048]{1,0:T(8,128)(2,1)S(1)}, u32[]{:S(2)}, u32[]{:S(2)}) %collective-permute-start.23) | collective-permute-done | bytes 1048608 | tf_op jit(solution)/shard_map/ppermute | solution.py:353
  362.7 29.0 %collective-permute-done.32 = bf16[512,1024]{1,0:T(8,128)(2,1)S(1)} collective-permute-done((bf16[512,1024]{1,0:T(8,128)(2,1)S(1)}, bf16[512,1024]{1,0:T(8,128)(2,1)S(1)}, u32[]{:S(2)}, u32[]{:S(2)}) %collective-permute-start.32) | collective-permute-done | bytes 1048608 | tf_op jit(solution)/shard_map/ppermute | solution.py:353
  395.2 25.3 %shard_map.190 = (f32[4,512,512]{2,1,0:T(8,128)}, f32[4,512,512]{2,1,0:T(8,128)}, bf16[4,512,512]{2,1,0:T(8,128)(2,1)S(1)}) custom-call(bf16[256,2048]{1,0:T(8,128)(2,1)S(1)} %collective-permute-done.28.refs_0_.refs_1_, bf16[256,2048]{1,0:T(8,128)(2,1)S(1)} %collective-permute-done.29.refs_1_.refs_2_, bf16[4,1024,512]{2,1,0:T(8,128)(2,1)} %copy-done.75, ...), custom_call_target="tpu_custom_call" | custom-call | flops 8589934592 | bytes 16777216 | tf_op jit(solution)/shard_map/pallas_call | solution.py:738
  516.0 11.7 %shard_map.196 = (bf16[4,512,512]{2,1,0:T(8,128)(2,1)S(1)}, bf16[4,512,512]{2,1,0:T(8,128)(2,1)S(1)}) custom-call(bf16[256,2048]{1,0:T(8,128)(2,1)S(1)} %collective-permute-done.41.refs_0_.refs_4_, bf16[256,2048]{1,0:T(8,128)(2,1)} %collective-permute-done.42.refs_1_.refs_5_, f32[4,512,512]{2,1,0:T(8,128)} %get-tuple-element.257.refs_2_, ...), custom_call_target="tpu_custom_call" | custom-call | flops 4294967296 | bytes 16777216 | tf_op jit(solution)/shard_map/pallas_call | solution.py:797
  549.5 13.9 %shard_map.199 = (f32[128,2048]{1,0:T(8,128)S(1)}, bf16[128,2048]{1,0:T(8,128)(2,1)S(1)}, bf16[128,2048]{1,0:T(8,128)(2,1)S(1)}, f32[128,2048]{1,0:T(8,128)S(1)}) custom-call(bf16[4,512,512]{2,1,0:T(8,128)(2,1)S(1)} %copy-done.50, bf16[4,512,512]{2,1,0:T(8,128)(2,1)} %copy-done.47, bf16[4,1024,512]{2,1,0:T(8,128)(2,1)} %copy-done.75, ...), custom_call_target="tpu_custom_call" | custom-call | flops 8589934592 | bytes 18874368 | tf_op jit(solution)/shard_map/pallas_call | solution.py:836
  569.0 15.4 %shard_map.200 = (bf16[2,2,512,1024]{3,2,1,0:T(8,128)(2,1)S(1)}, bf16[2,2,512,1024]{3,2,1,0:T(8,128)(2,1)}) custom-call(bf16[4,256,512]{2,1,0:T(8,128)(2,1)S(1)} %copy-done.32, bf16[4,512,512]{2,1,0:T(8,128)(2,1)S(1)} %copy-done.70, bf16[4,256,512]{2,1,0:T(8,128)(2,1)S(1)} %copy-done.20, bf16[256,2048]{1,0:T(8,128)(2,1)S(1)} %fusion.13.refs_0_.refs_3_, ...), custom_call_target="tpu_custom_call" | custom-call | flops 8589934592 | bytes 16777216 | tf_op jit(solution)/shard_map/pallas_call | solution.py:912
  634.7 42.2 %collective-permute-done.52.refs_2_ = bf16[256,2048]{1,0:T(8,128)(2,1)S(1)} collective-permute-done((bf16[256,2048]{1,0:T(8,128)(2,1)S(1)}, bf16[256,2048]{1,0:T(8,128)(2,1)S(1)}, u32[]{:S(2)}, u32[]{:S(2)}) %collective-permute-start.52) | collective-permute-done | bytes 1048608 | tf_op jit(solution)/shard_map/ppermute | solution.py:353
  680.8 12.1 %shard_map.203 = (bf16[2,2,1024,512]{3,2,1,0:T(8,128)(2,1)S(1)}, bf16[2,2,1024,512]{3,2,1,0:T(8,128)(2,1)}) custom-call(bf16[256,2048]{1,0:T(8,128)(2,1)S(1)} %get-tuple-element.413.refs_0_, bf16[256,2048]{1,0:T(8,128)(2,1)S(1)} %copy-done.44, bf16[256,2048]{1,0:T(8,128)(2,1)S(1)} %copy-done.46, bf16[128,2048]{1,0:T(8,128)(2,1)S(1)} %copy-done.34, ...), custom_call_target="tpu_custom_call" | custom-call | flops 8589934592 | bytes 16777216 | tf_op jit(solution)/shard_map/pallas_call | solution.py:873
  728.6 22.2 %collective-permute-done.59.refs_5_ = bf16[4,256,128]{2,1,0:T(8,128)(2,1)S(1)} collective-permute-done((bf16[4,256,128]{2,1,0:T(8,128)(2,1)}, bf16[4,256,128]{2,1,0:T(8,128)(2,1)S(1)}, u32[]{:S(2)}, u32[]{:S(2)}) %collective-permute-start.59) | collective-permute-done | bytes 262176 | tf_op jit(solution)/shard_map/ppermute | solution.py:353
  756.0 40.8 %shard_map.206 = (bf16[3,4,256,128]{3,2,1,0:T(8,128)(2,1)S(1)}, bf16[3,4,256,128]{3,2,1,0:T(8,128)(2,1)}, bf16[3,4,256,128]{3,2,1,0:T(8,128)(2,1)}, bf16[3,4,256,128]{3,2,1,0:T(8,128)(2,1)}) custom-call(s32[16]{0:T(128)S(1)} %fusion.36.place_ref, s32[8]{0:T(128)S(1)} %convert_reduce_fusion.1.starts_ref, bf16[3,4,256,128]{3,2,1,0:T(8,128)(2,1)} %copy-done.71, ...), custom_call_target="tpu_custom_call" | custom-call | flops 21474836480 | bytes 16777216 | tf_op jit(solution)/shard_map/pallas_call | solution.py:1159
  840.2 12.7 %collective-permute-done.68.refs_6_.refs_2_ = bf16[3,4,256,128]{3,2,1,0:T(8,128)(2,1)} collective-permute-done((bf16[3,4,256,128]{3,2,1,0:T(8,128)(2,1)}, bf16[3,4,256,128]{3,2,1,0:T(8,128)(2,1)}, u32[]{:S(2)}, u32[]{:S(2)}) %collective-permute-start.68) | collective-permute-done | bytes 786464 | tf_op jit(solution)/shard_map/ppermute | solution.py:353
  852.9 14.8 %collective-permute-done.69.refs_7_.refs_3_ = bf16[3,4,256,128]{3,2,1,0:T(8,128)(2,1)} collective-permute-done((bf16[3,4,256,128]{3,2,1,0:T(8,128)(2,1)}, bf16[3,4,256,128]{3,2,1,0:T(8,128)(2,1)}, u32[]{:S(2)}, u32[]{:S(2)}) %collective-permute-start.69) | collective-permute-done | bytes 786464 | tf_op jit(solution)/shard_map/ppermute | solution.py:376
  871.4 12.6 %shard_map.207 = (bf16[2,2,4,1024,128]{4,3,2,1,0:T(8,128)(2,1)}, bf16[2,2,4,1024,128]{4,3,2,1,0:T(8,128)(2,1)}) custom-call(bf16[256,2048]{1,0:T(8,128)(2,1)S(1)} %copy-done.30, bf16[256,2048]{1,0:T(8,128)(2,1)S(1)} %copy-done.54, bf16[256,2048]{1,0:T(8,128)(2,1)} %collective-permute-done.3.refs_2_, bf16[256,2048]{1,0:T(8,128)(2,1)} %collective-permute-done.4.refs_3_, ...), custom_call_target="tpu_custom_call" | custom-call | flops 6442450944 | bytes 12582912 | tf_op jit(solution)/shard_map/pallas_call | solution.py:957
  901.0 19.4 %collective-permute-done.73 = bf16[256,2048]{1,0:T(8,128)(2,1)S(1)} collective-permute-done((bf16[256,2048]{1,0:T(8,128)(2,1)S(1)}, bf16[256,2048]{1,0:T(8,128)(2,1)S(1)}, u32[]{:S(2)}, u32[]{:S(2)}) %collective-permute-start.73) | collective-permute-done | bytes 1048608 | tf_op jit(solution)/shard_map/ppermute | solution.py:353
  928.5 44.2 %collective-permute-done.80 = bf16[1024,512]{1,0:T(8,128)(2,1)S(1)} collective-permute-done((bf16[1024,512]{1,0:T(8,128)(2,1)S(1)}, bf16[1024,512]{1,0:T(8,128)(2,1)S(1)}, u32[]{:S(2)}, u32[]{:S(2)}) %collective-permute-start.80) | collective-permute-done | bytes 1048608 | tf_op jit(solution)/shard_map/ppermute | solution.py:353
  975.5 19.0 %collective-permute-done.75 = bf16[256,2048]{1,0:T(8,128)(2,1)S(1)} collective-permute-done((bf16[256,2048]{1,0:T(8,128)(2,1)S(1)}, bf16[256,2048]{1,0:T(8,128)(2,1)S(1)}, u32[]{:S(2)}, u32[]{:S(2)}) %collective-permute-start.75) | collective-permute-done | bytes 1048608 | tf_op jit(solution)/shard_map/ppermute | solution.py:353
  1003.3 21.6 %collective-permute-done.83 = bf16[2,512,512]{2,1,0:T(8,128)(2,1)S(1)} collective-permute-done((bf16[2,512,512]{2,1,0:T(8,128)(2,1)S(1)}, bf16[2,512,512]{2,1,0:T(8,128)(2,1)S(1)}, u32[]{:S(2)}, u32[]{:S(2)}) %collective-permute-start.83) | collective-permute-done | bytes 1048608 | tf_op jit(solution)/shard_map/ppermute | solution.py:353
  (565 shorter events, 510.4 us)
Async XLA Ops:
  29.0 70.0 %collective-permute-start.5 = (bf16[4,1024,128]{2,1,0:T(8,128)(2,1)}, bf16[4,1024,128]{2,1,0:T(8,128)(2,1)}, u32[]{:S(2)}, u32[]{:S(2)}) collective-permute-start(bf16[4,1024,128]{2,1,0:T(8,128)(2,1)} %maximum_select_fusion.2), channel_id=1, source_target_pairs={{0,24},{4,28},{8,16},{12,20},{16,8},{20,12},{24,0},{28,4},{1,25},{... | collective-permute-start | bytes 3145736 | tf_op jit(solution)/shard_map/ppermute | solution.py:389
  50.3 47.8 %collective-permute-start.3 = (bf16[256,2048]{1,0:T(8,128)(2,1)S(1)}, bf16[256,2048]{1,0:T(8,128)(2,1)}, u32[]{:S(2)}, u32[]{:S(2)}) collective-permute-start(bf16[256,2048]{1,0:T(8,128)(2,1)S(1)} %fusion.14.refs_0_), channel_id=1, source_target_pairs={{0,2},{1,3},{2,0},{3,1},{4,6},{5,7},{6,4},{7,5},{8,10},{9,11},{10,... | collective-permute-start | bytes 3145736 | tf_op jit(solution)/shard_map/ppermute | solution.py:353
  50.8 47.3 %collective-permute-start.2 = (bf16[256,2048]{1,0:T(8,128)(2,1)S(1)}, bf16[256,2048]{1,0:T(8,128)(2,1)S(1)}, u32[]{:S(2)}, u32[]{:S(2)}) collective-permute-start(bf16[256,2048]{1,0:T(8,128)(2,1)S(1)} %fusion.14.refs_0_), channel_id=1, source_target_pairs={{0,4},{4,0},{8,12},{12,8},{1,5},{5,1},{9,13},{13,9},{2,6},{6,2},{1... | collective-permute-start | bytes 3145736 | tf_op jit(solution)/shard_map/ppermute | solution.py:353
  128.4 57.7 %collective-permute-start.14 = (bf16[1024,512]{1,0:T(8,128)(2,1)}, bf16[1024,512]{1,0:T(8,128)(2,1)}, u32[]{:S(2)}, u32[]{:S(2)}) collective-permute-start(bf16[1024,512]{1,0:T(8,128)(2,1)} %maximum_select_fusion.3), channel_id=1, source_target_pairs={{0,24},{4,28},{8,16},{12,20},{16,8},{20,12},{24,0},{28,4},{1,25},{... | collective-permute-start | bytes 3145736 | tf_op jit(solution)/shard_map/ppermute | solution.py:389
  143.2 55.9 %collective-permute-start.12 = (bf16[2,512,512]{2,1,0:T(8,128)(2,1)}, bf16[2,512,512]{2,1,0:T(8,128)(2,1)}, u32[]{:S(2)}, u32[]{:S(2)}) collective-permute-start(bf16[2,512,512]{2,1,0:T(8,128)(2,1)} %pad_maximum_fusion.6), channel_id=1, source_target_pairs={{0,4},{4,0},{8,12},{12,8},{1,5},{5,1},{9,13},{13,9},{2,6},{6,2},{1... | collective-permute-start | bytes 3145736 | tf_op jit(solution)/shard_map/ppermute | solution.py:353
  201.9 47.2 %collective-permute-start.20 = (bf16[1024,512]{1,0:T(8,128)(2,1)S(1)}, bf16[1024,512]{1,0:T(8,128)(2,1)S(1)}, u32[]{:S(2)}, u32[]{:S(2)}) collective-permute-start(bf16[1024,512]{1,0:T(8,128)(2,1)S(1)} %maximum_select_fusion.4), channel_id=1, source_target_pairs={{0,24},{4,28},{8,16},{12,20},{16,8},{20,12},{24,0},{28,4},{1,25},{... | collective-permute-start | bytes 3145736 | tf_op jit(solution)/shard_map/ppermute | solution.py:389
  260.6 81.1 %collective-permute-start.25 = (bf16[4,1024,512]{2,1,0:T(8,128)(2,1)S(1)}, bf16[4,1024,512]{2,1,0:T(8,128)(2,1)}, u32[]{:S(2)}, u32[]{:S(2)}) collective-permute-start(bf16[4,1024,512]{2,1,0:T(8,128)(2,1)S(1)} %pad_maximum_fusion.1.refs_1_.refs_2_), channel_id=1, source_target_pairs={{0,16},{16,0},{1,17},{17,1},{2,18},{18,2},{3,19},{19,3},{4,20},{20... | collective-permute-start | bytes 12582920 | tf_op jit(solution)/shard_map/ppermute | solution.py:384
  292.9 48.0 %collective-permute-start.23 = (bf16[256,2048]{1,0:T(8,128)(2,1)S(1)}, bf16[256,2048]{1,0:T(8,128)(2,1)S(1)}, u32[]{:S(2)}, u32[]{:S(2)}) collective-permute-start(bf16[256,2048]{1,0:T(8,128)(2,1)S(1)} %add_convert_fusion.10), channel_id=1, source_target_pairs={{0,2},{1,3},{2,0},{3,1},{4,6},{5,7},{6,4},{7,5},{8,10},{9,11},{10,... | collective-permute-start | bytes 3145736 | tf_op jit(solution)/shard_map/ppermute | solution.py:353
  294.0 47.7 %collective-permute-start.26 = (bf16[512,1024]{1,0:T(8,128)(2,1)S(1)}, bf16[512,1024]{1,0:T(8,128)(2,1)S(1)}, u32[]{:S(2)}, u32[]{:S(2)}) collective-permute-start(bf16[512,1024]{1,0:T(8,128)(2,1)S(1)} %maximum_select_fusion.6), channel_id=1, source_target_pairs={{0,24},{4,28},{8,16},{12,20},{16,8},{20,12},{24,0},{28,4},{1,25},{... | collective-permute-start | bytes 3145736 | tf_op jit(solution)/shard_map/ppermute | solution.py:389
  344.1 47.6 %collective-permute-start.32 = (bf16[512,1024]{1,0:T(8,128)(2,1)S(1)}, bf16[512,1024]{1,0:T(8,128)(2,1)S(1)}, u32[]{:S(2)}, u32[]{:S(2)}) collective-permute-start(bf16[512,1024]{1,0:T(8,128)(2,1)S(1)} %maximum_select_fusion.6), channel_id=1, source_target_pairs={{0,2},{1,3},{2,0},{3,1},{4,6},{5,7},{6,4},{7,5},{8,10},{9,11},{10,... | collective-permute-start | bytes 3145736 | tf_op jit(solution)/shard_map/ppermute | solution.py:353
  344.2 47.5 %collective-permute-start.28 = (bf16[256,2048]{1,0:T(8,128)(2,1)S(1)}, bf16[256,2048]{1,0:T(8,128)(2,1)S(1)}, u32[]{:S(2)}, u32[]{:S(2)}) collective-permute-start(bf16[256,2048]{1,0:T(8,128)(2,1)S(1)} %get-tuple-element.413.refs_0_), channel_id=1, source_target_pairs={{0,4},{4,0},{8,12},{12,8},{1,5},{5,1},{9,13},{13,9},{2,6},{6,2},{1... | collective-permute-start | bytes 3145736 | tf_op jit(solution)/shard_map/ppermute | solution.py:353
  345.9 47.6 %collective-permute-start.29 = (bf16[256,2048]{1,0:T(8,128)(2,1)S(1)}, bf16[256,2048]{1,0:T(8,128)(2,1)S(1)}, u32[]{:S(2)}, u32[]{:S(2)}) collective-permute-start(bf16[256,2048]{1,0:T(8,128)(2,1)S(1)} %get-tuple-element.413.refs_0_), channel_id=1, source_target_pairs={{0,1},{1,0},{2,3},{3,2},{4,5},{5,4},{6,7},{7,6},{8,9},{9,8},{10,11... | collective-permute-start | bytes 3145736 | tf_op jit(solution)/shard_map/ppermute | solution.py:353
  627.8 50.6 %collective-permute-start.57 = (bf16[2,2,1024,512]{3,2,1,0:T(8,128)(2,1)S(1)}, bf16[2,2,1024,512]{3,2,1,0:T(8,128)(2,1)S(1)}, u32[]{:S(2)}, u32[]{:S(2)}) collective-permute-start(bf16[2,2,1024,512]{3,2,1,0:T(8,128)(2,1)S(1)} %get-tuple-element.295), channel_id=1, source_target_pairs={{0,16},{16,0},{1,17},{17,1},{2,18},{18,2},{3,19},{19,3},{4,20},{20... | collective-permute-start | bytes 12582920 | tf_op jit(solution)/shard_map/ppermute | solution.py:384
  627.9 48.9 %collective-permute-start.52 = (bf16[256,2048]{1,0:T(8,128)(2,1)S(1)}, bf16[256,2048]{1,0:T(8,128)(2,1)S(1)}, u32[]{:S(2)}, u32[]{:S(2)}) collective-permute-start(bf16[256,2048]{1,0:T(8,128)(2,1)S(1)} %get-tuple-element.306.refs_0_), channel_id=1, source_target_pairs={{0,2},{1,3},{2,0},{3,1},{4,6},{5,7},{6,4},{7,5},{8,10},{9,11},{10,... | collective-permute-start | bytes 3145736 | tf_op jit(solution)/shard_map/ppermute | solution.py:353
  633.2 47.5 %collective-permute-start.51 = (bf16[256,2048]{1,0:T(8,128)(2,1)S(1)}, bf16[256,2048]{1,0:T(8,128)(2,1)S(1)}, u32[]{:S(2)}, u32[]{:S(2)}) collective-permute-start(bf16[256,2048]{1,0:T(8,128)(2,1)S(1)} %get-tuple-element.306.refs_0_), channel_id=1, source_target_pairs={{0,4},{4,0},{8,12},{12,8},{1,5},{5,1},{9,13},{13,9},{2,6},{6,2},{1... | collective-permute-start | bytes 3145736 | tf_op jit(solution)/shard_map/ppermute | solution.py:353
  750.8 47.9 %collective-permute-start.64 = (bf16[512,1024]{1,0:T(8,128)(2,1)S(1)}, bf16[512,1024]{1,0:T(8,128)(2,1)S(1)}, u32[]{:S(2)}, u32[]{:S(2)}) collective-permute-start(bf16[512,1024]{1,0:T(8,128)(2,1)S(1)} %fusion.12), channel_id=1, source_target_pairs={{0,2},{1,3},{2,0},{3,1},{4,6},{5,7},{6,4},{7,5},{8,10},{9,11},{10,... | collective-permute-start | bytes 3145736 | tf_op jit(solution)/shard_map/ppermute | solution.py:353
  754.2 47.4 %collective-permute-start.65 = (bf16[1024,512]{1,0:T(8,128)(2,1)S(1)}, bf16[1024,512]{1,0:T(8,128)(2,1)S(1)}, u32[]{:S(2)}, u32[]{:S(2)}) collective-permute-start(bf16[1024,512]{1,0:T(8,128)(2,1)S(1)} %get-tuple-element.325), channel_id=1, source_target_pairs={{0,24},{4,28},{8,16},{12,20},{16,8},{20,12},{24,0},{28,4},{1,25},{... | collective-permute-start | bytes 3145736 | tf_op jit(solution)/shard_map/ppermute | solution.py:389
  801.6 66.2 %collective-permute-start.71 = (bf16[1024,512]{1,0:T(8,128)(2,1)}, bf16[1024,512]{1,0:T(8,128)(2,1)}, u32[]{:S(2)}, u32[]{:S(2)}) collective-permute-start(bf16[1024,512]{1,0:T(8,128)(2,1)} %fusion.9), channel_id=1, source_target_pairs={{0,2},{1,3},{2,0},{3,1},{4,6},{5,7},{6,4},{7,5},{8,10},{9,11},{10,... | collective-permute-start | bytes 3145736 | tf_op jit(solution)/shard_map/ppermute | solution.py:353
  811.6 56.2 %collective-permute-start.69 = (bf16[3,4,256,128]{3,2,1,0:T(8,128)(2,1)}, bf16[3,4,256,128]{3,2,1,0:T(8,128)(2,1)}, u32[]{:S(2)}, u32[]{:S(2)}) collective-permute-start(bf16[3,4,256,128]{3,2,1,0:T(8,128)(2,1)} %get-tuple-element.330), channel_id=1, source_target_pairs={{0,9},{1,8},{2,11},{3,10},{4,13},{5,12},{6,15},{7,14},{8,1},{9,0},... | collective-permute-start | bytes 2359304 | tf_op jit(solution)/shard_map/ppermute | solution.py:376
  900.7 72.0 %collective-permute-start.80 = (bf16[1024,512]{1,0:T(8,128)(2,1)S(1)}, bf16[1024,512]{1,0:T(8,128)(2,1)S(1)}, u32[]{:S(2)}, u32[]{:S(2)}) collective-permute-start(bf16[1024,512]{1,0:T(8,128)(2,1)S(1)} %fusion.7), channel_id=1, source_target_pairs={{0,2},{1,3},{2,0},{3,1},{4,6},{5,7},{6,4},{7,5},{8,10},{9,11},{10,... | collective-permute-start | bytes 3145736 | tf_op jit(solution)/shard_map/ppermute | solution.py:353
  920.5 55.0 %collective-permute-start.74 = (bf16[256,2048]{1,0:T(8,128)(2,1)S(1)}, bf16[256,2048]{1,0:T(8,128)(2,1)S(1)}, u32[]{:S(2)}, u32[]{:S(2)}) collective-permute-start(bf16[256,2048]{1,0:T(8,128)(2,1)S(1)} %get-tuple-element.350), channel_id=1, source_target_pairs={{0,4},{4,0},{8,12},{12,8},{1,5},{5,1},{9,13},{13,9},{2,6},{6,2},{1... | collective-permute-start | bytes 3145736 | tf_op jit(solution)/shard_map/ppermute | solution.py:353
  921.2 73.3 %collective-permute-start.75 = (bf16[256,2048]{1,0:T(8,128)(2,1)S(1)}, bf16[256,2048]{1,0:T(8,128)(2,1)S(1)}, u32[]{:S(2)}, u32[]{:S(2)}) collective-permute-start(bf16[256,2048]{1,0:T(8,128)(2,1)S(1)} %add_convert_fusion.3), channel_id=1, source_target_pairs={{0,2},{1,3},{2,0},{3,1},{4,6},{5,7},{6,4},{7,5},{8,10},{9,11},{10,... | collective-permute-start | bytes 3145736 | tf_op jit(solution)/shard_map/ppermute | solution.py:353
  925.5 69.4 %collective-permute-start.79 = (bf16[2,512,512]{2,1,0:T(8,128)(2,1)S(1)}, bf16[2,512,512]{2,1,0:T(8,128)(2,1)S(1)}, u32[]{:S(2)}, u32[]{:S(2)}) collective-permute-start(bf16[2,512,512]{2,1,0:T(8,128)(2,1)S(1)} %maximum_select_fusion.11), channel_id=1, source_target_pairs={{0,16},{16,0},{1,17},{17,1},{2,18},{18,2},{3,19},{19,3},{4,20},{20... | collective-permute-start | bytes 3145736 | tf_op jit(solution)/shard_map/ppermute | solution.py:384
  926.0 70.4 %collective-permute-start.78 = (bf16[4,1024,128]{2,1,0:T(8,128)(2,1)S(1)}, bf16[4,1024,128]{2,1,0:T(8,128)(2,1)S(1)}, u32[]{:S(2)}, u32[]{:S(2)}) collective-permute-start(bf16[4,1024,128]{2,1,0:T(8,128)(2,1)S(1)} %fusion.8), channel_id=1, source_target_pairs={{0,1},{1,0},{2,3},{3,2},{4,5},{5,4},{6,7},{7,6},{8,9},{9,8},{10,11... | collective-permute-start | bytes 3145736 | tf_op jit(solution)/shard_map/ppermute | solution.py:353
  (199 other events, 3401.5 us)

commit v4 on v3

--- a/solution.py
+++ b/solution.py
@@ -429,8 +429,9 @@
     return [block, by_x, by_z, flip_x(after(by_z, *events) if events else by_z)]
 
 
-def square_reduce(far, by_x, by_z, own):
+def square_reduce(far, by_x, by_z, own, *events):
     got_far = flip_x(far)
+    got_far = after(got_far, *events) if events else got_far
     got_x = flip_x(after(by_x, got_far))
     got_z = flip_far((by_z + wide(got_far)).astype(BF))
     return own + wide(got_x) + wide(got_z)
@@ -1230,31 +1231,54 @@
     cos_wide, sin_wide = jnp.cos(angles), jnp.sin(angles) * sign[None, :]
 
     heads_x = flip_x(head_cut(1 - x))
-    count = exchanged_sum(jnp.sum(valid.astype(F32)), ("dp", "col"), 2 * SIDE)
-    heads_x = after(heads_x, count)
     gates_x = flip_x(after(cut(gate_weight, 1 - x, 1), heads_x))
-    hidden = swap_y(to_tokens(after(hidden_in, heads_x))).astype(F32)
+    rows_y = hidden_in.shape[0] // 2
+    kept = lax.dynamic_slice_in_dim(hidden_in, y * rows_y, rows_y, 0)
+    sent = lax.dynamic_slice_in_dim(hidden_in, (1 - y) * rows_y, rows_y, 0)
+    piece_here = jnp.concatenate((kept, flip_y(sent)), axis=1)
+    piece_far = flip_far(piece_here)
+    piece_x = flip_x(after(piece_here, heads_x))
+    piece_far_x = flip_x(piece_far)
+
+    count = after(jnp.sum(valid.astype(F32)), piece_here)
+    count = exchanged_sum(count, ("dp", "col"), 2 * SIDE)
+    target = to_tokens(after(teacher, piece_x))
+
+    def whole_rows(own, other):
+        width = own.shape[1] // 2
+        first, second = jnp.where(x == 0, own, other), jnp.where(x == 0, other, own)
+        return jnp.concatenate(
+            (first[:, :width], second[:, :width], first[:, width:], second[:, width:]), axis=1
+        )
+
+    def own_and_x(rows):
+        half = rows.shape[0] // 2
+        return [lax.dynamic_slice_in_dim(rows, at * half, half, 0) for at in (x, 1 - x)]
+
+    hidden_rows = whole_rows(piece_here, piece_x)
+    hidden = own_and_x(hidden_rows)[0].astype(F32)
+    acts_here = own_and_x(local_norm(hidden_rows.astype(F32))[0].astype(BF))
+    far_rows = whole_rows(piece_far, piece_far_x)
+    acts_far = own_and_x(local_norm(far_rows.astype(F32))[0].astype(BF))
+    normed_acts = acts_here + acts_far
     heads_tall = ordered(x, head_cut(x), heads_x, 1)
     heads_high = flip_near(heads_tall)
     heads_y = flip_dp_y(heads_tall)
-    normed, inverse_one = local_norm(after(hidden, gates_x))
-    low_normed = normed.astype(BF)
-    normed_acts = square_gather(low_normed)
-    heads_y_high = flip_dp_y(after(heads_high, low_normed))
+    normed, inverse_one = local_norm(hidden)
+    heads_y_high = flip_dp_y(after(heads_high, piece_x, count))
     gates_tall = ordered(x, cut(gate_weight, x, 1), gates_x, 0)
-    gates_high = flip_far(after(gates_tall, heads_high, normed_acts[1:3]))
+    gates_high = flip_far(after(gates_tall, heads_high, piece_far))
     cos_wide, sin_wide = after((cos_wide, sin_wide), heads_tall)
     heads = both_cores(
-        heads_tall, heads_y, heads_high, after(heads_y_high, normed_acts[1:3], cos_wide, sin_wide)
-    )
-    gates_y = flip_dp_y(after(gates_tall, normed_acts))
+        heads_tall, heads_y, heads_high, after(heads_y_high, piece_far, target, cos_wide, sin_wide)
+    )
+    gates_y = flip_dp_y(after(gates_tall, piece_far_x))
 
     messages = run_qkv(pieces, normed_acts, heads, cos_wide, sin_wide)
     mlp_x = jnp.stack((cut(up_weight, 1 - x, 1), cut(down_weight, 1 - x, 0)))
     mlp_x = flip_x(after(mlp_x, messages[0]))
-    target = to_tokens(after(teacher, messages[0]))
     messages = swap_slots(messages)
-    messages = after(messages, mlp_x, gates_high, gates_y, target)
+    messages = after(messages, mlp_x, gates_high, gates_y)
 
     ups_tall = ordered(x, cut(up_weight, x, 1), after(mlp_x[0], messages), 0)
     ups_high = flip_far(after(ups_tall, gates_high))
@@ -1319,13 +1343,14 @@
     down_y1 = down_grads.to_y(1)
     middle_grad = out_grad + local_norm_backward(normed_two_grad, normed_two, inverse_two)
     low_middle = middle_grad.astype(BF)
+    layer_output = to_width(swap_y(after(output, low_middle).astype(BF)))
     gate_core = gate_grads.to_core(low_middle)
     down_y0 = down_grads.to_y(0, low_middle)
     up_pair = run_wide_grad(two_acts, after([low[1] for low in lows], gate_pair))
     up_grads = Spread(up_pair)
     middle_acts = square_gather(low_middle, gate_pair, down_y1)
     gate_y1 = gate_grads.to_y(1, down_y0, middle_acts[1:3])
-    middle_acts = after(middle_acts, up_pair, down_y0, gate_y1)
+    middle_acts = after(middle_acts, up_pair, down_y0, gate_y1, layer_output)
     grad_messages = run_attended_grad(middle_acts, heads)
     up_core = up_grads.to_core(grad_messages)
     gate_y0 = gate_grads.to_y(0, gate_y1)
@@ -1333,7 +1358,6 @@
     out_pair = run_head_grad(1, after(middle_acts, grad_messages), mixed)
     grad_messages = swap_slots(grad_messages)
     grad_messages = after(grad_messages, up_core, out_pair, gate_y0)
-    layer_output = to_width(swap_y(after(output, grad_messages).astype(BF)))
     up_y0 = up_grads.to_y(0, grad_messages)
     up_y1 = up_grads.to_y(1, grad_messages)
     back = run_backward(
@@ -1344,40 +1368,41 @@
     own_down, send_down = to_x(down_grads.total(back), x, 1)
     down_x = flip_x(send_down)
     back = swap_slots(back)
-    back = after(back, down_x, gate_grads.high, layer_output)
+    back = after(back, down_x, gate_grads.high)
     up_grads.to_high(flip_far, back)
+    own_gate, send_gate = to_x(gate_grads.total(back), x, 0)
+    gate_x = flip_x(send_gate)
     head_pair = run_head_grad(3, normed_acts, back, out_pair)
     head_grads = Spread(head_pair)
     head_core = head_grads.to_core()
     input_sums = run_input(after(back, head_pair), heads)
     input_sums = after(input_sums, head_core)
     head_y1 = head_grads.to_y(1)
-    normed_grad = square_reduce(*input_sums)
+    normed_grad = square_reduce(*input_sums, up_grads.high)
     head_y0 = head_grads.to_y(0, head_y1)
     head_grads.to_high(flip_near, head_y1)
-    down_mine = pair_up(own_down, down_x, x)
-    down_theirs = flip_dp(after(down_mine, input_sums))
-    normed_grad = after(normed_grad, head_y0, head_grads.high, down_theirs, up_grads.high)
+    first_mine = jnp.stack((pair_up(own_gate, gate_x, x), pair_up(own_down, down_x, x)))
+    first_theirs = flip_dp(after(first_mine, head_y1))
+    normed_grad = after(normed_grad, head_y0, head_grads.high, first_theirs)
     input_gradient = middle_grad + local_norm_backward(normed_grad, normed, inverse_one)
     own_head, send_head = to_x(head_grads.total(normed_grad), x, 1)
-    own_gate, send_gate = to_x(gate_grads.total(input_sums), x, 0)
     own_up, send_up = to_x(up_grads.total(normed_grad), x, 0)
     head_x = flip_x(send_head)
-    last_x = flip_x(jnp.stack((send_gate, send_up)))
-    last_mine = jnp.stack((pair_up(own_gate, last_x[0], x), pair_up(own_up, last_x[1], x)))
-    last_theirs = flip_dp(last_mine)
+    last_mine = pair_up(own_up, flip_x(send_up), x)
+    input_out = to_width(swap_y(input_gradient.astype(BF)))
+    last_theirs = flip_dp(after(last_mine, input_out))
     head_mine = pair_up(own_head, head_x, x)
     head_theirs = flip_dp(head_mine)
     mean_loss = loss / total_count
 
-    gate_grad = unite(last_mine[0], last_theirs[0], q, 1)
-    down_grad = unite(down_mine, down_theirs, q, 0)
-    up_grad = unite(last_mine[1], last_theirs[1], q, 1)
+    gate_grad = unite(first_mine[0], first_theirs[0], q, 1)
+    down_grad = unite(first_mine[1], first_theirs[1], q, 0)
+    up_grad = unite(last_mine, last_theirs, q, 1)
     head_grads = unite(head_mine, head_theirs, q, 2)
     return (
         layer_output,
         mean_loss,
-        to_width(swap_y(input_gradient.astype(BF))).astype(F32),
+        input_out.astype(F32),
         head_grads[0],
         head_grads[1],
         head_grads[2],

time: 1070 us -> 1040 us (0.972)
  waiting for transfers between devices: 526 us -> 479 us
  other arithmetic: 87.9 us -> 112 us
  Pallas kernels: 279 us -> 265 us
    ppermute x54 -> x56, waiting for transfers between devices: 438 us -> 369 us  [flip(): return lax.ppermute(values, axis, [(i, i ^ bit) for i in range(SIDE)])]
    ppermute x4, waiting for transfers between devices: 26.5 us -> 42.3 us  [flip_y_near(): return lax.ppermute(values, ('row', 'col'), pairs)]
    all_to_all x2 -> x1, waiting for transfers between devices: 32.7 us -> 24.7 us  [to_tokens(): lax.all_to_all(values, 'row', split_axis=0, concat_axis=1, tiled=True)]
    ppermute x54 -> x56, starting transfers between devices: 53.6 us -> 58.9 us  [flip(): return lax.ppermute(values, axis, [(i, i ^ bit) for i in range(SIDE)])]
    unnamed x268 -> x292, local copies, waits for them, and re-layouts: 41.1 us -> 44.6 us
  transfers between devices with their start and end apart: 91 -> 92, of which waited for: 46 -> 41; matrix products, arithmetic and copies ran while one was open for 9% -> 12% of each run, Pallas kernels for 20% -> 19%
where the time goes in v4:
time: 1040 us; the launch traced here: 1030 us
  waiting for transfers between devices  479 us (46%)
  Pallas kernels  265 us (25%)
  other arithmetic  112 us (11%)
  starting transfers between devices  98.6 us (9%)
  local copies, waits for them, and re-layouts  69.3 us (7%)
    ppermute x56, waiting for transfers between devices, flip(): return lax.ppermute(values, axis, [(i, i ^ bit) for i in range(SIDE)])  369 us
    ppermute x56, starting transfers between devices, flip(): return lax.ppermute(values, axis, [(i, i ^ bit) for i in range(SIDE)])  58.9 us
    unnamed x292, local copies, waits for them, and re-layouts  44.6 us
    ppermute x4, waiting for transfers between devices, flip_y_near(): return lax.ppermute(values, ('row', 'col'), pairs)  42.3 us
    pallas_call x1, Pallas kernels, run_backward(): pl.pallas_call(attention_backward, out_shape=[jax.ShapeDtypeStruct((3, 4,...  40.6 us
    pallas_call x3, Pallas kernels, run_up(): pl.pallas_call(lambda *refs: up_kernel(len(acts), *refs), grid=(width //...  35.1 us
    pallas_call x3, Pallas kernels, run_normed_two(): pl.pallas_call(lambda *refs: normed_two_kernel(kind, *refs), grid=(2,), o...  32.9 us
    pallas_call x1, Pallas kernels, run_forward(): pl.pallas_call(attention_forward, out_shape=out_shape, in_specs=[SMEM_SPE...  30 us
  transfers between devices with their start and end apart: 92, of which 41 were waited for; matrix products, arithmetic and copies ran while one was open for 12% of the time, Pallas kernels for 19%

profile of v4, /device:TPU:0, one launch (start us, length us, event | category | flops | bytes accessed | tf_op | source)
XLA Modules:
  0.0 1029.4 jit_solution(11631709048956369046)
XLA Ops:
  39.5 14.9 %all-to-all-done = f32[8,8,128]{2,1,0:T(8,128)S(1)} async-done(((f32[8,8,128]{2,1,0:T(8,128)}), f32[8,8,128]{2,1,0:T(8,128)S(1)}, u32[]{:S(2)}, u32[]{:S(2)}) %all-to-all-start) | async-done | bytes 32800 | tf_op jit(solution)/shard_map/all_to_all | solution.py:510
  73.2 24.7 %all-to-all-done.1 = bf16[4,256,512]{2,1,0:T(8,128)(2,1)} async-done(((bf16[4,256,512]{2,1,0:T(8,128)(2,1)}), bf16[4,256,512]{2,1,0:T(8,128)(2,1)}, u32[]{:S(2)}, u32[]{:S(2)}) %all-to-all-start.1) | async-done | bytes 1048608 | tf_op jit(solution)/shard_map/all_to_all | solution.py:1180
  110.0 21.8 %collective-permute-done.4 = bf16[512,1024]{1,0:T(8,128)(2,1)S(1)} collective-permute-done((bf16[512,1024]{1,0:T(8,128)(2,1)}, bf16[512,1024]{1,0:T(8,128)(2,1)S(1)}, u32[]{:S(2)}, u32[]{:S(2)}) %collective-permute-start.4) | collective-permute-done | bytes 1048608 | tf_op jit(solution)/shard_map/ppermute | solution.py:353
  158.4 13.3 %collective-permute-done.10.refs_2_ = bf16[3,4,256,128]{3,2,1,0:T(8,128)(2,1)S(1)} collective-permute-done((bf16[3,4,256,128]{3,2,1,0:T(8,128)(2,1)S(1)}, bf16[3,4,256,128]{3,2,1,0:T(8,128)(2,1)S(1)}, u32[]{:S(2)}, u32[]{:S(2)}) %collective-permute-start.10) | collective-permute-done | bytes 786464 | tf_op jit(solution)/shard_map/ppermute | solution.py:353
  171.7 17.9 %collective-permute-done.11.refs_3_ = bf16[3,4,256,128]{3,2,1,0:T(8,128)(2,1)S(1)} collective-permute-done((bf16[3,4,256,128]{3,2,1,0:T(8,128)(2,1)S(1)}, bf16[3,4,256,128]{3,2,1,0:T(8,128)(2,1)S(1)}, u32[]{:S(2)}, u32[]{:S(2)}) %collective-permute-start.11) | collective-permute-done | bytes 786464 | tf_op jit(solution)/shard_map/ppermute | solution.py:376
  195.8 30.0 %shard_map.187 = (bf16[4,256,128]{2,1,0:T(8,128)(2,1)S(1)}, bf16[4,256,128]{2,1,0:T(8,128)(2,1)S(1)}, bf16[4,256,128]{2,1,0:T(8,128)(2,1)S(1)}, bf16[4,256,128]{...) custom-call(s32[16]{0:T(128)S(1)} %fusion.49.place_ref, s32[8]{0:T(128)S(1)} %convert_reduce_fusion.4.starts_ref, ...), custom_call_target="tpu_custom_call" | custom-call | flops 8589934592 | bytes 8388608 | tf_op jit(solution)/shard_map/pallas_call | solution.py:1135
  230.4 11.4 %collective-permute-done.20 = bf16[1024,512]{1,0:T(8,128)(2,1)} collective-permute-done((bf16[1024,512]{1,0:T(8,128)(2,1)S(1)}, bf16[1024,512]{1,0:T(8,128)(2,1)}, u32[]{:S(2)}, u32[]{:S(2)}) %collective-permute-start.20) | collective-permute-done | bytes 1048608 | tf_op jit(solution)/shard_map/ppermute | solution.py:353
  261.0 23.8 %collective-permute-done.22 = bf16[256,2048]{1,0:T(8,128)(2,1)S(1)} collective-permute-done((bf16[256,2048]{1,0:T(8,128)(2,1)S(1)}, bf16[256,2048]{1,0:T(8,128)(2,1)S(1)}, u32[]{:S(2)}, u32[]{:S(2)}) %collective-permute-start.22) | collective-permute-done | bytes 1048608 | tf_op jit(solution)/shard_map/ppermute | solution.py:353
  290.8 18.7 %collective-permute-done.23 = bf16[256,2048]{1,0:T(8,128)(2,1)S(1)} collective-permute-done((bf16[256,2048]{1,0:T(8,128)(2,1)S(1)}, bf16[256,2048]{1,0:T(8,128)(2,1)S(1)}, u32[]{:S(2)}, u32[]{:S(2)}) %collective-permute-start.23) | collective-permute-done | bytes 1048608 | tf_op jit(solution)/shard_map/ppermute | solution.py:353
  309.5 24.2 %collective-permute-done.24 = bf16[256,2048]{1,0:T(8,128)(2,1)S(1)} collective-permute-done((bf16[256,2048]{1,0:T(8,128)(2,1)S(1)}, bf16[256,2048]{1,0:T(8,128)(2,1)S(1)}, u32[]{:S(2)}, u32[]{:S(2)}) %collective-permute-start.24) | collective-permute-done | bytes 1048608 | tf_op jit(solution)/shard_map/ppermute | solution.py:353
  356.0 30.4 %collective-permute-done.33 = bf16[512,1024]{1,0:T(8,128)(2,1)} collective-permute-done((bf16[512,1024]{1,0:T(8,128)(2,1)}, bf16[512,1024]{1,0:T(8,128)(2,1)}, u32[]{:S(2)}, u32[]{:S(2)}) %collective-permute-start.33) | collective-permute-done | bytes 1048608 | tf_op jit(solution)/shard_map/ppermute | solution.py:353
  388.7 14.6 %shard_map.190 = (f32[4,512,512]{2,1,0:T(8,128)}, f32[4,512,512]{2,1,0:T(8,128)}, bf16[4,512,512]{2,1,0:T(8,128)(2,1)S(1)}) custom-call(bf16[256,2048]{1,0:T(8,128)(2,1)S(1)} %collective-permute-done.29.refs_0_.refs_1_, bf16[256,2048]{1,0:T(8,128)(2,1)S(1)} %collective-permute-done.30.refs_1_.refs_2_, bf16[4,1024,512]{2,1,0:T(8,128)(2,1)} %copy-done.76, ...), custom_call_target="tpu_custom_call" | custom-call | flops 8589934592 | bytes 16777216 | tf_op jit(solution)/shard_map/pallas_call | solution.py:739
  502.5 11.7 %shard_map.196 = (bf16[4,512,512]{2,1,0:T(8,128)(2,1)S(1)}, bf16[4,512,512]{2,1,0:T(8,128)(2,1)S(1)}) custom-call(bf16[256,2048]{1,0:T(8,128)(2,1)S(1)} %collective-permute-done.42.refs_0_.refs_4_, bf16[256,2048]{1,0:T(8,128)(2,1)} %collective-permute-done.43.refs_1_.refs_5_, f32[4,512,512]{2,1,0:T(8,128)} %get-tuple-element.257.refs_2_, ...), custom_call_target="tpu_custom_call" | custom-call | flops 4294967296 | bytes 16777216 | tf_op jit(solution)/shard_map/pallas_call | solution.py:798
  537.8 13.9 %shard_map.199 = (f32[128,2048]{1,0:T(8,128)S(1)}, bf16[128,2048]{1,0:T(8,128)(2,1)S(1)}, bf16[128,2048]{1,0:T(8,128)(2,1)S(1)}, f32[128,2048]{1,0:T(8,128)S(1)}) custom-call(bf16[4,512,512]{2,1,0:T(8,128)(2,1)S(1)} %copy-done.61, bf16[4,512,512]{2,1,0:T(8,128)(2,1)} %copy-done.58, bf16[4,1024,512]{2,1,0:T(8,128)(2,1)} %copy-done.76, ...), custom_call_target="tpu_custom_call" | custom-call | flops 8589934592 | bytes 18874368 | tf_op jit(solution)/shard_map/pallas_call | solution.py:837
  554.6 15.3 %shard_map.200 = (bf16[2,2,512,1024]{3,2,1,0:T(8,128)(2,1)S(1)}, bf16[2,2,512,1024]{3,2,1,0:T(8,128)(2,1)}) custom-call(bf16[4,256,512]{2,1,0:T(8,128)(2,1)S(1)} %copy-done.37, bf16[4,512,512]{2,1,0:T(8,128)(2,1)S(1)} %copy-done.72, bf16[4,256,512]{2,1,0:T(8,128)(2,1)S(1)} %copy-done.29, bf16[256,2048]{1,0:T(8,128)(2,1)S(1)} %fusion.28.refs_0_.refs_3_, ...), custom_call_target="tpu_custom_call" | custom-call | flops 8589934592 | bytes 16777216 | tf_op jit(solution)/shard_map/pallas_call | solution.py:913
  619.8 42.3 %collective-permute-done.53.refs_2_ = bf16[256,2048]{1,0:T(8,128)(2,1)} collective-permute-done((bf16[256,2048]{1,0:T(8,128)(2,1)S(1)}, bf16[256,2048]{1,0:T(8,128)(2,1)}, u32[]{:S(2)}, u32[]{:S(2)}) %collective-permute-start.53) | collective-permute-done | bytes 1048608 | tf_op jit(solution)/shard_map/ppermute | solution.py:353
  726.7 20.5 %collective-permute-done.60.refs_5_ = bf16[4,256,128]{2,1,0:T(8,128)(2,1)S(1)} collective-permute-done((bf16[4,256,128]{2,1,0:T(8,128)(2,1)S(1)}, bf16[4,256,128]{2,1,0:T(8,128)(2,1)S(1)}, u32[]{:S(2)}, u32[]{:S(2)}) %collective-permute-start.60) | collective-permute-done | bytes 262176 | tf_op jit(solution)/shard_map/ppermute | solution.py:353
  752.7 40.6 %shard_map.206 = (bf16[3,4,256,128]{3,2,1,0:T(8,128)(2,1)S(1)}, bf16[3,4,256,128]{3,2,1,0:T(8,128)(2,1)}, bf16[3,4,256,128]{3,2,1,0:T(8,128)(2,1)}, bf16[3,4,256,128]{3,2,1,0:T(8,128)(2,1)}) custom-call(s32[16]{0:T(128)S(1)} %fusion.49.place_ref, s32[8]{0:T(128)S(1)} %convert_reduce_fusion.4.starts_ref, bf16[3,4,256,128]{3,2,1,0:T(8,128)(2,1)} %copy-done.73, ...), custom_call_target="tpu_custom_call" | custom-call | flops 21474836480 | bytes 16777216 | tf_op jit(solution)/shard_map/pallas_call | solution.py:1160
  821.4 20.5 %collective-permute-done.69.refs_6_.refs_2_ = bf16[3,4,256,128]{3,2,1,0:T(8,128)(2,1)S(1)} collective-permute-done((bf16[3,4,256,128]{3,2,1,0:T(8,128)(2,1)}, bf16[3,4,256,128]{3,2,1,0:T(8,128)(2,1)S(1)}, u32[]{:S(2)}, u32[]{:S(2)}) %collective-permute-start.69) | collective-permute-done | bytes 786464 | tf_op jit(solution)/shard_map/ppermute | solution.py:353
  841.9 18.6 %collective-permute-done.70.refs_7_.refs_3_ = bf16[3,4,256,128]{3,2,1,0:T(8,128)(2,1)S(1)} collective-permute-done((bf16[3,4,256,128]{3,2,1,0:T(8,128)(2,1)}, bf16[3,4,256,128]{3,2,1,0:T(8,128)(2,1)S(1)}, u32[]{:S(2)}, u32[]{:S(2)}) %collective-permute-start.70) | collective-permute-done | bytes 786464 | tf_op jit(solution)/shard_map/ppermute | solution.py:376
  911.1 16.7 %collective-permute-done.75 = bf16[1024,512]{1,0:T(8,128)(2,1)} collective-permute-done((bf16[1024,512]{1,0:T(8,128)(2,1)}, bf16[1024,512]{1,0:T(8,128)(2,1)}, u32[]{:S(2)}, u32[]{:S(2)}) %collective-permute-start.75) | collective-permute-done | bytes 1048608 | tf_op jit(solution)/shard_map/ppermute | solution.py:353
  937.0 16.4 %collective-permute-done.80 = bf16[4,1024,128]{2,1,0:T(8,128)(2,1)S(1)} collective-permute-done((bf16[4,1024,128]{2,1,0:T(8,128)(2,1)S(1)}, bf16[4,1024,128]{2,1,0:T(8,128)(2,1)S(1)}, u32[]{:S(2)}, u32[]{:S(2)}) %collective-permute-start.80) | collective-permute-done | bytes 1048608 | tf_op jit(solution)/shard_map/ppermute | solution.py:353
  954.0 24.5 %collective-permute-done.77 = bf16[256,2048]{1,0:T(8,128)(2,1)S(1)} collective-permute-done((bf16[256,2048]{1,0:T(8,128)(2,1)S(1)}, bf16[256,2048]{1,0:T(8,128)(2,1)S(1)}, u32[]{:S(2)}, u32[]{:S(2)}) %collective-permute-start.77) | collective-permute-done | bytes 1048608 | tf_op jit(solution)/shard_map/ppermute | solution.py:353
  991.6 15.0 %collective-permute-done.83 = bf16[4,512,128]{2,1,0:T(8,128)(2,1)} collective-permute-done((bf16[4,512,128]{2,1,0:T(8,128)(2,1)}, bf16[4,512,128]{2,1,0:T(8,128)(2,1)}, u32[]{:S(2)}, u32[]{:S(2)}) %collective-permute-start.83) | collective-permute-done | bytes 524320 | tf_op jit(solution)/shard_map/ppermute | solution.py:353
  (599 shorter events, 521.6 us)
Async XLA Ops:
  35.6 64.8 %collective-permute-start.3 = (bf16[512,1024]{1,0:T(8,128)(2,1)}, bf16[512,1024]{1,0:T(8,128)(2,1)}, u32[]{:S(2)}, u32[]{:S(2)}) collective-permute-start(bf16[512,1024]{1,0:T(8,128)(2,1)} %pad_maximum_fusion.8), channel_id=1, source_target_pairs={{0,2},{1,3},{2,0},{3,1},{4,6},{5,7},{6,4},{7,5},{8,10},{9,11},{10,... | collective-permute-start | bytes 3145736 | tf_op jit(solution)/shard_map/ppermute | solution.py:353
  38.5 61.9 %collective-permute-start.5 = (bf16[4,1024,128]{2,1,0:T(8,128)(2,1)}, bf16[4,1024,128]{2,1,0:T(8,128)(2,1)}, u32[]{:S(2)}, u32[]{:S(2)}) collective-permute-start(bf16[4,1024,128]{2,1,0:T(8,128)(2,1)} %maximum_select_fusion.1), channel_id=1, source_target_pairs={{0,24},{4,28},{8,16},{12,20},{16,8},{20,12},{24,0},{28,4},{1,25},{... | collective-permute-start | bytes 3145736 | tf_op jit(solution)/shard_map/ppermute | solution.py:389
  55.0 45.4 %collective-permute-start.7 = (bf16[4,1024,128]{2,1,0:T(8,128)(2,1)}, bf16[4,1024,128]{2,1,0:T(8,128)(2,1)}, u32[]{:S(2)}, u32[]{:S(2)}) collective-permute-start(bf16[4,1024,128]{2,1,0:T(8,128)(2,1)} %collective-permute-done.6), channel_id=1, source_target_pairs={{0,24},{4,28},{8,16},{12,20},{16,8},{20,12},{24,0},{28,4},{1,25},{... | collective-permute-start | bytes 3145736 | tf_op jit(solution)/shard_map/ppermute | solution.py:389
  105.8 49.1 %collective-permute-start.14 = (bf16[1024,512]{1,0:T(8,128)(2,1)S(1)}, bf16[1024,512]{1,0:T(8,128)(2,1)S(1)}, u32[]{:S(2)}, u32[]{:S(2)}) collective-permute-start(bf16[1024,512]{1,0:T(8,128)(2,1)S(1)} %maximum_select_fusion.2), channel_id=1, source_target_pairs={{0,2},{1,3},{2,0},{3,1},{4,6},{5,7},{6,4},{7,5},{8,10},{9,11},{10,... | collective-permute-start | bytes 3145736 | tf_op jit(solution)/shard_map/ppermute | solution.py:353
  191.5 50.4 %collective-permute-start.21 = (bf16[1024,512]{1,0:T(8,128)(2,1)S(1)}, bf16[1024,512]{1,0:T(8,128)(2,1)S(1)}, u32[]{:S(2)}, u32[]{:S(2)}) collective-permute-start(bf16[1024,512]{1,0:T(8,128)(2,1)S(1)} %maximum_select_fusion.3), channel_id=1, source_target_pairs={{0,24},{4,28},{8,16},{12,20},{16,8},{20,12},{24,0},{28,4},{1,25},{... | collective-permute-start | bytes 3145736 | tf_op jit(solution)/shard_map/ppermute | solution.py:389
  193.3 48.6 %collective-permute-start.20 = (bf16[1024,512]{1,0:T(8,128)(2,1)S(1)}, bf16[1024,512]{1,0:T(8,128)(2,1)}, u32[]{:S(2)}, u32[]{:S(2)}) collective-permute-start(bf16[1024,512]{1,0:T(8,128)(2,1)S(1)} %maximum_select_fusion.3), channel_id=1, source_target_pairs={{0,2},{1,3},{2,0},{3,1},{4,6},{5,7},{6,4},{7,5},{8,10},{9,11},{10,... | collective-permute-start | bytes 3145736 | tf_op jit(solution)/shard_map/ppermute | solution.py:353
  253.2 81.8 %collective-permute-start.26 = (bf16[4,1024,512]{2,1,0:T(8,128)(2,1)S(1)}, bf16[4,1024,512]{2,1,0:T(8,128)(2,1)}, u32[]{:S(2)}, u32[]{:S(2)}) collective-permute-start(bf16[4,1024,512]{2,1,0:T(8,128)(2,1)S(1)} %pad_maximum_fusion.1.refs_1_.refs_2_), channel_id=1, source_target_pairs={{0,16},{16,0},{1,17},{17,1},{2,18},{18,2},{3,19},{19,3},{4,20},{20... | collective-permute-start | bytes 12582920 | tf_op jit(solution)/shard_map/ppermute | solution.py:384
  285.8 47.9 %collective-permute-start.24 = (bf16[256,2048]{1,0:T(8,128)(2,1)S(1)}, bf16[256,2048]{1,0:T(8,128)(2,1)S(1)}, u32[]{:S(2)}, u32[]{:S(2)}) collective-permute-start(bf16[256,2048]{1,0:T(8,128)(2,1)S(1)} %add_convert_fusion.9), channel_id=1, source_target_pairs={{0,2},{1,3},{2,0},{3,1},{4,6},{5,7},{6,4},{7,5},{8,10},{9,11},{10,... | collective-permute-start | bytes 3145736 | tf_op jit(solution)/shard_map/ppermute | solution.py:353
  288.5 46.5 %collective-permute-start.27 = (bf16[512,1024]{1,0:T(8,128)(2,1)}, bf16[512,1024]{1,0:T(8,128)(2,1)S(1)}, u32[]{:S(2)}, u32[]{:S(2)}) collective-permute-start(bf16[512,1024]{1,0:T(8,128)(2,1)} %maximum_select_fusion.5), channel_id=1, source_target_pairs={{0,24},{4,28},{8,16},{12,20},{16,8},{20,12},{24,0},{28,4},{1,25},{... | collective-permute-start | bytes 3145736 | tf_op jit(solution)/shard_map/ppermute | solution.py:389
  337.5 48.9 %collective-permute-start.33 = (bf16[512,1024]{1,0:T(8,128)(2,1)}, bf16[512,1024]{1,0:T(8,128)(2,1)}, u32[]{:S(2)}, u32[]{:S(2)}) collective-permute-start(bf16[512,1024]{1,0:T(8,128)(2,1)} %maximum_select_fusion.5), channel_id=1, source_target_pairs={{0,2},{1,3},{2,0},{3,1},{4,6},{5,7},{6,4},{7,5},{8,10},{9,11},{10,... | collective-permute-start | bytes 3145736 | tf_op jit(solution)/shard_map/ppermute | solution.py:353
  337.5 48.9 %collective-permute-start.29 = (bf16[256,2048]{1,0:T(8,128)(2,1)S(1)}, bf16[256,2048]{1,0:T(8,128)(2,1)S(1)}, u32[]{:S(2)}, u32[]{:S(2)}) collective-permute-start(bf16[256,2048]{1,0:T(8,128)(2,1)S(1)} %get-tuple-element.419.refs_0_), channel_id=1, source_target_pairs={{0,4},{4,0},{8,12},{12,8},{1,5},{5,1},{9,13},{13,9},{2,6},{6,2},{1... | collective-permute-start | bytes 3145736 | tf_op jit(solution)/shard_map/ppermute | solution.py:353
  338.8 48.3 %collective-permute-start.30 = (bf16[256,2048]{1,0:T(8,128)(2,1)S(1)}, bf16[256,2048]{1,0:T(8,128)(2,1)S(1)}, u32[]{:S(2)}, u32[]{:S(2)}) collective-permute-start(bf16[256,2048]{1,0:T(8,128)(2,1)S(1)} %get-tuple-element.419.refs_0_), channel_id=1, source_target_pairs={{0,1},{1,0},{2,3},{3,2},{4,5},{5,4},{6,7},{7,6},{8,9},{9,8},{10,11... | collective-permute-start | bytes 3145736 | tf_op jit(solution)/shard_map/ppermute | solution.py:353
  613.3 49.4 %collective-permute-start.58 = (bf16[2,2,1024,512]{3,2,1,0:T(8,128)(2,1)S(1)}, bf16[2,2,1024,512]{3,2,1,0:T(8,128)(2,1)S(1)}, u32[]{:S(2)}, u32[]{:S(2)}) collective-permute-start(bf16[2,2,1024,512]{3,2,1,0:T(8,128)(2,1)S(1)} %get-tuple-element.296), channel_id=1, source_target_pairs={{0,16},{16,0},{1,17},{17,1},{2,18},{18,2},{3,19},{19,3},{4,20},{20... | collective-permute-start | bytes 12582920 | tf_op jit(solution)/shard_map/ppermute | solution.py:384
  613.4 48.8 %collective-permute-start.53 = (bf16[256,2048]{1,0:T(8,128)(2,1)S(1)}, bf16[256,2048]{1,0:T(8,128)(2,1)}, u32[]{:S(2)}, u32[]{:S(2)}) collective-permute-start(bf16[256,2048]{1,0:T(8,128)(2,1)S(1)} %get-tuple-element.307.refs_0_), channel_id=1, source_target_pairs={{0,2},{1,3},{2,0},{3,1},{4,6},{5,7},{6,4},{7,5},{8,10},{9,11},{10,... | collective-permute-start | bytes 3145736 | tf_op jit(solution)/shard_map/ppermute | solution.py:353
  617.6 44.5 %collective-permute-start.55 = (bf16[512,1024]{1,0:T(8,128)(2,1)S(1)}, bf16[512,1024]{1,0:T(8,128)(2,1)S(1)}, u32[]{:S(2)}, u32[]{:S(2)}) collective-permute-start(bf16[512,1024]{1,0:T(8,128)(2,1)S(1)} %get-tuple-element.429), channel_id=1, source_target_pairs={{0,24},{4,28},{8,16},{12,20},{16,8},{20,12},{24,0},{28,4},{1,25},{... | collective-permute-start | bytes 3145736 | tf_op jit(solution)/shard_map/ppermute | solution.py:389
  617.7 47.7 %collective-permute-start.52 = (bf16[256,2048]{1,0:T(8,128)(2,1)S(1)}, bf16[256,2048]{1,0:T(8,128)(2,1)S(1)}, u32[]{:S(2)}, u32[]{:S(2)}) collective-permute-start(bf16[256,2048]{1,0:T(8,128)(2,1)S(1)} %get-tuple-element.307.refs_0_), channel_id=1, source_target_pairs={{0,4},{4,0},{8,12},{12,8},{1,5},{5,1},{9,13},{13,9},{2,6},{6,2},{1... | collective-permute-start | bytes 3145736 | tf_op jit(solution)/shard_map/ppermute | solution.py:353
  618.3 47.1 %collective-permute-start.57 = (bf16[512,1024]{1,0:T(8,128)(2,1)S(1)}, bf16[512,1024]{1,0:T(8,128)(2,1)S(1)}, u32[]{:S(2)}, u32[]{:S(2)}) collective-permute-start(bf16[512,1024]{1,0:T(8,128)(2,1)S(1)} %get-tuple-element.295), channel_id=1, source_target_pairs={{0,24},{4,28},{8,16},{12,20},{16,8},{20,12},{24,0},{28,4},{1,25},{... | collective-permute-start | bytes 3145736 | tf_op jit(solution)/shard_map/ppermute | solution.py:389
  747.2 47.9 %collective-permute-start.65 = (bf16[512,1024]{1,0:T(8,128)(2,1)}, bf16[512,1024]{1,0:T(8,128)(2,1)S(1)}, u32[]{:S(2)}, u32[]{:S(2)}) collective-permute-start(bf16[512,1024]{1,0:T(8,128)(2,1)} %fusion.27), channel_id=1, source_target_pairs={{0,2},{1,3},{2,0},{3,1},{4,6},{5,7},{6,4},{7,5},{8,10},{9,11},{10,... | collective-permute-start | bytes 3145736 | tf_op jit(solution)/shard_map/ppermute | solution.py:353
  751.0 47.4 %collective-permute-start.66 = (bf16[1024,512]{1,0:T(8,128)(2,1)S(1)}, bf16[1024,512]{1,0:T(8,128)(2,1)S(1)}, u32[]{:S(2)}, u32[]{:S(2)}) collective-permute-start(bf16[1024,512]{1,0:T(8,128)(2,1)S(1)} %get-tuple-element.325), channel_id=1, source_target_pairs={{0,24},{4,28},{8,16},{12,20},{16,8},{20,12},{24,0},{28,4},{1,25},{... | collective-permute-start | bytes 3145736 | tf_op jit(solution)/shard_map/ppermute | solution.py:389
  799.4 61.1 %collective-permute-start.72 = (bf16[1024,512]{1,0:T(8,128)(2,1)}, bf16[1024,512]{1,0:T(8,128)(2,1)S(1)}, u32[]{:S(2)}, u32[]{:S(2)}) collective-permute-start(bf16[1024,512]{1,0:T(8,128)(2,1)} %fusion.24), channel_id=1, source_target_pairs={{0,2},{1,3},{2,0},{3,1},{4,6},{5,7},{6,4},{7,5},{8,10},{9,11},{10,... | collective-permute-start | bytes 3145736 | tf_op jit(solution)/shard_map/ppermute | solution.py:353
  802.5 58.0 %collective-permute-start.70 = (bf16[3,4,256,128]{3,2,1,0:T(8,128)(2,1)}, bf16[3,4,256,128]{3,2,1,0:T(8,128)(2,1)S(1)}, u32[]{:S(2)}, u32[]{:S(2)}) collective-permute-start(bf16[3,4,256,128]{3,2,1,0:T(8,128)(2,1)} %get-tuple-element.330), channel_id=1, source_target_pairs={{0,9},{1,8},{2,11},{3,10},{4,13},{5,12},{6,15},{7,14},{8,1},{9,0},... | collective-permute-start | bytes 2359304 | tf_op jit(solution)/shard_map/ppermute | solution.py:376
  878.8 49.0 %collective-permute-start.75 = (bf16[1024,512]{1,0:T(8,128)(2,1)}, bf16[1024,512]{1,0:T(8,128)(2,1)}, u32[]{:S(2)}, u32[]{:S(2)}) collective-permute-start(bf16[1024,512]{1,0:T(8,128)(2,1)} %fusion.23), channel_id=1, source_target_pairs={{0,2},{1,3},{2,0},{3,1},{4,6},{5,7},{6,4},{7,5},{8,10},{9,11},{10,... | collective-permute-start | bytes 3145736 | tf_op jit(solution)/shard_map/ppermute | solution.py:353
  907.9 71.2 %collective-permute-start.82 = (bf16[2,2,512,512]{3,2,1,0:T(8,128)(2,1)S(1)}, bf16[2,2,512,512]{3,2,1,0:T(8,128)(2,1)S(1)}, u32[]{:S(2)}, u32[]{:S(2)}) collective-permute-start(bf16[2,2,512,512]{3,2,1,0:T(8,128)(2,1)S(1)} %pad_maximum_fusion.7), channel_id=1, source_target_pairs={{0,16},{16,0},{1,17},{17,1},{2,18},{18,2},{3,19},{19,3},{4,20},{20... | collective-permute-start | bytes 6291464 | tf_op jit(solution)/shard_map/ppermute | solution.py:384
  930.3 48.2 %collective-permute-start.77 = (bf16[256,2048]{1,0:T(8,128)(2,1)S(1)}, bf16[256,2048]{1,0:T(8,128)(2,1)S(1)}, u32[]{:S(2)}, u32[]{:S(2)}) collective-permute-start(bf16[256,2048]{1,0:T(8,128)(2,1)S(1)} %add_convert_fusion.2), channel_id=1, source_target_pairs={{0,2},{1,3},{2,0},{3,1},{4,6},{5,7},{6,4},{7,5},{8,10},{9,11},{10,... | collective-permute-start | bytes 3145736 | tf_op jit(solution)/shard_map/ppermute | solution.py:353
  (212 other events, 3912.7 us)

commit v5 on v4

--- a/solution.py
+++ b/solution.py
@@ -1333,42 +1333,42 @@
     two_sides = run_normed_two("sides", *after(low_sides, two_far), gates, ups)
 
     first = near_reduce_far(two_far)
-    down_grads = Spread(run_down_grad(after(units, two_sides, first), out_acts))
     got = near_reduce_sides(first, two_sides)
+    two_own = run_normed_two("own", *after(low_own, two_sides, first), gates, ups)
+    down_grads = Spread(run_down_grad(after(units, two_own, got[1:3]), out_acts))
     down_core = down_grads.to_core()
-    two_own = run_normed_two("own", *after(low_own, down_grads.keep, got[1:3]), gates, ups)
     normed_two_grad = near_reduce_end(got, two_own[0])
-    gate_pair = run_wide_grad(two_acts, after([low[0] for low in lows], two_own, down_core))
+    middle_grad = out_grad + local_norm_backward(normed_two_grad, normed_two, inverse_two)
+    low_middle = middle_grad.astype(BF)
+    gate_pair = run_wide_grad(two_acts, after([low[0] for low in lows], low_middle, down_core))
     gate_grads = Spread(gate_pair)
     down_y1 = down_grads.to_y(1)
-    middle_grad = out_grad + local_norm_backward(normed_two_grad, normed_two, inverse_two)
-    low_middle = middle_grad.astype(BF)
     layer_output = to_width(swap_y(after(output, low_middle).astype(BF)))
     gate_core = gate_grads.to_core(low_middle)
     down_y0 = down_grads.to_y(0, low_middle)
-    up_pair = run_wide_grad(two_acts, after([low[1] for low in lows], gate_pair))
+    up_pair = run_wide_grad(two_acts, after([low[1] for low in lows], gate_pair, down_y1))
     up_grads = Spread(up_pair)
-    middle_acts = square_gather(low_middle, gate_pair, down_y1)
-    gate_y1 = gate_grads.to_y(1, down_y0, middle_acts[1:3])
-    middle_acts = after(middle_acts, up_pair, down_y0, gate_y1, layer_output)
+    middle_acts = square_gather(low_middle, gate_pair, up_pair, layer_output)
+    middle_acts = after(middle_acts, up_pair, down_y0, layer_output)
     grad_messages = run_attended_grad(middle_acts, heads)
     up_core = up_grads.to_core(grad_messages)
-    gate_y0 = gate_grads.to_y(0, gate_y1)
     down_grads.to_high(flip_far, middle_acts[1:3])
     out_pair = run_head_grad(1, after(middle_acts, grad_messages), mixed)
     grad_messages = swap_slots(grad_messages)
-    grad_messages = after(grad_messages, up_core, out_pair, gate_y0)
+    grad_messages = after(grad_messages, up_core, out_pair)
+    gate_y1 = gate_grads.to_y(1, grad_messages)
+    gate_y0 = gate_grads.to_y(0, grad_messages)
     up_y0 = up_grads.to_y(0, grad_messages)
     up_y1 = up_grads.to_y(1, grad_messages)
     back = run_backward(
         pieces, starts, messages, grad_messages, wide_mixed, log_total, cos_wide, sin_wide
     )
-    back = after(back, down_grads.high, up_y1, up_y0)
+    back = after(back, down_grads.high, gate_y1, gate_y0)
     gate_grads.to_high(flip_far, back)
     own_down, send_down = to_x(down_grads.total(back), x, 1)
     down_x = flip_x(send_down)
     back = swap_slots(back)
-    back = after(back, down_x, gate_grads.high)
+    back = after(back, down_x, gate_grads.high, up_y1, up_y0)
     up_grads.to_high(flip_far, back)
     own_gate, send_gate = to_x(gate_grads.total(back), x, 0)
     gate_x = flip_x(send_gate)

time: 1040 us -> 1010 us (0.971)
  waiting for transfers between devices: 479 us -> 448 us
    ppermute x56, waiting for transfers between devices: 369 us -> 312 us  [flip(): return lax.ppermute(values, axis, [(i, i ^ bit) for i in range(SIDE)])]
    ppermute x16, waiting for transfers between devices: 17.2 us -> 63.6 us  [flip_dp_y(): return lax.ppermute(values, ('dp', 'row'), pairs)]
    ppermute x4, waiting for transfers between devices: 42.3 us -> 29.4 us  [flip_y_near(): return lax.ppermute(values, ('row', 'col'), pairs)]
    unnamed x292 -> x270, local copies, waits for them, and re-layouts: 44.6 us -> 45.5 us
  transfers between devices with their start and end apart: 92 -> 92, of which waited for: 41 -> 40; matrix products, arithmetic and copies ran while one was open for 12% -> 12% of each run, Pallas kernels for 19% -> 22%
where the time goes in v5:
time: 1010 us; the launch traced here: 1000 us
  waiting for transfers between devices  448 us (44%)
  Pallas kernels  264 us (26%)
  other arithmetic  114 us (11%)
  starting transfers between devices  100 us (10%)
  local copies, waits for them, and re-layouts  69.5 us (7%)
    ppermute x56, waiting for transfers between devices, flip(): return lax.ppermute(values, axis, [(i, i ^ bit) for i in range(SIDE)])  312 us
    ppermute x16, waiting for transfers between devices, flip_dp_y(): return lax.ppermute(values, ('dp', 'row'), pairs)  63.6 us
    ppermute x56, starting transfers between devices, flip(): return lax.ppermute(values, axis, [(i, i ^ bit) for i in range(SIDE)])  61.2 us
    unnamed x270, local copies, waits for them, and re-layouts  45.5 us
    pallas_call x1, Pallas kernels, run_backward(): pl.pallas_call(attention_backward, out_shape=[jax.ShapeDtypeStruct((3, 4,...  41.1 us
    pallas_call x3, Pallas kernels, run_up(): pl.pallas_call(lambda *refs: up_kernel(len(acts), *refs), grid=(width //...  35.3 us
    pallas_call x3, Pallas kernels, run_normed_two(): pl.pallas_call(lambda *refs: normed_two_kernel(kind, *refs), grid=(2,), o...  32.6 us
    pallas_call x1, Pallas kernels, run_forward(): pl.pallas_call(attention_forward, out_shape=out_shape, in_specs=[SMEM_SPE...  30.3 us
  transfers between devices with their start and end apart: 92, of which 40 were waited for; matrix products, arithmetic and copies ran while one was open for 12% of the time, Pallas kernels for 22%

profile of v5, /device:TPU:0, one launch (start us, length us, event | category | flops | bytes accessed | tf_op | source)
XLA Modules:
  0.0 1000.8 jit_solution(8275394809555373909)
XLA Ops:
  38.7 16.5 %all-to-all-done = f32[8,8,128]{2,1,0:T(8,128)S(1)} async-done(((f32[8,8,128]{2,1,0:T(8,128)}), f32[8,8,128]{2,1,0:T(8,128)S(1)}, u32[]{:S(2)}, u32[]{:S(2)}) %all-to-all-start) | async-done | bytes 32800 | tf_op jit(solution)/shard_map/all_to_all | solution.py:510
  74.0 23.2 %all-to-all-done.1 = bf16[4,256,512]{2,1,0:T(8,128)(2,1)} async-done(((bf16[4,256,512]{2,1,0:T(8,128)(2,1)}), bf16[4,256,512]{2,1,0:T(8,128)(2,1)}, u32[]{:S(2)}, u32[]{:S(2)}) %all-to-all-start.1) | async-done | bytes 1048608 | tf_op jit(solution)/shard_map/all_to_all | solution.py:1180
  110.0 21.1 %collective-permute-done.4 = bf16[512,1024]{1,0:T(8,128)(2,1)S(1)} collective-permute-done((bf16[512,1024]{1,0:T(8,128)(2,1)}, bf16[512,1024]{1,0:T(8,128)(2,1)S(1)}, u32[]{:S(2)}, u32[]{:S(2)}) %collective-permute-start.4) | collective-permute-done | bytes 1048608 | tf_op jit(solution)/shard_map/ppermute | solution.py:353
  157.7 13.4 %collective-permute-done.10.refs_2_ = bf16[3,4,256,128]{3,2,1,0:T(8,128)(2,1)S(1)} collective-permute-done((bf16[3,4,256,128]{3,2,1,0:T(8,128)(2,1)S(1)}, bf16[3,4,256,128]{3,2,1,0:T(8,128)(2,1)S(1)}, u32[]{:S(2)}, u32[]{:S(2)}) %collective-permute-start.10) | collective-permute-done | bytes 786464 | tf_op jit(solution)/shard_map/ppermute | solution.py:353
  171.1 17.9 %collective-permute-done.11.refs_3_ = bf16[3,4,256,128]{3,2,1,0:T(8,128)(2,1)S(1)} collective-permute-done((bf16[3,4,256,128]{3,2,1,0:T(8,128)(2,1)S(1)}, bf16[3,4,256,128]{3,2,1,0:T(8,128)(2,1)S(1)}, u32[]{:S(2)}, u32[]{:S(2)}) %collective-permute-start.11) | collective-permute-done | bytes 786464 | tf_op jit(solution)/shard_map/ppermute | solution.py:376
  195.2 30.3 %shard_map.187 = (bf16[4,256,128]{2,1,0:T(8,128)(2,1)S(1)}, bf16[4,256,128]{2,1,0:T(8,128)(2,1)S(1)}, bf16[4,256,128]{2,1,0:T(8,128)(2,1)S(1)}, bf16[4,256,128]{...) custom-call(s32[16]{0:T(128)S(1)} %fusion.49.place_ref, s32[8]{0:T(128)S(1)} %convert_reduce_fusion.4.starts_ref, ...), custom_call_target="tpu_custom_call" | custom-call | flops 8589934592 | bytes 8388608 | tf_op jit(solution)/shard_map/pallas_call | solution.py:1135
  260.4 23.8 %collective-permute-done.22 = bf16[256,2048]{1,0:T(8,128)(2,1)S(1)} collective-permute-done((bf16[256,2048]{1,0:T(8,128)(2,1)S(1)}, bf16[256,2048]{1,0:T(8,128)(2,1)S(1)}, u32[]{:S(2)}, u32[]{:S(2)}) %collective-permute-start.22) | collective-permute-done | bytes 1048608 | tf_op jit(solution)/shard_map/ppermute | solution.py:353
  289.5 19.3 %collective-permute-done.23 = bf16[256,2048]{1,0:T(8,128)(2,1)S(1)} collective-permute-done((bf16[256,2048]{1,0:T(8,128)(2,1)S(1)}, bf16[256,2048]{1,0:T(8,128)(2,1)S(1)}, u32[]{:S(2)}, u32[]{:S(2)}) %collective-permute-start.23) | collective-permute-done | bytes 1048608 | tf_op jit(solution)/shard_map/ppermute | solution.py:353
  308.8 24.3 %collective-permute-done.24 = bf16[256,2048]{1,0:T(8,128)(2,1)S(1)} collective-permute-done((bf16[256,2048]{1,0:T(8,128)(2,1)S(1)}, bf16[256,2048]{1,0:T(8,128)(2,1)S(1)}, u32[]{:S(2)}, u32[]{:S(2)}) %collective-permute-start.24) | collective-permute-done | bytes 1048608 | tf_op jit(solution)/shard_map/ppermute | solution.py:353
  355.4 30.1 %collective-permute-done.33 = bf16[512,1024]{1,0:T(8,128)(2,1)S(1)} collective-permute-done((bf16[512,1024]{1,0:T(8,128)(2,1)S(1)}, bf16[512,1024]{1,0:T(8,128)(2,1)S(1)}, u32[]{:S(2)}, u32[]{:S(2)}) %collective-permute-start.33) | collective-permute-done | bytes 1048608 | tf_op jit(solution)/shard_map/ppermute | solution.py:353
  387.9 14.7 %shard_map.190 = (f32[4,512,512]{2,1,0:T(8,128)}, f32[4,512,512]{2,1,0:T(8,128)}, bf16[4,512,512]{2,1,0:T(8,128)(2,1)S(1)}) custom-call(bf16[256,2048]{1,0:T(8,128)(2,1)S(1)} %collective-permute-done.29.refs_0_.refs_1_, bf16[256,2048]{1,0:T(8,128)(2,1)S(1)} %collective-permute-done.30.refs_1_.refs_2_, bf16[4,1024,512]{2,1,0:T(8,128)(2,1)} %copy-done.79, ...), custom_call_target="tpu_custom_call" | custom-call | flops 8589934592 | bytes 16777216 | tf_op jit(solution)/shard_map/pallas_call | solution.py:739
  501.1 11.7 %shard_map.196 = (bf16[4,512,512]{2,1,0:T(8,128)(2,1)S(1)}, bf16[4,512,512]{2,1,0:T(8,128)(2,1)S(1)}) custom-call(bf16[256,2048]{1,0:T(8,128)(2,1)S(1)} %collective-permute-done.42.refs_0_.refs_4_, bf16[256,2048]{1,0:T(8,128)(2,1)} %collective-permute-done.43.refs_1_.refs_5_, f32[4,512,512]{2,1,0:T(8,128)} %get-tuple-element.257.refs_2_, ...), custom_call_target="tpu_custom_call" | custom-call | flops 4294967296 | bytes 16777216 | tf_op jit(solution)/shard_map/pallas_call | solution.py:798
  537.0 13.9 %shard_map.199 = (f32[128,2048]{1,0:T(8,128)S(1)}, bf16[128,2048]{1,0:T(8,128)(2,1)S(1)}, bf16[128,2048]{1,0:T(8,128)(2,1)S(1)}, f32[128,2048]{1,0:T(8,128)S(1)}) custom-call(bf16[4,512,512]{2,1,0:T(8,128)(2,1)S(1)} %get-tuple-element.284.refs_0_.refs_6_, bf16[4,512,512]{2,1,0:T(8,128)(2,1)} %copy-done.62, bf16[4,1024,512]{2,1,0:T(8,128)(2,1)} %copy-done.79, ...), custom_call_target="tpu_custom_call" | custom-call | flops 8589934592 | bytes 18874368 | tf_op jit(solution)/shard_map/pallas_call | solution.py:837
  564.5 14.4 %shard_map.201 = (bf16[2,2,512,1024]{3,2,1,0:T(8,128)(2,1)S(1)}, bf16[2,2,512,1024]{3,2,1,0:T(8,128)(2,1)S(1)}) custom-call(bf16[4,256,512]{2,1,0:T(8,128)(2,1)S(1)} %copy-done.44, bf16[4,512,512]{2,1,0:T(8,128)(2,1)S(1)} %copy-done.75, bf16[4,256,512]{2,1,0:T(8,128)(2,1)S(1)} %copy-done.28, bf16[256,2048]{1,0:T(8,128)(2,1)S(1)} %fusion.28.refs_0_.refs_3_, ...), custom_call_target="tpu_custom_call" | custom-call | flops 8589934592 | bytes 16777216 | tf_op jit(solution)/shard_map/pallas_call | solution.py:913
  663.1 12.4 %collective-permute-done.56.refs_3_ = bf16[256,2048]{1,0:T(8,128)(2,1)S(1)} collective-permute-done((bf16[256,2048]{1,0:T(8,128)(2,1)}, bf16[256,2048]{1,0:T(8,128)(2,1)S(1)}, u32[]{:S(2)}, u32[]{:S(2)}) %collective-permute-start.56) | collective-permute-done | bytes 1048608 | tf_op jit(solution)/shard_map/ppermute | solution.py:353
  712.5 41.1 %shard_map.206 = (bf16[3,4,256,128]{3,2,1,0:T(8,128)(2,1)S(1)}, bf16[3,4,256,128]{3,2,1,0:T(8,128)(2,1)}, bf16[3,4,256,128]{3,2,1,0:T(8,128)(2,1)}, bf16[3,4,256,128]{3,2,1,0:T(8,128)(2,1)}) custom-call(s32[16]{0:T(128)S(1)} %fusion.49.place_ref, s32[8]{0:T(128)S(1)} %convert_reduce_fusion.4.starts_ref, bf16[3,4,256,128]{3,2,1,0:T(8,128)(2,1)} %copy-done.76, ...), custom_call_target="tpu_custom_call" | custom-call | flops 21474836480 | bytes 16777216 | tf_op jit(solution)/shard_map/pallas_call | solution.py:1160
  758.6 17.5 %collective-permute-done.72 = bf16[1024,512]{1,0:T(8,128)(2,1)S(1)} collective-permute-done((bf16[1024,512]{1,0:T(8,128)(2,1)}, bf16[1024,512]{1,0:T(8,128)(2,1)S(1)}, u32[]{:S(2)}, u32[]{:S(2)}) %collective-permute-start.72) | collective-permute-done | bytes 1048608 | tf_op jit(solution)/shard_map/ppermute | solution.py:389
  780.7 20.1 %collective-permute-done.71 = bf16[1024,512]{1,0:T(8,128)(2,1)} collective-permute-done((bf16[1024,512]{1,0:T(8,128)(2,1)}, bf16[1024,512]{1,0:T(8,128)(2,1)}, u32[]{:S(2)}, u32[]{:S(2)}) %collective-permute-start.71) | collective-permute-done | bytes 1048608 | tf_op jit(solution)/shard_map/ppermute | solution.py:389
  801.3 12.9 %collective-permute-done.69 = bf16[512,512]{1,0:T(8,128)(2,1)S(1)} collective-permute-done((bf16[512,512]{1,0:T(8,128)(2,1)S(1)}, bf16[512,512]{1,0:T(8,128)(2,1)S(1)}, u32[]{:S(2)}, u32[]{:S(2)}) %collective-permute-start.69) | collective-permute-done | bytes 524320 | tf_op jit(solution)/shard_map/ppermute | solution.py:353
  814.2 17.4 %collective-permute-done.66.refs_5_.refs_1_ = bf16[3,4,256,128]{3,2,1,0:T(8,128)(2,1)S(1)} collective-permute-done((bf16[3,4,256,128]{3,2,1,0:T(8,128)(2,1)}, bf16[3,4,256,128]{3,2,1,0:T(8,128)(2,1)S(1)}, u32[]{:S(2)}, u32[]{:S(2)}) %collective-permute-start.66) | collective-permute-done | bytes 786464 | tf_op jit(solution)/shard_map/ppermute | solution.py:353
  884.0 14.7 %collective-permute-done.75 = bf16[1024,512]{1,0:T(8,128)(2,1)} collective-permute-done((bf16[1024,512]{1,0:T(8,128)(2,1)}, bf16[1024,512]{1,0:T(8,128)(2,1)}, u32[]{:S(2)}, u32[]{:S(2)}) %collective-permute-start.75) | collective-permute-done | bytes 1048608 | tf_op jit(solution)/shard_map/ppermute | solution.py:353
  908.3 16.7 %collective-permute-done.80 = bf16[4,1024,128]{2,1,0:T(8,128)(2,1)S(1)} collective-permute-done((bf16[4,1024,128]{2,1,0:T(8,128)(2,1)S(1)}, bf16[4,1024,128]{2,1,0:T(8,128)(2,1)S(1)}, u32[]{:S(2)}, u32[]{:S(2)}) %collective-permute-start.80) | collective-permute-done | bytes 1048608 | tf_op jit(solution)/shard_map/ppermute | solution.py:353
  925.5 24.3 %collective-permute-done.77 = bf16[256,2048]{1,0:T(8,128)(2,1)S(1)} collective-permute-done((bf16[256,2048]{1,0:T(8,128)(2,1)S(1)}, bf16[256,2048]{1,0:T(8,128)(2,1)S(1)}, u32[]{:S(2)}, u32[]{:S(2)}) %collective-permute-start.77) | collective-permute-done | bytes 1048608 | tf_op jit(solution)/shard_map/ppermute | solution.py:353
  962.9 15.0 %collective-permute-done.83 = bf16[4,512,128]{2,1,0:T(8,128)(2,1)} collective-permute-done((bf16[4,512,128]{2,1,0:T(8,128)(2,1)}, bf16[4,512,128]{2,1,0:T(8,128)(2,1)}, u32[]{:S(2)}, u32[]{:S(2)}) %collective-permute-start.83) | collective-permute-done | bytes 524320 | tf_op jit(solution)/shard_map/ppermute | solution.py:353
  (577 shorter events, 528.2 us)
Async XLA Ops:
  34.8 64.8 %collective-permute-start.3 = (bf16[512,1024]{1,0:T(8,128)(2,1)}, bf16[512,1024]{1,0:T(8,128)(2,1)}, u32[]{:S(2)}, u32[]{:S(2)}) collective-permute-start(bf16[512,1024]{1,0:T(8,128)(2,1)} %pad_maximum_fusion.8), channel_id=1, source_target_pairs={{0,2},{1,3},{2,0},{3,1},{4,6},{5,7},{6,4},{7,5},{8,10},{9,11},{10,... | collective-permute-start | bytes 3145736 | tf_op jit(solution)/shard_map/ppermute | solution.py:353
  37.7 61.9 %collective-permute-start.5 = (bf16[4,1024,128]{2,1,0:T(8,128)(2,1)}, bf16[4,1024,128]{2,1,0:T(8,128)(2,1)}, u32[]{:S(2)}, u32[]{:S(2)}) collective-permute-start(bf16[4,1024,128]{2,1,0:T(8,128)(2,1)} %maximum_select_fusion.1), channel_id=1, source_target_pairs={{0,24},{4,28},{8,16},{12,20},{16,8},{20,12},{24,0},{28,4},{1,25},{... | collective-permute-start | bytes 3145736 | tf_op jit(solution)/shard_map/ppermute | solution.py:389
  105.2 49.1 %collective-permute-start.14 = (bf16[1024,512]{1,0:T(8,128)(2,1)S(1)}, bf16[1024,512]{1,0:T(8,128)(2,1)S(1)}, u32[]{:S(2)}, u32[]{:S(2)}) collective-permute-start(bf16[1024,512]{1,0:T(8,128)(2,1)S(1)} %maximum_select_fusion.2), channel_id=1, source_target_pairs={{0,2},{1,3},{2,0},{3,1},{4,6},{5,7},{6,4},{7,5},{8,10},{9,11},{10,... | collective-permute-start | bytes 3145736 | tf_op jit(solution)/shard_map/ppermute | solution.py:353
  190.8 50.4 %collective-permute-start.21 = (bf16[1024,512]{1,0:T(8,128)(2,1)S(1)}, bf16[1024,512]{1,0:T(8,128)(2,1)S(1)}, u32[]{:S(2)}, u32[]{:S(2)}) collective-permute-start(bf16[1024,512]{1,0:T(8,128)(2,1)S(1)} %maximum_select_fusion.3), channel_id=1, source_target_pairs={{0,24},{4,28},{8,16},{12,20},{16,8},{20,12},{24,0},{28,4},{1,25},{... | collective-permute-start | bytes 3145736 | tf_op jit(solution)/shard_map/ppermute | solution.py:389
  192.6 48.6 %collective-permute-start.20 = (bf16[1024,512]{1,0:T(8,128)(2,1)S(1)}, bf16[1024,512]{1,0:T(8,128)(2,1)}, u32[]{:S(2)}, u32[]{:S(2)}) collective-permute-start(bf16[1024,512]{1,0:T(8,128)(2,1)S(1)} %maximum_select_fusion.3), channel_id=1, source_target_pairs={{0,2},{1,3},{2,0},{3,1},{4,6},{5,7},{6,4},{7,5},{8,10},{9,11},{10,... | collective-permute-start | bytes 3145736 | tf_op jit(solution)/shard_map/ppermute | solution.py:353
  252.5 81.9 %collective-permute-start.26 = (bf16[4,1024,512]{2,1,0:T(8,128)(2,1)S(1)}, bf16[4,1024,512]{2,1,0:T(8,128)(2,1)}, u32[]{:S(2)}, u32[]{:S(2)}) collective-permute-start(bf16[4,1024,512]{2,1,0:T(8,128)(2,1)S(1)} %pad_maximum_fusion.1.refs_1_.refs_2_), channel_id=1, source_target_pairs={{0,16},{16,0},{1,17},{17,1},{2,18},{18,2},{3,19},{19,3},{4,20},{20... | collective-permute-start | bytes 12582920 | tf_op jit(solution)/shard_map/ppermute | solution.py:384
  336.8 48.6 %collective-permute-start.33 = (bf16[512,1024]{1,0:T(8,128)(2,1)S(1)}, bf16[512,1024]{1,0:T(8,128)(2,1)S(1)}, u32[]{:S(2)}, u32[]{:S(2)}) collective-permute-start(bf16[512,1024]{1,0:T(8,128)(2,1)S(1)} %maximum_select_fusion.5), channel_id=1, source_target_pairs={{0,2},{1,3},{2,0},{3,1},{4,6},{5,7},{6,4},{7,5},{8,10},{9,11},{10,... | collective-permute-start | bytes 3145736 | tf_op jit(solution)/shard_map/ppermute | solution.py:353
  336.9 48.6 %collective-permute-start.29 = (bf16[256,2048]{1,0:T(8,128)(2,1)S(1)}, bf16[256,2048]{1,0:T(8,128)(2,1)S(1)}, u32[]{:S(2)}, u32[]{:S(2)}) collective-permute-start(bf16[256,2048]{1,0:T(8,128)(2,1)S(1)} %get-tuple-element.419.refs_0_), channel_id=1, source_target_pairs={{0,4},{4,0},{8,12},{12,8},{1,5},{5,1},{9,13},{13,9},{2,6},{6,2},{1... | collective-permute-start | bytes 3145736 | tf_op jit(solution)/shard_map/ppermute | solution.py:353
  338.2 48.3 %collective-permute-start.30 = (bf16[256,2048]{1,0:T(8,128)(2,1)S(1)}, bf16[256,2048]{1,0:T(8,128)(2,1)S(1)}, u32[]{:S(2)}, u32[]{:S(2)}) collective-permute-start(bf16[256,2048]{1,0:T(8,128)(2,1)S(1)} %get-tuple-element.419.refs_0_), channel_id=1, source_target_pairs={{0,1},{1,0},{2,3},{3,2},{4,5},{5,4},{6,7},{7,6},{8,9},{9,8},{10,11... | collective-permute-start | bytes 3145736 | tf_op jit(solution)/shard_map/ppermute | solution.py:353
  598.8 51.4 %collective-permute-start.53 = (bf16[256,2048]{1,0:T(8,128)(2,1)S(1)}, bf16[256,2048]{1,0:T(8,128)(2,1)}, u32[]{:S(2)}, u32[]{:S(2)}) collective-permute-start(bf16[256,2048]{1,0:T(8,128)(2,1)S(1)} %get-tuple-element.305.refs_0_), channel_id=1, source_target_pairs={{0,2},{1,3},{2,0},{3,1},{4,6},{5,7},{6,4},{7,5},{8,10},{9,11},{10,... | collective-permute-start | bytes 3145736 | tf_op jit(solution)/shard_map/ppermute | solution.py:353
  600.1 51.4 %collective-permute-start.52 = (bf16[256,2048]{1,0:T(8,128)(2,1)S(1)}, bf16[256,2048]{1,0:T(8,128)(2,1)}, u32[]{:S(2)}, u32[]{:S(2)}) collective-permute-start(bf16[256,2048]{1,0:T(8,128)(2,1)S(1)} %get-tuple-element.305.refs_0_), channel_id=1, source_target_pairs={{0,4},{4,0},{8,12},{12,8},{1,5},{5,1},{9,13},{13,9},{2,6},{6,2},{1... | collective-permute-start | bytes 3145736 | tf_op jit(solution)/shard_map/ppermute | solution.py:353
  609.7 53.4 %collective-permute-start.57 = (bf16[512,1024]{1,0:T(8,128)(2,1)}, bf16[512,1024]{1,0:T(8,128)(2,1)}, u32[]{:S(2)}, u32[]{:S(2)}) collective-permute-start(bf16[512,1024]{1,0:T(8,128)(2,1)} %get-tuple-element.295), channel_id=1, source_target_pairs={{0,24},{4,28},{8,16},{12,20},{16,8},{20,12},{24,0},{28,4},{1,25},{... | collective-permute-start | bytes 3145736 | tf_op jit(solution)/shard_map/ppermute | solution.py:389
  694.4 59.3 %collective-permute-start.62 = (bf16[512,1024]{1,0:T(8,128)(2,1)}, bf16[512,1024]{1,0:T(8,128)(2,1)}, u32[]{:S(2)}, u32[]{:S(2)}) collective-permute-start(bf16[512,1024]{1,0:T(8,128)(2,1)} %fusion.27), channel_id=1, source_target_pairs={{0,2},{1,3},{2,0},{3,1},{4,6},{5,7},{6,4},{7,5},{8,10},{9,11},{10,... | collective-permute-start | bytes 3145736 | tf_op jit(solution)/shard_map/ppermute | solution.py:353
  705.5 48.1 %collective-permute-start.64 = (bf16[1024,512]{1,0:T(8,128)(2,1)}, bf16[1024,512]{1,0:T(8,128)(2,1)S(1)}, u32[]{:S(2)}, u32[]{:S(2)}) collective-permute-start(bf16[1024,512]{1,0:T(8,128)(2,1)} %get-tuple-element.323), channel_id=1, source_target_pairs={{0,24},{4,28},{8,16},{12,20},{16,8},{20,12},{24,0},{28,4},{1,25},{... | collective-permute-start | bytes 3145736 | tf_op jit(solution)/shard_map/ppermute | solution.py:389
  705.5 48.1 %collective-permute-start.65 = (bf16[1024,512]{1,0:T(8,128)(2,1)}, bf16[1024,512]{1,0:T(8,128)(2,1)S(1)}, u32[]{:S(2)}, u32[]{:S(2)}) collective-permute-start(bf16[1024,512]{1,0:T(8,128)(2,1)} %get-tuple-element.324), channel_id=1, source_target_pairs={{0,24},{4,28},{8,16},{12,20},{16,8},{20,12},{24,0},{28,4},{1,25},{... | collective-permute-start | bytes 3145736 | tf_op jit(solution)/shard_map/ppermute | solution.py:389
  710.8 65.3 %collective-permute-start.72 = (bf16[1024,512]{1,0:T(8,128)(2,1)}, bf16[1024,512]{1,0:T(8,128)(2,1)S(1)}, u32[]{:S(2)}, u32[]{:S(2)}) collective-permute-start(bf16[1024,512]{1,0:T(8,128)(2,1)} %get-tuple-element.332), channel_id=1, source_target_pairs={{0,24},{4,28},{8,16},{12,20},{16,8},{20,12},{24,0},{28,4},{1,25},{... | collective-permute-start | bytes 3145736 | tf_op jit(solution)/shard_map/ppermute | solution.py:389
  710.8 90.1 %collective-permute-start.71 = (bf16[1024,512]{1,0:T(8,128)(2,1)}, bf16[1024,512]{1,0:T(8,128)(2,1)}, u32[]{:S(2)}, u32[]{:S(2)}) collective-permute-start(bf16[1024,512]{1,0:T(8,128)(2,1)} %get-tuple-element.331), channel_id=1, source_target_pairs={{0,24},{4,28},{8,16},{12,20},{16,8},{20,12},{24,0},{28,4},{1,25},{... | collective-permute-start | bytes 3145736 | tf_op jit(solution)/shard_map/ppermute | solution.py:389
  756.6 75.1 %collective-permute-start.70 = (bf16[1024,512]{1,0:T(8,128)(2,1)}, bf16[1024,512]{1,0:T(8,128)(2,1)}, u32[]{:S(2)}, u32[]{:S(2)}) collective-permute-start(bf16[1024,512]{1,0:T(8,128)(2,1)} %fusion.24), channel_id=1, source_target_pairs={{0,2},{1,3},{2,0},{3,1},{4,6},{5,7},{6,4},{7,5},{8,10},{9,11},{10,... | collective-permute-start | bytes 3145736 | tf_op jit(solution)/shard_map/ppermute | solution.py:353
  756.6 75.1 %collective-permute-start.66 = (bf16[3,4,256,128]{3,2,1,0:T(8,128)(2,1)}, bf16[3,4,256,128]{3,2,1,0:T(8,128)(2,1)S(1)}, u32[]{:S(2)}, u32[]{:S(2)}) collective-permute-start(bf16[3,4,256,128]{3,2,1,0:T(8,128)(2,1)} %get-tuple-element.326), channel_id=1, source_target_pairs={{0,8},{4,12},{8,0},{12,4},{1,9},{5,13},{9,1},{13,5},{2,10},{6,14},... | collective-permute-start | bytes 2359304 | tf_op jit(solution)/shard_map/ppermute | solution.py:353
  756.7 75.0 %collective-permute-start.67 = (bf16[3,4,256,128]{3,2,1,0:T(8,128)(2,1)}, bf16[3,4,256,128]{3,2,1,0:T(8,128)(2,1)S(1)}, u32[]{:S(2)}, u32[]{:S(2)}) collective-permute-start(bf16[3,4,256,128]{3,2,1,0:T(8,128)(2,1)} %get-tuple-element.327), channel_id=1, source_target_pairs={{0,1},{1,0},{2,3},{3,2},{4,5},{5,4},{6,7},{7,6},{8,9},{9,8},{10,11... | collective-permute-start | bytes 2359304 | tf_op jit(solution)/shard_map/ppermute | solution.py:353
  776.1 55.6 %collective-permute-start.68 = (bf16[3,4,256,128]{3,2,1,0:T(8,128)(2,1)}, bf16[3,4,256,128]{3,2,1,0:T(8,128)(2,1)S(1)}, u32[]{:S(2)}, u32[]{:S(2)}) collective-permute-start(bf16[3,4,256,128]{3,2,1,0:T(8,128)(2,1)} %get-tuple-element.328), channel_id=1, source_target_pairs={{0,9},{1,8},{2,11},{3,10},{4,13},{5,12},{6,15},{7,14},{8,1},{9,0},... | collective-permute-start | bytes 2359304 | tf_op jit(solution)/shard_map/ppermute | solution.py:376
  850.6 48.0 %collective-permute-start.75 = (bf16[1024,512]{1,0:T(8,128)(2,1)}, bf16[1024,512]{1,0:T(8,128)(2,1)}, u32[]{:S(2)}, u32[]{:S(2)}) collective-permute-start(bf16[1024,512]{1,0:T(8,128)(2,1)} %fusion.23), channel_id=1, source_target_pairs={{0,2},{1,3},{2,0},{3,1},{4,6},{5,7},{6,4},{7,5},{8,10},{9,11},{10,... | collective-permute-start | bytes 3145736 | tf_op jit(solution)/shard_map/ppermute | solution.py:353
  878.8 71.6 %collective-permute-start.82 = (bf16[2,2,512,512]{3,2,1,0:T(8,128)(2,1)S(1)}, bf16[2,2,512,512]{3,2,1,0:T(8,128)(2,1)S(1)}, u32[]{:S(2)}, u32[]{:S(2)}) collective-permute-start(bf16[2,2,512,512]{3,2,1,0:T(8,128)(2,1)S(1)} %pad_maximum_fusion.7), channel_id=1, source_target_pairs={{0,16},{16,0},{1,17},{17,1},{2,18},{18,2},{3,19},{19,3},{4,20},{20... | collective-permute-start | bytes 6291464 | tf_op jit(solution)/shard_map/ppermute | solution.py:384
  901.5 48.2 %collective-permute-start.77 = (bf16[256,2048]{1,0:T(8,128)(2,1)S(1)}, bf16[256,2048]{1,0:T(8,128)(2,1)S(1)}, u32[]{:S(2)}, u32[]{:S(2)}) collective-permute-start(bf16[256,2048]{1,0:T(8,128)(2,1)S(1)} %add_convert_fusion.2), channel_id=1, source_target_pairs={{0,2},{1,3},{2,0},{3,1},{4,6},{5,7},{6,4},{7,5},{8,10},{9,11},{10,... | collective-permute-start | bytes 3145736 | tf_op jit(solution)/shard_map/ppermute | solution.py:353
  (201 other events, 3624.3 us)

commit v6 on v5

--- a/solution.py
+++ b/solution.py
@@ -1358,7 +1358,6 @@
     grad_messages = after(grad_messages, up_core, out_pair)
     gate_y1 = gate_grads.to_y(1, grad_messages)
     gate_y0 = gate_grads.to_y(0, grad_messages)
-    up_y0 = up_grads.to_y(0, grad_messages)
     up_y1 = up_grads.to_y(1, grad_messages)
     back = run_backward(
         pieces, starts, messages, grad_messages, wide_mixed, log_total, cos_wide, sin_wide
@@ -1368,7 +1367,8 @@
     own_down, send_down = to_x(down_grads.total(back), x, 1)
     down_x = flip_x(send_down)
     back = swap_slots(back)
-    back = after(back, down_x, gate_grads.high, up_y1, up_y0)
+    back = after(back, down_x, gate_grads.high, up_y1)
+    up_y0 = up_grads.to_y(0, back)
     up_grads.to_high(flip_far, back)
     own_gate, send_gate = to_x(gate_grads.total(back), x, 0)
     gate_x = flip_x(send_gate)

time: 1010 us -> 996 us (0.986)
  waiting for transfers between devices: 448 us -> 434 us
    ppermute x16, waiting for transfers between devices: 63.6 us -> 41.9 us  [flip_dp_y(): return lax.ppermute(values, ('dp', 'row'), pairs)]
    ppermute x4, waiting for transfers between devices: 29.4 us -> 47.8 us  [flip_y_near(): return lax.ppermute(values, ('row', 'col'), pairs)]
    ppermute x56, waiting for transfers between devices: 312 us -> 300 us  [flip(): return lax.ppermute(values, axis, [(i, i ^ bit) for i in range(SIDE)])]
    unnamed x270 -> x266, local copies, waits for them, and re-layouts: 45.5 us -> 45.3 us
  transfers between devices with their start and end apart: 92 -> 92, of which waited for: 40 -> 43; matrix products, arithmetic and copies ran while one was open for 12% -> 12% of each run, Pallas kernels for 22% -> 22%
where the time goes in v6:
time: 996 us; the launch traced here: 988 us
  waiting for transfers between devices  434 us (44%)
  Pallas kernels  263 us (26%)
  other arithmetic  113 us (11%)
  starting transfers between devices  104 us (10%)
  local copies, waits for them, and re-layouts  69.3 us (7%)
    ppermute x56, waiting for transfers between devices, flip(): return lax.ppermute(values, axis, [(i, i ^ bit) for i in range(SIDE)])  300 us
    ppermute x56, starting transfers between devices, flip(): return lax.ppermute(values, axis, [(i, i ^ bit) for i in range(SIDE)])  63.9 us
    ppermute x4, waiting for transfers between devices, flip_y_near(): return lax.ppermute(values, ('row', 'col'), pairs)  47.8 us
    unnamed x266, local copies, waits for them, and re-layouts  45.3 us
    ppermute x16, waiting for transfers between devices, flip_dp_y(): return lax.ppermute(values, ('dp', 'row'), pairs)  41.9 us
    pallas_call x1, Pallas kernels, run_backward(): pl.pallas_call(attention_backward, out_shape=[jax.ShapeDtypeStruct((3, 4,...  40.6 us
    pallas_call x3, Pallas kernels, run_up(): pl.pallas_call(lambda *refs: up_kernel(len(acts), *refs), grid=(width //...  35.2 us
    pallas_call x3, Pallas kernels, run_normed_two(): pl.pallas_call(lambda *refs: normed_two_kernel(kind, *refs), grid=(2,), o...  32.6 us
  transfers between devices with their start and end apart: 92, of which 43 were waited for; matrix products, arithmetic and copies ran while one was open for 12% of the time, Pallas kernels for 22%

profile of v6, /device:TPU:0, one launch (start us, length us, event | category | flops | bytes accessed | tf_op | source)
XLA Modules:
  0.0 987.9 jit_solution(2934507581019537136)
XLA Ops:
  38.7 16.5 %all-to-all-done = f32[8,8,128]{2,1,0:T(8,128)S(1)} async-done(((f32[8,8,128]{2,1,0:T(8,128)}), f32[8,8,128]{2,1,0:T(8,128)S(1)}, u32[]{:S(2)}, u32[]{:S(2)}) %all-to-all-start) | async-done | bytes 32800 | tf_op jit(solution)/shard_map/all_to_all | solution.py:510
  74.0 23.2 %all-to-all-done.1 = bf16[4,256,512]{2,1,0:T(8,128)(2,1)} async-done(((bf16[4,256,512]{2,1,0:T(8,128)(2,1)}), bf16[4,256,512]{2,1,0:T(8,128)(2,1)}, u32[]{:S(2)}, u32[]{:S(2)}) %all-to-all-start.1) | async-done | bytes 1048608 | tf_op jit(solution)/shard_map/all_to_all | solution.py:1180
  110.0 21.1 %collective-permute-done.4 = bf16[512,1024]{1,0:T(8,128)(2,1)S(1)} collective-permute-done((bf16[512,1024]{1,0:T(8,128)(2,1)}, bf16[512,1024]{1,0:T(8,128)(2,1)S(1)}, u32[]{:S(2)}, u32[]{:S(2)}) %collective-permute-start.4) | collective-permute-done | bytes 1048608 | tf_op jit(solution)/shard_map/ppermute | solution.py:353
  157.7 13.4 %collective-permute-done.10.refs_2_ = bf16[3,4,256,128]{3,2,1,0:T(8,128)(2,1)S(1)} collective-permute-done((bf16[3,4,256,128]{3,2,1,0:T(8,128)(2,1)S(1)}, bf16[3,4,256,128]{3,2,1,0:T(8,128)(2,1)S(1)}, u32[]{:S(2)}, u32[]{:S(2)}) %collective-permute-start.10) | collective-permute-done | bytes 786464 | tf_op jit(solution)/shard_map/ppermute | solution.py:353
  171.1 17.9 %collective-permute-done.11.refs_3_ = bf16[3,4,256,128]{3,2,1,0:T(8,128)(2,1)S(1)} collective-permute-done((bf16[3,4,256,128]{3,2,1,0:T(8,128)(2,1)S(1)}, bf16[3,4,256,128]{3,2,1,0:T(8,128)(2,1)S(1)}, u32[]{:S(2)}, u32[]{:S(2)}) %collective-permute-start.11) | collective-permute-done | bytes 786464 | tf_op jit(solution)/shard_map/ppermute | solution.py:376
  195.2 29.9 %shard_map.187 = (bf16[4,256,128]{2,1,0:T(8,128)(2,1)S(1)}, bf16[4,256,128]{2,1,0:T(8,128)(2,1)S(1)}, bf16[4,256,128]{2,1,0:T(8,128)(2,1)S(1)}, bf16[4,256,128]{...) custom-call(s32[16]{0:T(128)S(1)} %fusion.49.place_ref, s32[8]{0:T(128)S(1)} %convert_reduce_fusion.4.starts_ref, ...), custom_call_target="tpu_custom_call" | custom-call | flops 8589934592 | bytes 8388608 | tf_op jit(solution)/shard_map/pallas_call | solution.py:1135
  260.4 23.8 %collective-permute-done.22 = bf16[256,2048]{1,0:T(8,128)(2,1)S(1)} collective-permute-done((bf16[256,2048]{1,0:T(8,128)(2,1)S(1)}, bf16[256,2048]{1,0:T(8,128)(2,1)S(1)}, u32[]{:S(2)}, u32[]{:S(2)}) %collective-permute-start.22) | collective-permute-done | bytes 1048608 | tf_op jit(solution)/shard_map/ppermute | solution.py:353
  289.5 19.3 %collective-permute-done.23 = bf16[256,2048]{1,0:T(8,128)(2,1)S(1)} collective-permute-done((bf16[256,2048]{1,0:T(8,128)(2,1)S(1)}, bf16[256,2048]{1,0:T(8,128)(2,1)S(1)}, u32[]{:S(2)}, u32[]{:S(2)}) %collective-permute-start.23) | collective-permute-done | bytes 1048608 | tf_op jit(solution)/shard_map/ppermute | solution.py:353
  308.8 24.3 %collective-permute-done.24 = bf16[256,2048]{1,0:T(8,128)(2,1)S(1)} collective-permute-done((bf16[256,2048]{1,0:T(8,128)(2,1)S(1)}, bf16[256,2048]{1,0:T(8,128)(2,1)S(1)}, u32[]{:S(2)}, u32[]{:S(2)}) %collective-permute-start.24) | collective-permute-done | bytes 1048608 | tf_op jit(solution)/shard_map/ppermute | solution.py:353
  355.4 30.1 %collective-permute-done.33 = bf16[512,1024]{1,0:T(8,128)(2,1)S(1)} collective-permute-done((bf16[512,1024]{1,0:T(8,128)(2,1)S(1)}, bf16[512,1024]{1,0:T(8,128)(2,1)S(1)}, u32[]{:S(2)}, u32[]{:S(2)}) %collective-permute-start.33) | collective-permute-done | bytes 1048608 | tf_op jit(solution)/shard_map/ppermute | solution.py:353
  387.9 14.7 %shard_map.190 = (f32[4,512,512]{2,1,0:T(8,128)}, f32[4,512,512]{2,1,0:T(8,128)}, bf16[4,512,512]{2,1,0:T(8,128)(2,1)S(1)}) custom-call(bf16[256,2048]{1,0:T(8,128)(2,1)S(1)} %collective-permute-done.29.refs_0_.refs_1_, bf16[256,2048]{1,0:T(8,128)(2,1)S(1)} %collective-permute-done.30.refs_1_.refs_2_, bf16[4,1024,512]{2,1,0:T(8,128)(2,1)} %copy-done.79, ...), custom_call_target="tpu_custom_call" | custom-call | flops 8589934592 | bytes 16777216 | tf_op jit(solution)/shard_map/pallas_call | solution.py:739
  501.0 11.7 %shard_map.196 = (bf16[4,512,512]{2,1,0:T(8,128)(2,1)S(1)}, bf16[4,512,512]{2,1,0:T(8,128)(2,1)S(1)}) custom-call(bf16[256,2048]{1,0:T(8,128)(2,1)S(1)} %collective-permute-done.42.refs_0_.refs_4_, bf16[256,2048]{1,0:T(8,128)(2,1)} %collective-permute-done.43.refs_1_.refs_5_, f32[4,512,512]{2,1,0:T(8,128)} %get-tuple-element.257.refs_2_, ...), custom_call_target="tpu_custom_call" | custom-call | flops 4294967296 | bytes 16777216 | tf_op jit(solution)/shard_map/pallas_call | solution.py:798
  537.0 13.9 %shard_map.199 = (f32[128,2048]{1,0:T(8,128)S(1)}, bf16[128,2048]{1,0:T(8,128)(2,1)S(1)}, bf16[128,2048]{1,0:T(8,128)(2,1)S(1)}, f32[128,2048]{1,0:T(8,128)S(1)}) custom-call(bf16[4,512,512]{2,1,0:T(8,128)(2,1)S(1)} %get-tuple-element.284.refs_0_.refs_6_, bf16[4,512,512]{2,1,0:T(8,128)(2,1)} %copy-done.62, bf16[4,1024,512]{2,1,0:T(8,128)(2,1)} %copy-done.79, ...), custom_call_target="tpu_custom_call" | custom-call | flops 8589934592 | bytes 18874368 | tf_op jit(solution)/shard_map/pallas_call | solution.py:837
  564.4 14.4 %shard_map.201 = (bf16[2,2,512,1024]{3,2,1,0:T(8,128)(2,1)S(1)}, bf16[2,2,512,1024]{3,2,1,0:T(8,128)(2,1)S(1)}) custom-call(bf16[4,256,512]{2,1,0:T(8,128)(2,1)S(1)} %copy-done.44, bf16[4,512,512]{2,1,0:T(8,128)(2,1)S(1)} %copy-done.75, bf16[4,256,512]{2,1,0:T(8,128)(2,1)S(1)} %copy-done.28, bf16[256,2048]{1,0:T(8,128)(2,1)S(1)} %fusion.28.refs_0_.refs_3_, ...), custom_call_target="tpu_custom_call" | custom-call | flops 8589934592 | bytes 16777216 | tf_op jit(solution)/shard_map/pallas_call | solution.py:913
  581.8 11.6 %collective-permute-done.51 = bf16[128,2048]{1,0:T(8,128)(2,1)S(1)} collective-permute-done((bf16[128,2048]{1,0:T(8,128)(2,1)S(1)}, bf16[128,2048]{1,0:T(8,128)(2,1)S(1)}, u32[]{:S(2)}, u32[]{:S(2)}) %collective-permute-start.51) | collective-permute-done | bytes 524320 | tf_op jit(solution)/shard_map/ppermute | solution.py:353
  663.1 12.3 %collective-permute-done.56.refs_3_ = bf16[256,2048]{1,0:T(8,128)(2,1)S(1)} collective-permute-done((bf16[256,2048]{1,0:T(8,128)(2,1)}, bf16[256,2048]{1,0:T(8,128)(2,1)S(1)}, u32[]{:S(2)}, u32[]{:S(2)}) %collective-permute-start.56) | collective-permute-done | bytes 1048608 | tf_op jit(solution)/shard_map/ppermute | solution.py:353
  710.8 40.6 %shard_map.206 = (bf16[3,4,256,128]{3,2,1,0:T(8,128)(2,1)S(1)}, bf16[3,4,256,128]{3,2,1,0:T(8,128)(2,1)}, bf16[3,4,256,128]{3,2,1,0:T(8,128)(2,1)}, bf16[3,4,256,128]{3,2,1,0:T(8,128)(2,1)}) custom-call(s32[16]{0:T(128)S(1)} %fusion.49.place_ref, s32[8]{0:T(128)S(1)} %convert_reduce_fusion.4.starts_ref, bf16[3,4,256,128]{3,2,1,0:T(8,128)(2,1)} %copy-done.76, ...), custom_call_target="tpu_custom_call" | custom-call | flops 21474836480 | bytes 16777216 | tf_op jit(solution)/shard_map/pallas_call | solution.py:1160
  763.7 14.0 %collective-permute-done.71 = bf16[1024,512]{1,0:T(8,128)(2,1)} collective-permute-done((bf16[1024,512]{1,0:T(8,128)(2,1)}, bf16[1024,512]{1,0:T(8,128)(2,1)}, u32[]{:S(2)}, u32[]{:S(2)}) %collective-permute-start.71) | collective-permute-done | bytes 1048608 | tf_op jit(solution)/shard_map/ppermute | solution.py:389
  777.8 12.2 %collective-permute-done.69 = bf16[512,512]{1,0:T(8,128)(2,1)S(1)} collective-permute-done((bf16[512,512]{1,0:T(8,128)(2,1)S(1)}, bf16[512,512]{1,0:T(8,128)(2,1)S(1)}, u32[]{:S(2)}, u32[]{:S(2)}) %collective-permute-start.69) | collective-permute-done | bytes 524320 | tf_op jit(solution)/shard_map/ppermute | solution.py:353
  797.2 18.4 %collective-permute-done.68.refs_7_.refs_3_ = bf16[3,4,256,128]{3,2,1,0:T(8,128)(2,1)S(1)} collective-permute-done((bf16[3,4,256,128]{3,2,1,0:T(8,128)(2,1)}, bf16[3,4,256,128]{3,2,1,0:T(8,128)(2,1)S(1)}, u32[]{:S(2)}, u32[]{:S(2)}) %collective-permute-start.68) | collective-permute-done | bytes 786464 | tf_op jit(solution)/shard_map/ppermute | solution.py:376
  868.0 15.5 %collective-permute-done.74 = bf16[1024,512]{1,0:T(8,128)(2,1)} collective-permute-done((bf16[1024,512]{1,0:T(8,128)(2,1)}, bf16[1024,512]{1,0:T(8,128)(2,1)}, u32[]{:S(2)}, u32[]{:S(2)}) %collective-permute-start.74) | collective-permute-done | bytes 1048608 | tf_op jit(solution)/shard_map/ppermute | solution.py:353
  895.3 12.3 %collective-permute-done.79 = bf16[4,1024,128]{2,1,0:T(8,128)(2,1)S(1)} collective-permute-done((bf16[4,1024,128]{2,1,0:T(8,128)(2,1)S(1)}, bf16[4,1024,128]{2,1,0:T(8,128)(2,1)S(1)}, u32[]{:S(2)}, u32[]{:S(2)}) %collective-permute-start.79) | collective-permute-done | bytes 1048608 | tf_op jit(solution)/shard_map/ppermute | solution.py:353
  909.9 26.5 %collective-permute-done.76 = bf16[256,2048]{1,0:T(8,128)(2,1)S(1)} collective-permute-done((bf16[256,2048]{1,0:T(8,128)(2,1)S(1)}, bf16[256,2048]{1,0:T(8,128)(2,1)S(1)}, u32[]{:S(2)}, u32[]{:S(2)}) %collective-permute-start.76) | collective-permute-done | bytes 1048608 | tf_op jit(solution)/shard_map/ppermute | solution.py:353
  949.5 15.0 %collective-permute-done.82 = bf16[4,512,128]{2,1,0:T(8,128)(2,1)} collective-permute-done((bf16[4,512,128]{2,1,0:T(8,128)(2,1)}, bf16[4,512,128]{2,1,0:T(8,128)(2,1)}, u32[]{:S(2)}, u32[]{:S(2)}) %collective-permute-start.82) | collective-permute-done | bytes 524320 | tf_op jit(solution)/shard_map/ppermute | solution.py:353
  (573 shorter events, 529.4 us)
Async XLA Ops:
  34.8 64.8 %collective-permute-start.3 = (bf16[512,1024]{1,0:T(8,128)(2,1)}, bf16[512,1024]{1,0:T(8,128)(2,1)}, u32[]{:S(2)}, u32[]{:S(2)}) collective-permute-start(bf16[512,1024]{1,0:T(8,128)(2,1)} %pad_maximum_fusion.8), channel_id=1, source_target_pairs={{0,2},{1,3},{2,0},{3,1},{4,6},{5,7},{6,4},{7,5},{8,10},{9,11},{10,... | collective-permute-start | bytes 3145736 | tf_op jit(solution)/shard_map/ppermute | solution.py:353
  37.7 61.9 %collective-permute-start.5 = (bf16[4,1024,128]{2,1,0:T(8,128)(2,1)}, bf16[4,1024,128]{2,1,0:T(8,128)(2,1)}, u32[]{:S(2)}, u32[]{:S(2)}) collective-permute-start(bf16[4,1024,128]{2,1,0:T(8,128)(2,1)} %maximum_select_fusion.1), channel_id=1, source_target_pairs={{0,24},{4,28},{8,16},{12,20},{16,8},{20,12},{24,0},{28,4},{1,25},{... | collective-permute-start | bytes 3145736 | tf_op jit(solution)/shard_map/ppermute | solution.py:389
  105.2 49.1 %collective-permute-start.14 = (bf16[1024,512]{1,0:T(8,128)(2,1)S(1)}, bf16[1024,512]{1,0:T(8,128)(2,1)S(1)}, u32[]{:S(2)}, u32[]{:S(2)}) collective-permute-start(bf16[1024,512]{1,0:T(8,128)(2,1)S(1)} %maximum_select_fusion.2), channel_id=1, source_target_pairs={{0,2},{1,3},{2,0},{3,1},{4,6},{5,7},{6,4},{7,5},{8,10},{9,11},{10,... | collective-permute-start | bytes 3145736 | tf_op jit(solution)/shard_map/ppermute | solution.py:353
  190.8 50.4 %collective-permute-start.21 = (bf16[1024,512]{1,0:T(8,128)(2,1)S(1)}, bf16[1024,512]{1,0:T(8,128)(2,1)S(1)}, u32[]{:S(2)}, u32[]{:S(2)}) collective-permute-start(bf16[1024,512]{1,0:T(8,128)(2,1)S(1)} %maximum_select_fusion.3), channel_id=1, source_target_pairs={{0,24},{4,28},{8,16},{12,20},{16,8},{20,12},{24,0},{28,4},{1,25},{... | collective-permute-start | bytes 3145736 | tf_op jit(solution)/shard_map/ppermute | solution.py:389
  192.6 48.6 %collective-permute-start.20 = (bf16[1024,512]{1,0:T(8,128)(2,1)S(1)}, bf16[1024,512]{1,0:T(8,128)(2,1)}, u32[]{:S(2)}, u32[]{:S(2)}) collective-permute-start(bf16[1024,512]{1,0:T(8,128)(2,1)S(1)} %maximum_select_fusion.3), channel_id=1, source_target_pairs={{0,2},{1,3},{2,0},{3,1},{4,6},{5,7},{6,4},{7,5},{8,10},{9,11},{10,... | collective-permute-start | bytes 3145736 | tf_op jit(solution)/shard_map/ppermute | solution.py:353
  252.5 81.9 %collective-permute-start.26 = (bf16[4,1024,512]{2,1,0:T(8,128)(2,1)S(1)}, bf16[4,1024,512]{2,1,0:T(8,128)(2,1)}, u32[]{:S(2)}, u32[]{:S(2)}) collective-permute-start(bf16[4,1024,512]{2,1,0:T(8,128)(2,1)S(1)} %pad_maximum_fusion.1.refs_1_.refs_2_), channel_id=1, source_target_pairs={{0,16},{16,0},{1,17},{17,1},{2,18},{18,2},{3,19},{19,3},{4,20},{20... | collective-permute-start | bytes 12582920 | tf_op jit(solution)/shard_map/ppermute | solution.py:384
  285.3 47.9 %collective-permute-start.24 = (bf16[256,2048]{1,0:T(8,128)(2,1)S(1)}, bf16[256,2048]{1,0:T(8,128)(2,1)S(1)}, u32[]{:S(2)}, u32[]{:S(2)}) collective-permute-start(bf16[256,2048]{1,0:T(8,128)(2,1)S(1)} %add_convert_fusion.9), channel_id=1, source_target_pairs={{0,2},{1,3},{2,0},{3,1},{4,6},{5,7},{6,4},{7,5},{8,10},{9,11},{10,... | collective-permute-start | bytes 3145736 | tf_op jit(solution)/shard_map/ppermute | solution.py:353
  287.0 47.5 %collective-permute-start.27 = (bf16[512,1024]{1,0:T(8,128)(2,1)S(1)}, bf16[512,1024]{1,0:T(8,128)(2,1)S(1)}, u32[]{:S(2)}, u32[]{:S(2)}) collective-permute-start(bf16[512,1024]{1,0:T(8,128)(2,1)S(1)} %maximum_select_fusion.5), channel_id=1, source_target_pairs={{0,24},{4,28},{8,16},{12,20},{16,8},{20,12},{24,0},{28,4},{1,25},{... | collective-permute-start | bytes 3145736 | tf_op jit(solution)/shard_map/ppermute | solution.py:389
  336.8 48.6 %collective-permute-start.33 = (bf16[512,1024]{1,0:T(8,128)(2,1)S(1)}, bf16[512,1024]{1,0:T(8,128)(2,1)S(1)}, u32[]{:S(2)}, u32[]{:S(2)}) collective-permute-start(bf16[512,1024]{1,0:T(8,128)(2,1)S(1)} %maximum_select_fusion.5), channel_id=1, source_target_pairs={{0,2},{1,3},{2,0},{3,1},{4,6},{5,7},{6,4},{7,5},{8,10},{9,11},{10,... | collective-permute-start | bytes 3145736 | tf_op jit(solution)/shard_map/ppermute | solution.py:353
  336.9 48.5 %collective-permute-start.29 = (bf16[256,2048]{1,0:T(8,128)(2,1)S(1)}, bf16[256,2048]{1,0:T(8,128)(2,1)S(1)}, u32[]{:S(2)}, u32[]{:S(2)}) collective-permute-start(bf16[256,2048]{1,0:T(8,128)(2,1)S(1)} %get-tuple-element.419.refs_0_), channel_id=1, source_target_pairs={{0,4},{4,0},{8,12},{12,8},{1,5},{5,1},{9,13},{13,9},{2,6},{6,2},{1... | collective-permute-start | bytes 3145736 | tf_op jit(solution)/shard_map/ppermute | solution.py:353
  338.2 48.3 %collective-permute-start.30 = (bf16[256,2048]{1,0:T(8,128)(2,1)S(1)}, bf16[256,2048]{1,0:T(8,128)(2,1)S(1)}, u32[]{:S(2)}, u32[]{:S(2)}) collective-permute-start(bf16[256,2048]{1,0:T(8,128)(2,1)S(1)} %get-tuple-element.419.refs_0_), channel_id=1, source_target_pairs={{0,1},{1,0},{2,3},{3,2},{4,5},{5,4},{6,7},{7,6},{8,9},{9,8},{10,11... | collective-permute-start | bytes 3145736 | tf_op jit(solution)/shard_map/ppermute | solution.py:353
  598.7 51.5 %collective-permute-start.53 = (bf16[256,2048]{1,0:T(8,128)(2,1)S(1)}, bf16[256,2048]{1,0:T(8,128)(2,1)}, u32[]{:S(2)}, u32[]{:S(2)}) collective-permute-start(bf16[256,2048]{1,0:T(8,128)(2,1)S(1)} %get-tuple-element.305.refs_0_), channel_id=1, source_target_pairs={{0,2},{1,3},{2,0},{3,1},{4,6},{5,7},{6,4},{7,5},{8,10},{9,11},{10,... | collective-permute-start | bytes 3145736 | tf_op jit(solution)/shard_map/ppermute | solution.py:353
  600.1 51.4 %collective-permute-start.52 = (bf16[256,2048]{1,0:T(8,128)(2,1)S(1)}, bf16[256,2048]{1,0:T(8,128)(2,1)}, u32[]{:S(2)}, u32[]{:S(2)}) collective-permute-start(bf16[256,2048]{1,0:T(8,128)(2,1)S(1)} %get-tuple-element.305.refs_0_), channel_id=1, source_target_pairs={{0,4},{4,0},{8,12},{12,8},{1,5},{5,1},{9,13},{13,9},{2,6},{6,2},{1... | collective-permute-start | bytes 3145736 | tf_op jit(solution)/shard_map/ppermute | solution.py:353
  605.1 45.0 %all-to-all-start.3 = ((bf16[256,4,512]{2,0,1:T(8,128)(2,1)}), bf16[256,4,512]{2,0,1:T(8,128)(2,1)}, u32[]{:S(2)}, u32[]{:S(2)}) async-start(bf16[256,4,512]{2,0,1:T(8,128)(2,1)} %bitcast.231), calls=%async_computation.3 | async-start | bytes 2097152 | tf_op jit(solution)/shard_map/all_to_all | solution.py:1184
  609.6 53.4 %collective-permute-start.57 = (bf16[512,1024]{1,0:T(8,128)(2,1)}, bf16[512,1024]{1,0:T(8,128)(2,1)}, u32[]{:S(2)}, u32[]{:S(2)}) collective-permute-start(bf16[512,1024]{1,0:T(8,128)(2,1)} %get-tuple-element.295), channel_id=1, source_target_pairs={{0,24},{4,28},{8,16},{12,20},{16,8},{20,12},{24,0},{28,4},{1,25},{... | collective-permute-start | bytes 3145736 | tf_op jit(solution)/shard_map/ppermute | solution.py:389
  694.3 57.1 %collective-permute-start.62 = (bf16[512,1024]{1,0:T(8,128)(2,1)}, bf16[512,1024]{1,0:T(8,128)(2,1)S(1)}, u32[]{:S(2)}, u32[]{:S(2)}) collective-permute-start(bf16[512,1024]{1,0:T(8,128)(2,1)} %fusion.27), channel_id=1, source_target_pairs={{0,2},{1,3},{2,0},{3,1},{4,6},{5,7},{6,4},{7,5},{8,10},{9,11},{10,... | collective-permute-start | bytes 3145736 | tf_op jit(solution)/shard_map/ppermute | solution.py:353
  705.5 45.9 %collective-permute-start.64 = (bf16[1024,512]{1,0:T(8,128)(2,1)}, bf16[1024,512]{1,0:T(8,128)(2,1)S(1)}, u32[]{:S(2)}, u32[]{:S(2)}) collective-permute-start(bf16[1024,512]{1,0:T(8,128)(2,1)} %get-tuple-element.323), channel_id=1, source_target_pairs={{0,24},{4,28},{8,16},{12,20},{16,8},{20,12},{24,0},{28,4},{1,25},{... | collective-permute-start | bytes 3145736 | tf_op jit(solution)/shard_map/ppermute | solution.py:389
  705.5 48.1 %collective-permute-start.65 = (bf16[1024,512]{1,0:T(8,128)(2,1)}, bf16[1024,512]{1,0:T(8,128)(2,1)S(1)}, u32[]{:S(2)}, u32[]{:S(2)}) collective-permute-start(bf16[1024,512]{1,0:T(8,128)(2,1)} %get-tuple-element.324), channel_id=1, source_target_pairs={{0,24},{4,28},{8,16},{12,20},{16,8},{20,12},{24,0},{28,4},{1,25},{... | collective-permute-start | bytes 3145736 | tf_op jit(solution)/shard_map/ppermute | solution.py:389
  710.7 67.0 %collective-permute-start.71 = (bf16[1024,512]{1,0:T(8,128)(2,1)}, bf16[1024,512]{1,0:T(8,128)(2,1)}, u32[]{:S(2)}, u32[]{:S(2)}) collective-permute-start(bf16[1024,512]{1,0:T(8,128)(2,1)} %get-tuple-element.331), channel_id=1, source_target_pairs={{0,24},{4,28},{8,16},{12,20},{16,8},{20,12},{24,0},{28,4},{1,25},{... | collective-permute-start | bytes 3145736 | tf_op jit(solution)/shard_map/ppermute | solution.py:389
  756.2 59.5 %collective-permute-start.70 = (bf16[1024,512]{1,0:T(8,128)(2,1)}, bf16[1024,512]{1,0:T(8,128)(2,1)}, u32[]{:S(2)}, u32[]{:S(2)}) collective-permute-start(bf16[1024,512]{1,0:T(8,128)(2,1)} %fusion.24), channel_id=1, source_target_pairs={{0,2},{1,3},{2,0},{3,1},{4,6},{5,7},{6,4},{7,5},{8,10},{9,11},{10,... | collective-permute-start | bytes 3145736 | tf_op jit(solution)/shard_map/ppermute | solution.py:353
  758.2 57.4 %collective-permute-start.68 = (bf16[3,4,256,128]{3,2,1,0:T(8,128)(2,1)}, bf16[3,4,256,128]{3,2,1,0:T(8,128)(2,1)S(1)}, u32[]{:S(2)}, u32[]{:S(2)}) collective-permute-start(bf16[3,4,256,128]{3,2,1,0:T(8,128)(2,1)} %get-tuple-element.328), channel_id=1, source_target_pairs={{0,9},{1,8},{2,11},{3,10},{4,13},{5,12},{6,15},{7,14},{8,1},{9,0},... | collective-permute-start | bytes 2359304 | tf_op jit(solution)/shard_map/ppermute | solution.py:376
  835.1 48.4 %collective-permute-start.74 = (bf16[1024,512]{1,0:T(8,128)(2,1)}, bf16[1024,512]{1,0:T(8,128)(2,1)}, u32[]{:S(2)}, u32[]{:S(2)}) collective-permute-start(bf16[1024,512]{1,0:T(8,128)(2,1)} %fusion.23), channel_id=1, source_target_pairs={{0,2},{1,3},{2,0},{3,1},{4,6},{5,7},{6,4},{7,5},{8,10},{9,11},{10,... | collective-permute-start | bytes 3145736 | tf_op jit(solution)/shard_map/ppermute | solution.py:353
  863.2 73.8 %collective-permute-start.81 = (bf16[2,2,512,512]{3,2,1,0:T(8,128)(2,1)S(1)}, bf16[2,2,512,512]{3,2,1,0:T(8,128)(2,1)S(1)}, u32[]{:S(2)}, u32[]{:S(2)}) collective-permute-start(bf16[2,2,512,512]{3,2,1,0:T(8,128)(2,1)S(1)} %pad_maximum_fusion.7), channel_id=1, source_target_pairs={{0,16},{16,0},{1,17},{17,1},{2,18},{18,2},{3,19},{19,3},{4,20},{20... | collective-permute-start | bytes 6291464 | tf_op jit(solution)/shard_map/ppermute | solution.py:384
  887.6 48.7 %collective-permute-start.76 = (bf16[256,2048]{1,0:T(8,128)(2,1)S(1)}, bf16[256,2048]{1,0:T(8,128)(2,1)S(1)}, u32[]{:S(2)}, u32[]{:S(2)}) collective-permute-start(bf16[256,2048]{1,0:T(8,128)(2,1)S(1)} %add_convert_fusion.3), channel_id=1, source_target_pairs={{0,2},{1,3},{2,0},{3,1},{4,6},{5,7},{6,4},{7,5},{8,10},{9,11},{10,... | collective-permute-start | bytes 3145736 | tf_op jit(solution)/shard_map/ppermute | solution.py:353
  (199 other events, 3598.8 us)

commit v7 on v6

--- a/solution.py
+++ b/solution.py
@@ -1385,7 +1385,7 @@
     first_theirs = flip_dp(after(first_mine, head_y1))
     normed_grad = after(normed_grad, head_y0, head_grads.high, first_theirs)
     input_gradient = middle_grad + local_norm_backward(normed_grad, normed, inverse_one)
-    own_head, send_head = to_x(head_grads.total(normed_grad), x, 1)
+    own_head, send_head = to_x(head_grads.total(), x, 1)
     own_up, send_up = to_x(up_grads.total(normed_grad), x, 0)
     head_x = flip_x(send_head)
     last_mine = pair_up(own_up, flip_x(send_up), x)

time: 996 us -> 983 us (0.987)
  waiting for transfers between devices: 434 us -> 420 us
    ppermute x56, waiting for transfers between devices: 300 us -> 284 us  [flip(): return lax.ppermute(values, axis, [(i, i ^ bit) for i in range(SIDE)])]
    unnamed x266 -> x264, local copies, waits for them, and re-layouts: 45.3 us -> 46.6 us
  transfers between devices with their start and end apart: 92 -> 92, of which waited for: 43 -> 41; matrix products, arithmetic and copies ran while one was open for 12% -> 13% of each run, Pallas kernels for 22% -> 22%
where the time goes in v7:
time: 983 us; the launch traced here: 975 us
  waiting for transfers between devices  420 us (43%)
  Pallas kernels  264 us (27%)
  other arithmetic  113 us (11%)
  starting transfers between devices  103 us (10%)
  local copies, waits for them, and re-layouts  69.6 us (7%)
    ppermute x56, waiting for transfers between devices, flip(): return lax.ppermute(values, axis, [(i, i ^ bit) for i in range(SIDE)])  284 us
    ppermute x56, starting transfers between devices, flip(): return lax.ppermute(values, axis, [(i, i ^ bit) for i in range(SIDE)])  63.4 us
    ppermute x4, waiting for transfers between devices, flip_y_near(): return lax.ppermute(values, ('row', 'col'), pairs)  47.9 us
    unnamed x264, local copies, waits for them, and re-layouts  46.6 us
    pallas_call x1, Pallas kernels, run_backward(): pl.pallas_call(attention_backward, out_shape=[jax.ShapeDtypeStruct((3, 4,...  41.1 us
    ppermute x16, waiting for transfers between devices, flip_dp_y(): return lax.ppermute(values, ('dp', 'row'), pairs)  40.7 us
    pallas_call x3, Pallas kernels, run_up(): pl.pallas_call(lambda *refs: up_kernel(len(acts), *refs), grid=(width //...  35.3 us
    pallas_call x3, Pallas kernels, run_normed_two(): pl.pallas_call(lambda *refs: normed_two_kernel(kind, *refs), grid=(2,), o...  32.6 us
  transfers between devices with their start and end apart: 92, of which 41 were waited for; matrix products, arithmetic and copies ran while one was open for 13% of the time, Pallas kernels for 22%

profile of v7, /device:TPU:0, one launch (start us, length us, event | category | flops | bytes accessed | tf_op | source)
XLA Modules:
  0.0 974.7 jit_solution(6270248477706676470)
XLA Ops:
  38.7 16.5 %all-to-all-done = f32[8,8,128]{2,1,0:T(8,128)S(1)} async-done(((f32[8,8,128]{2,1,0:T(8,128)}), f32[8,8,128]{2,1,0:T(8,128)S(1)}, u32[]{:S(2)}, u32[]{:S(2)}) %all-to-all-start) | async-done | bytes 32800 | tf_op jit(solution)/shard_map/all_to_all | solution.py:510
  74.0 23.2 %all-to-all-done.1 = bf16[4,256,512]{2,1,0:T(8,128)(2,1)} async-done(((bf16[4,256,512]{2,1,0:T(8,128)(2,1)}), bf16[4,256,512]{2,1,0:T(8,128)(2,1)}, u32[]{:S(2)}, u32[]{:S(2)}) %all-to-all-start.1) | async-done | bytes 1048608 | tf_op jit(solution)/shard_map/all_to_all | solution.py:1180
  110.0 21.1 %collective-permute-done.4 = bf16[512,1024]{1,0:T(8,128)(2,1)S(1)} collective-permute-done((bf16[512,1024]{1,0:T(8,128)(2,1)}, bf16[512,1024]{1,0:T(8,128)(2,1)S(1)}, u32[]{:S(2)}, u32[]{:S(2)}) %collective-permute-start.4) | collective-permute-done | bytes 1048608 | tf_op jit(solution)/shard_map/ppermute | solution.py:353
  157.7 13.4 %collective-permute-done.10.refs_2_ = bf16[3,4,256,128]{3,2,1,0:T(8,128)(2,1)S(1)} collective-permute-done((bf16[3,4,256,128]{3,2,1,0:T(8,128)(2,1)S(1)}, bf16[3,4,256,128]{3,2,1,0:T(8,128)(2,1)S(1)}, u32[]{:S(2)}, u32[]{:S(2)}) %collective-permute-start.10) | collective-permute-done | bytes 786464 | tf_op jit(solution)/shard_map/ppermute | solution.py:353
  171.1 17.9 %collective-permute-done.11.refs_3_ = bf16[3,4,256,128]{3,2,1,0:T(8,128)(2,1)S(1)} collective-permute-done((bf16[3,4,256,128]{3,2,1,0:T(8,128)(2,1)S(1)}, bf16[3,4,256,128]{3,2,1,0:T(8,128)(2,1)S(1)}, u32[]{:S(2)}, u32[]{:S(2)}) %collective-permute-start.11) | collective-permute-done | bytes 786464 | tf_op jit(solution)/shard_map/ppermute | solution.py:376
  195.2 30.2 %shard_map.187 = (bf16[4,256,128]{2,1,0:T(8,128)(2,1)S(1)}, bf16[4,256,128]{2,1,0:T(8,128)(2,1)S(1)}, bf16[4,256,128]{2,1,0:T(8,128)(2,1)S(1)}, bf16[4,256,128]{...) custom-call(s32[16]{0:T(128)S(1)} %fusion.49.place_ref, s32[8]{0:T(128)S(1)} %convert_reduce_fusion.4.starts_ref, ...), custom_call_target="tpu_custom_call" | custom-call | flops 8589934592 | bytes 8388608 | tf_op jit(solution)/shard_map/pallas_call | solution.py:1135
  260.4 23.8 %collective-permute-done.22 = bf16[256,2048]{1,0:T(8,128)(2,1)S(1)} collective-permute-done((bf16[256,2048]{1,0:T(8,128)(2,1)S(1)}, bf16[256,2048]{1,0:T(8,128)(2,1)S(1)}, u32[]{:S(2)}, u32[]{:S(2)}) %collective-permute-start.22) | collective-permute-done | bytes 1048608 | tf_op jit(solution)/shard_map/ppermute | solution.py:353
  289.5 19.3 %collective-permute-done.23 = bf16[256,2048]{1,0:T(8,128)(2,1)S(1)} collective-permute-done((bf16[256,2048]{1,0:T(8,128)(2,1)S(1)}, bf16[256,2048]{1,0:T(8,128)(2,1)S(1)}, u32[]{:S(2)}, u32[]{:S(2)}) %collective-permute-start.23) | collective-permute-done | bytes 1048608 | tf_op jit(solution)/shard_map/ppermute | solution.py:353
  308.8 24.3 %collective-permute-done.24 = bf16[256,2048]{1,0:T(8,128)(2,1)S(1)} collective-permute-done((bf16[256,2048]{1,0:T(8,128)(2,1)S(1)}, bf16[256,2048]{1,0:T(8,128)(2,1)S(1)}, u32[]{:S(2)}, u32[]{:S(2)}) %collective-permute-start.24) | collective-permute-done | bytes 1048608 | tf_op jit(solution)/shard_map/ppermute | solution.py:353
  355.4 30.1 %collective-permute-done.33 = bf16[512,1024]{1,0:T(8,128)(2,1)S(1)} collective-permute-done((bf16[512,1024]{1,0:T(8,128)(2,1)S(1)}, bf16[512,1024]{1,0:T(8,128)(2,1)S(1)}, u32[]{:S(2)}, u32[]{:S(2)}) %collective-permute-start.33) | collective-permute-done | bytes 1048608 | tf_op jit(solution)/shard_map/ppermute | solution.py:353
  387.9 14.7 %shard_map.190 = (f32[4,512,512]{2,1,0:T(8,128)}, f32[4,512,512]{2,1,0:T(8,128)}, bf16[4,512,512]{2,1,0:T(8,128)(2,1)S(1)}) custom-call(bf16[256,2048]{1,0:T(8,128)(2,1)S(1)} %collective-permute-done.29.refs_0_.refs_1_, bf16[256,2048]{1,0:T(8,128)(2,1)S(1)} %collective-permute-done.30.refs_1_.refs_2_, bf16[4,1024,512]{2,1,0:T(8,128)(2,1)} %copy-done.79, ...), custom_call_target="tpu_custom_call" | custom-call | flops 8589934592 | bytes 16777216 | tf_op jit(solution)/shard_map/pallas_call | solution.py:739
  501.0 11.7 %shard_map.196 = (bf16[4,512,512]{2,1,0:T(8,128)(2,1)S(1)}, bf16[4,512,512]{2,1,0:T(8,128)(2,1)S(1)}) custom-call(bf16[256,2048]{1,0:T(8,128)(2,1)S(1)} %collective-permute-done.42.refs_0_.refs_4_, bf16[256,2048]{1,0:T(8,128)(2,1)} %collective-permute-done.43.refs_1_.refs_5_, f32[4,512,512]{2,1,0:T(8,128)} %get-tuple-element.256.refs_2_, ...), custom_call_target="tpu_custom_call" | custom-call | flops 4294967296 | bytes 16777216 | tf_op jit(solution)/shard_map/pallas_call | solution.py:798
  536.9 13.9 %shard_map.199 = (f32[128,2048]{1,0:T(8,128)S(1)}, bf16[128,2048]{1,0:T(8,128)(2,1)S(1)}, bf16[128,2048]{1,0:T(8,128)(2,1)S(1)}, f32[128,2048]{1,0:T(8,128)S(1)}) custom-call(bf16[4,512,512]{2,1,0:T(8,128)(2,1)S(1)} %get-tuple-element.283.refs_0_.refs_6_, bf16[4,512,512]{2,1,0:T(8,128)(2,1)} %copy-done.62, bf16[4,1024,512]{2,1,0:T(8,128)(2,1)} %copy-done.79, ...), custom_call_target="tpu_custom_call" | custom-call | flops 8589934592 | bytes 18874368 | tf_op jit(solution)/shard_map/pallas_call | solution.py:837
  564.4 14.4 %shard_map.201 = (bf16[2,2,512,1024]{3,2,1,0:T(8,128)(2,1)S(1)}, bf16[2,2,512,1024]{3,2,1,0:T(8,128)(2,1)S(1)}) custom-call(bf16[4,256,512]{2,1,0:T(8,128)(2,1)S(1)} %copy-done.44, bf16[4,512,512]{2,1,0:T(8,128)(2,1)S(1)} %copy-done.75, bf16[4,256,512]{2,1,0:T(8,128)(2,1)S(1)} %copy-done.28, bf16[256,2048]{1,0:T(8,128)(2,1)S(1)} %fusion.28.refs_0_.refs_3_, ...), custom_call_target="tpu_custom_call" | custom-call | flops 8589934592 | bytes 16777216 | tf_op jit(solution)/shard_map/pallas_call | solution.py:913
  581.8 11.6 %collective-permute-done.51 = bf16[128,2048]{1,0:T(8,128)(2,1)S(1)} collective-permute-done((bf16[128,2048]{1,0:T(8,128)(2,1)S(1)}, bf16[128,2048]{1,0:T(8,128)(2,1)S(1)}, u32[]{:S(2)}, u32[]{:S(2)}) %collective-permute-start.51) | collective-permute-done | bytes 524320 | tf_op jit(solution)/shard_map/ppermute | solution.py:353
  651.5 11.6 %collective-permute-done.57 = bf16[512,1024]{1,0:T(8,128)(2,1)} collective-permute-done((bf16[512,1024]{1,0:T(8,128)(2,1)}, bf16[512,1024]{1,0:T(8,128)(2,1)}, u32[]{:S(2)}, u32[]{:S(2)}) %collective-permute-start.57) | collective-permute-done | bytes 1048608 | tf_op jit(solution)/shard_map/ppermute | solution.py:389
  663.0 12.4 %collective-permute-done.56.refs_3_ = bf16[256,2048]{1,0:T(8,128)(2,1)S(1)} collective-permute-done((bf16[256,2048]{1,0:T(8,128)(2,1)}, bf16[256,2048]{1,0:T(8,128)(2,1)S(1)}, u32[]{:S(2)}, u32[]{:S(2)}) %collective-permute-start.56) | collective-permute-done | bytes 1048608 | tf_op jit(solution)/shard_map/ppermute | solution.py:353
  710.7 41.1 %shard_map.206 = (bf16[3,4,256,128]{3,2,1,0:T(8,128)(2,1)S(1)}, bf16[3,4,256,128]{3,2,1,0:T(8,128)(2,1)}, bf16[3,4,256,128]{3,2,1,0:T(8,128)(2,1)}, bf16[3,4,256,128]{3,2,1,0:T(8,128)(2,1)}) custom-call(s32[16]{0:T(128)S(1)} %fusion.49.place_ref, s32[8]{0:T(128)S(1)} %convert_reduce_fusion.4.starts_ref, bf16[3,4,256,128]{3,2,1,0:T(8,128)(2,1)} %copy-done.76, ...), custom_call_target="tpu_custom_call" | custom-call | flops 21474836480 | bytes 16777216 | tf_op jit(solution)/shard_map/pallas_call | solution.py:1160
  763.7 14.0 %collective-permute-done.71 = bf16[1024,512]{1,0:T(8,128)(2,1)} collective-permute-done((bf16[1024,512]{1,0:T(8,128)(2,1)}, bf16[1024,512]{1,0:T(8,128)(2,1)}, u32[]{:S(2)}, u32[]{:S(2)}) %collective-permute-start.71) | collective-permute-done | bytes 1048608 | tf_op jit(solution)/shard_map/ppermute | solution.py:389
  777.7 12.2 %collective-permute-done.69 = bf16[512,512]{1,0:T(8,128)(2,1)S(1)} collective-permute-done((bf16[512,512]{1,0:T(8,128)(2,1)S(1)}, bf16[512,512]{1,0:T(8,128)(2,1)S(1)}, u32[]{:S(2)}, u32[]{:S(2)}) %collective-permute-start.69) | collective-permute-done | bytes 524320 | tf_op jit(solution)/shard_map/ppermute | solution.py:353
  797.2 18.5 %collective-permute-done.68.refs_7_.refs_3_ = bf16[3,4,256,128]{3,2,1,0:T(8,128)(2,1)S(1)} collective-permute-done((bf16[3,4,256,128]{3,2,1,0:T(8,128)(2,1)}, bf16[3,4,256,128]{3,2,1,0:T(8,128)(2,1)S(1)}, u32[]{:S(2)}, u32[]{:S(2)}) %collective-permute-start.68) | collective-permute-done | bytes 786464 | tf_op jit(solution)/shard_map/ppermute | solution.py:376
  868.1 15.5 %collective-permute-done.74 = bf16[1024,512]{1,0:T(8,128)(2,1)} collective-permute-done((bf16[1024,512]{1,0:T(8,128)(2,1)}, bf16[1024,512]{1,0:T(8,128)(2,1)}, u32[]{:S(2)}, u32[]{:S(2)}) %collective-permute-start.74) | collective-permute-done | bytes 1048608 | tf_op jit(solution)/shard_map/ppermute | solution.py:353
  894.7 13.0 %collective-permute-done.79 = bf16[4,1024,128]{2,1,0:T(8,128)(2,1)S(1)} collective-permute-done((bf16[4,1024,128]{2,1,0:T(8,128)(2,1)S(1)}, bf16[4,1024,128]{2,1,0:T(8,128)(2,1)S(1)}, u32[]{:S(2)}, u32[]{:S(2)}) %collective-permute-start.79) | collective-permute-done | bytes 1048608 | tf_op jit(solution)/shard_map/ppermute | solution.py:353
  910.8 25.5 %collective-permute-done.76 = bf16[256,2048]{1,0:T(8,128)(2,1)S(1)} collective-permute-done((bf16[256,2048]{1,0:T(8,128)(2,1)S(1)}, bf16[256,2048]{1,0:T(8,128)(2,1)S(1)}, u32[]{:S(2)}, u32[]{:S(2)}) %collective-permute-start.76) | collective-permute-done | bytes 1048608 | tf_op jit(solution)/shard_map/ppermute | solution.py:353
  (571 shorter events, 518.9 us)
Async XLA Ops:
  34.8 64.8 %collective-permute-start.3 = (bf16[512,1024]{1,0:T(8,128)(2,1)}, bf16[512,1024]{1,0:T(8,128)(2,1)}, u32[]{:S(2)}, u32[]{:S(2)}) collective-permute-start(bf16[512,1024]{1,0:T(8,128)(2,1)} %pad_maximum_fusion.8), channel_id=1, source_target_pairs={{0,2},{1,3},{2,0},{3,1},{4,6},{5,7},{6,4},{7,5},{8,10},{9,11},{10,... | collective-permute-start | bytes 3145736 | tf_op jit(solution)/shard_map/ppermute | solution.py:353
  37.7 61.9 %collective-permute-start.5 = (bf16[4,1024,128]{2,1,0:T(8,128)(2,1)}, bf16[4,1024,128]{2,1,0:T(8,128)(2,1)}, u32[]{:S(2)}, u32[]{:S(2)}) collective-permute-start(bf16[4,1024,128]{2,1,0:T(8,128)(2,1)} %maximum_select_fusion.1), channel_id=1, source_target_pairs={{0,24},{4,28},{8,16},{12,20},{16,8},{20,12},{24,0},{28,4},{1,25},{... | collective-permute-start | bytes 3145736 | tf_op jit(solution)/shard_map/ppermute | solution.py:389
  105.2 49.1 %collective-permute-start.14 = (bf16[1024,512]{1,0:T(8,128)(2,1)S(1)}, bf16[1024,512]{1,0:T(8,128)(2,1)S(1)}, u32[]{:S(2)}, u32[]{:S(2)}) collective-permute-start(bf16[1024,512]{1,0:T(8,128)(2,1)S(1)} %maximum_select_fusion.2), channel_id=1, source_target_pairs={{0,2},{1,3},{2,0},{3,1},{4,6},{5,7},{6,4},{7,5},{8,10},{9,11},{10,... | collective-permute-start | bytes 3145736 | tf_op jit(solution)/shard_map/ppermute | solution.py:353
  190.8 50.4 %collective-permute-start.21 = (bf16[1024,512]{1,0:T(8,128)(2,1)S(1)}, bf16[1024,512]{1,0:T(8,128)(2,1)S(1)}, u32[]{:S(2)}, u32[]{:S(2)}) collective-permute-start(bf16[1024,512]{1,0:T(8,128)(2,1)S(1)} %maximum_select_fusion.3), channel_id=1, source_target_pairs={{0,24},{4,28},{8,16},{12,20},{16,8},{20,12},{24,0},{28,4},{1,25},{... | collective-permute-start | bytes 3145736 | tf_op jit(solution)/shard_map/ppermute | solution.py:389
  192.6 48.6 %collective-permute-start.20 = (bf16[1024,512]{1,0:T(8,128)(2,1)S(1)}, bf16[1024,512]{1,0:T(8,128)(2,1)}, u32[]{:S(2)}, u32[]{:S(2)}) collective-permute-start(bf16[1024,512]{1,0:T(8,128)(2,1)S(1)} %maximum_select_fusion.3), channel_id=1, source_target_pairs={{0,2},{1,3},{2,0},{3,1},{4,6},{5,7},{6,4},{7,5},{8,10},{9,11},{10,... | collective-permute-start | bytes 3145736 | tf_op jit(solution)/shard_map/ppermute | solution.py:353
  252.5 81.9 %collective-permute-start.26 = (bf16[4,1024,512]{2,1,0:T(8,128)(2,1)S(1)}, bf16[4,1024,512]{2,1,0:T(8,128)(2,1)}, u32[]{:S(2)}, u32[]{:S(2)}) collective-permute-start(bf16[4,1024,512]{2,1,0:T(8,128)(2,1)S(1)} %pad_maximum_fusion.1.refs_1_.refs_2_), channel_id=1, source_target_pairs={{0,16},{16,0},{1,17},{17,1},{2,18},{18,2},{3,19},{19,3},{4,20},{20... | collective-permute-start | bytes 12582920 | tf_op jit(solution)/shard_map/ppermute | solution.py:384
  285.3 47.9 %collective-permute-start.24 = (bf16[256,2048]{1,0:T(8,128)(2,1)S(1)}, bf16[256,2048]{1,0:T(8,128)(2,1)S(1)}, u32[]{:S(2)}, u32[]{:S(2)}) collective-permute-start(bf16[256,2048]{1,0:T(8,128)(2,1)S(1)} %add_convert_fusion.9), channel_id=1, source_target_pairs={{0,2},{1,3},{2,0},{3,1},{4,6},{5,7},{6,4},{7,5},{8,10},{9,11},{10,... | collective-permute-start | bytes 3145736 | tf_op jit(solution)/shard_map/ppermute | solution.py:353
  287.0 47.5 %collective-permute-start.27 = (bf16[512,1024]{1,0:T(8,128)(2,1)S(1)}, bf16[512,1024]{1,0:T(8,128)(2,1)S(1)}, u32[]{:S(2)}, u32[]{:S(2)}) collective-permute-start(bf16[512,1024]{1,0:T(8,128)(2,1)S(1)} %maximum_select_fusion.5), channel_id=1, source_target_pairs={{0,24},{4,28},{8,16},{12,20},{16,8},{20,12},{24,0},{28,4},{1,25},{... | collective-permute-start | bytes 3145736 | tf_op jit(solution)/shard_map/ppermute | solution.py:389
  336.8 48.6 %collective-permute-start.33 = (bf16[512,1024]{1,0:T(8,128)(2,1)S(1)}, bf16[512,1024]{1,0:T(8,128)(2,1)S(1)}, u32[]{:S(2)}, u32[]{:S(2)}) collective-permute-start(bf16[512,1024]{1,0:T(8,128)(2,1)S(1)} %maximum_select_fusion.5), channel_id=1, source_target_pairs={{0,2},{1,3},{2,0},{3,1},{4,6},{5,7},{6,4},{7,5},{8,10},{9,11},{10,... | collective-permute-start | bytes 3145736 | tf_op jit(solution)/shard_map/ppermute | solution.py:353
  336.9 48.6 %collective-permute-start.29 = (bf16[256,2048]{1,0:T(8,128)(2,1)S(1)}, bf16[256,2048]{1,0:T(8,128)(2,1)S(1)}, u32[]{:S(2)}, u32[]{:S(2)}) collective-permute-start(bf16[256,2048]{1,0:T(8,128)(2,1)S(1)} %get-tuple-element.417.refs_0_), channel_id=1, source_target_pairs={{0,4},{4,0},{8,12},{12,8},{1,5},{5,1},{9,13},{13,9},{2,6},{6,2},{1... | collective-permute-start | bytes 3145736 | tf_op jit(solution)/shard_map/ppermute | solution.py:353
  338.2 48.3 %collective-permute-start.30 = (bf16[256,2048]{1,0:T(8,128)(2,1)S(1)}, bf16[256,2048]{1,0:T(8,128)(2,1)S(1)}, u32[]{:S(2)}, u32[]{:S(2)}) collective-permute-start(bf16[256,2048]{1,0:T(8,128)(2,1)S(1)} %get-tuple-element.417.refs_0_), channel_id=1, source_target_pairs={{0,1},{1,0},{2,3},{3,2},{4,5},{5,4},{6,7},{7,6},{8,9},{9,8},{10,11... | collective-permute-start | bytes 3145736 | tf_op jit(solution)/shard_map/ppermute | solution.py:353
  598.7 51.4 %collective-permute-start.53 = (bf16[256,2048]{1,0:T(8,128)(2,1)S(1)}, bf16[256,2048]{1,0:T(8,128)(2,1)}, u32[]{:S(2)}, u32[]{:S(2)}) collective-permute-start(bf16[256,2048]{1,0:T(8,128)(2,1)S(1)} %get-tuple-element.304.refs_0_), channel_id=1, source_target_pairs={{0,2},{1,3},{2,0},{3,1},{4,6},{5,7},{6,4},{7,5},{8,10},{9,11},{10,... | collective-permute-start | bytes 3145736 | tf_op jit(solution)/shard_map/ppermute | solution.py:353
  600.1 51.4 %collective-permute-start.52 = (bf16[256,2048]{1,0:T(8,128)(2,1)S(1)}, bf16[256,2048]{1,0:T(8,128)(2,1)}, u32[]{:S(2)}, u32[]{:S(2)}) collective-permute-start(bf16[256,2048]{1,0:T(8,128)(2,1)S(1)} %get-tuple-element.304.refs_0_), channel_id=1, source_target_pairs={{0,4},{4,0},{8,12},{12,8},{1,5},{5,1},{9,13},{13,9},{2,6},{6,2},{1... | collective-permute-start | bytes 3145736 | tf_op jit(solution)/shard_map/ppermute | solution.py:353
  605.1 45.0 %all-to-all-start.3 = ((bf16[256,4,512]{2,0,1:T(8,128)(2,1)}), bf16[256,4,512]{2,0,1:T(8,128)(2,1)}, u32[]{:S(2)}, u32[]{:S(2)}) async-start(bf16[256,4,512]{2,0,1:T(8,128)(2,1)} %bitcast.231), calls=%async_computation.3 | async-start | bytes 2097152 | tf_op jit(solution)/shard_map/all_to_all | solution.py:1184
  609.6 53.4 %collective-permute-start.57 = (bf16[512,1024]{1,0:T(8,128)(2,1)}, bf16[512,1024]{1,0:T(8,128)(2,1)}, u32[]{:S(2)}, u32[]{:S(2)}) collective-permute-start(bf16[512,1024]{1,0:T(8,128)(2,1)} %get-tuple-element.294), channel_id=1, source_target_pairs={{0,24},{4,28},{8,16},{12,20},{16,8},{20,12},{24,0},{28,4},{1,25},{... | collective-permute-start | bytes 3145736 | tf_op jit(solution)/shard_map/ppermute | solution.py:389
  694.3 57.6 %collective-permute-start.62 = (bf16[512,1024]{1,0:T(8,128)(2,1)}, bf16[512,1024]{1,0:T(8,128)(2,1)S(1)}, u32[]{:S(2)}, u32[]{:S(2)}) collective-permute-start(bf16[512,1024]{1,0:T(8,128)(2,1)} %fusion.27), channel_id=1, source_target_pairs={{0,2},{1,3},{2,0},{3,1},{4,6},{5,7},{6,4},{7,5},{8,10},{9,11},{10,... | collective-permute-start | bytes 3145736 | tf_op jit(solution)/shard_map/ppermute | solution.py:353
  705.5 46.4 %collective-permute-start.64 = (bf16[1024,512]{1,0:T(8,128)(2,1)}, bf16[1024,512]{1,0:T(8,128)(2,1)S(1)}, u32[]{:S(2)}, u32[]{:S(2)}) collective-permute-start(bf16[1024,512]{1,0:T(8,128)(2,1)} %get-tuple-element.322), channel_id=1, source_target_pairs={{0,24},{4,28},{8,16},{12,20},{16,8},{20,12},{24,0},{28,4},{1,25},{... | collective-permute-start | bytes 3145736 | tf_op jit(solution)/shard_map/ppermute | solution.py:389
  705.5 48.1 %collective-permute-start.65 = (bf16[1024,512]{1,0:T(8,128)(2,1)}, bf16[1024,512]{1,0:T(8,128)(2,1)S(1)}, u32[]{:S(2)}, u32[]{:S(2)}) collective-permute-start(bf16[1024,512]{1,0:T(8,128)(2,1)} %get-tuple-element.323), channel_id=1, source_target_pairs={{0,24},{4,28},{8,16},{12,20},{16,8},{20,12},{24,0},{28,4},{1,25},{... | collective-permute-start | bytes 3145736 | tf_op jit(solution)/shard_map/ppermute | solution.py:389
  710.7 67.0 %collective-permute-start.71 = (bf16[1024,512]{1,0:T(8,128)(2,1)}, bf16[1024,512]{1,0:T(8,128)(2,1)}, u32[]{:S(2)}, u32[]{:S(2)}) collective-permute-start(bf16[1024,512]{1,0:T(8,128)(2,1)} %get-tuple-element.330), channel_id=1, source_target_pairs={{0,24},{4,28},{8,16},{12,20},{16,8},{20,12},{24,0},{28,4},{1,25},{... | collective-permute-start | bytes 3145736 | tf_op jit(solution)/shard_map/ppermute | solution.py:389
  756.2 59.5 %collective-permute-start.70 = (bf16[1024,512]{1,0:T(8,128)(2,1)}, bf16[1024,512]{1,0:T(8,128)(2,1)}, u32[]{:S(2)}, u32[]{:S(2)}) collective-permute-start(bf16[1024,512]{1,0:T(8,128)(2,1)} %fusion.24), channel_id=1, source_target_pairs={{0,2},{1,3},{2,0},{3,1},{4,6},{5,7},{6,4},{7,5},{8,10},{9,11},{10,... | collective-permute-start | bytes 3145736 | tf_op jit(solution)/shard_map/ppermute | solution.py:353
  758.1 57.5 %collective-permute-start.68 = (bf16[3,4,256,128]{3,2,1,0:T(8,128)(2,1)}, bf16[3,4,256,128]{3,2,1,0:T(8,128)(2,1)S(1)}, u32[]{:S(2)}, u32[]{:S(2)}) collective-permute-start(bf16[3,4,256,128]{3,2,1,0:T(8,128)(2,1)} %get-tuple-element.327), channel_id=1, source_target_pairs={{0,9},{1,8},{2,11},{3,10},{4,13},{5,12},{6,15},{7,14},{8,1},{9,0},... | collective-permute-start | bytes 2359304 | tf_op jit(solution)/shard_map/ppermute | solution.py:376
  835.2 48.5 %collective-permute-start.74 = (bf16[1024,512]{1,0:T(8,128)(2,1)}, bf16[1024,512]{1,0:T(8,128)(2,1)}, u32[]{:S(2)}, u32[]{:S(2)}) collective-permute-start(bf16[1024,512]{1,0:T(8,128)(2,1)} %fusion.23), channel_id=1, source_target_pairs={{0,2},{1,3},{2,0},{3,1},{4,6},{5,7},{6,4},{7,5},{8,10},{9,11},{10,... | collective-permute-start | bytes 3145736 | tf_op jit(solution)/shard_map/ppermute | solution.py:353
  863.3 74.0 %collective-permute-start.81 = (bf16[2,2,512,512]{3,2,1,0:T(8,128)(2,1)S(1)}, bf16[2,2,512,512]{3,2,1,0:T(8,128)(2,1)S(1)}, u32[]{:S(2)}, u32[]{:S(2)}) collective-permute-start(bf16[2,2,512,512]{3,2,1,0:T(8,128)(2,1)S(1)} %pad_maximum_fusion.7), channel_id=1, source_target_pairs={{0,16},{16,0},{1,17},{17,1},{2,18},{18,2},{3,19},{19,3},{4,20},{20... | collective-permute-start | bytes 6291464 | tf_op jit(solution)/shard_map/ppermute | solution.py:384
  887.6 48.8 %collective-permute-start.76 = (bf16[256,2048]{1,0:T(8,128)(2,1)S(1)}, bf16[256,2048]{1,0:T(8,128)(2,1)S(1)}, u32[]{:S(2)}, u32[]{:S(2)}) collective-permute-start(bf16[256,2048]{1,0:T(8,128)(2,1)S(1)} %add_convert_fusion.3), channel_id=1, source_target_pairs={{0,2},{1,3},{2,0},{3,1},{4,6},{5,7},{6,4},{7,5},{8,10},{9,11},{10,... | collective-permute-start | bytes 3145736 | tf_op jit(solution)/shard_map/ppermute | solution.py:353
  (198 other events, 3554.4 us)
